TPU v7x, 256 devices: a whole 4x4x8 slice. The times are simulated.
256 devices in a mesh: scan: 2 (over core), gz: 16 (over y_lo, z), gy: 8 (over x, y_hi).
Axes of the slice: x: 4, y: 4 (y_hi: 2, y_lo: 2; y = y_hi * 2 + y_lo), z: 8, core: 2. Of those that a mesh axis runs over, the one named last changes fastest.
Arguments:
- scans: bfloat16 [2, 64, 64, 16, 256], P('scan', 'gz', 'gy'), may hold values from -16 to 16
- proj_weight: bfloat16 [256, 256], replicated, may hold values from -0.375 to 0.375
- value_weight: bfloat16 [256, 256], replicated, may hold values from -0.375 to 0.375
- out_weight: bfloat16 [256, 256], replicated, may hold values from -0.375 to 0.375
- flags: int32 [2, 16, 16, 4], replicated, may hold values 0 or 1
- cotangent: bfloat16 [2, 64, 64, 16, 256], P('scan', 'gz', 'gy'), may hold values from -6 to 6
Outputs:
- mixed: bfloat16 [2, 64, 64, 16, 256], P('scan', 'gz', 'gy')
- grad_scans: bfloat16 [2, 64, 64, 16, 256], P('scan', 'gz', 'gy')
- grad_proj_weight: float32 [256, 256], replicated
- grad_value_weight: float32 [256, 256], replicated
- grad_out_weight: float32 [256, 256], replicated
All inputs are finite; a program needn't handle non-finite values.
Results may differ from a plain program's by a relative error of at most 0.035.
Values may be sent and summed in bfloat16 or wider, within the bound.
No kernel may reach another device: no remote copies, remote signals or barrier semaphores. Data moves between devices by JAX's collectives and lax.ppermute only.
A program may use at most 128 MiB of HBM per device.

v0:
```python
import jax
import jax.numpy as jnp
from jax import lax
from jax.sharding import PartitionSpec as P

D = 256
HEADS = 4
HEAD_DIM = 64
BLK = 4
CZ = 4
CY = 8
CX = 16


def swapped(block, axis, stride):
    count = lax.axis_size(axis)
    route = []
    for low in range(count):
        high = low | 1 << stride
        if high != low and high < count:
            route += [(low, high), (high, low)]
    return lax.ppermute(block, axis, route)


def padded_2(block, sides, width):
    for axis, dim in sides:
        count = lax.axis_size(axis)
        forward = [(i, i + 1) for i in range(count - 1)]
        backward = [(target, source) for source, target in forward]
        low = lax.ppermute(
            lax.slice_in_dim(block, block.shape[dim] - width, None, axis=dim), axis, forward
        )
        high = lax.ppermute(lax.slice_in_dim(block, 0, width, axis=dim), axis, backward)
        block = jnp.concatenate([low, block, high], axis=dim)
    return block


def to_blocks(field):
    depth_cells, height_cells, across_cells, channels = field.shape
    shaped = field.reshape(
        depth_cells // BLK, BLK, height_cells // BLK, BLK, across_cells // BLK, BLK, channels
    )
    shaped = shaped.transpose(0, 2, 4, 1, 3, 5, 6)
    return shaped.reshape(
        depth_cells // BLK, height_cells // BLK, across_cells // BLK, BLK**3, channels
    )


def from_blocks(blocks):
    planes, row_blocks, column_blocks, members, channels = blocks.shape
    shaped = blocks.reshape(planes, row_blocks, column_blocks, BLK, BLK, BLK, channels)
    shaped = shaped.transpose(0, 3, 1, 4, 2, 5, 6)
    return shaped.reshape(planes * BLK, row_blocks * BLK, column_blocks * BLK, channels)


def padded_blocks(field):
    return jnp.pad(to_blocks(field), ((0, 0), (0, 0), (1, 1), (0, 0), (0, 0)))


def on_device(scans, proj_weight, value_weight, out_weight, flags, cotangent):
    own = scans[0]
    field = own.shape
    cube = BLK**3
    scale = HEAD_DIM ** (-0.5)
    flat = own.reshape(-1, D)
    proj_own = jnp.dot(flat, proj_weight, preferred_element_type=jnp.float32).astype(jnp.bfloat16)
    vals_own = jnp.dot(flat, value_weight, preferred_element_type=jnp.float32).astype(jnp.bfloat16)
    cot_flat = cotangent[0].reshape(-1, D)
    grad_z = jnp.dot(cot_flat, out_weight.T, preferred_element_type=jnp.float32).astype(
        jnp.bfloat16
    )
    partner = swapped((proj_own.reshape(field), vals_own.reshape(field)), "scan", 0)
    proj_halo, vals_halo = (
        padded_2(partner[0], (("gz", 0), ("gy", 1)), BLK),
        padded_2(partner[1], (("gz", 0), ("gy", 1)), BLK),
    )
    depth_blocks = CZ // BLK
    height_blocks = CY // BLK
    across_blocks = CX // BLK
    total_blocks = depth_blocks * height_blocks * across_blocks
    side = lax.axis_index("scan")
    plane_start = lax.axis_index("gz") * depth_blocks
    row_start = lax.axis_index("gy") * height_blocks
    flag_pad = jnp.pad(flags, ((0, 0), (1, 1), (1, 1), (1, 1)))
    window_shape = (1, depth_blocks + 2, height_blocks + 2, across_blocks + 2)
    near_other = lax.dynamic_slice(flag_pad, (1 - side, plane_start, row_start, 0), window_shape)[0]
    near_own = lax.dynamic_slice(flag_pad, (side, plane_start, row_start, 0), window_shape)[0]
    inside = jnp.pad(jnp.ones(flags.shape[1:], jnp.int32), 1)
    near_inside = lax.dynamic_slice(inside, (plane_start, row_start, 0), window_shape[1:])
    center = lax.iota(jnp.int32, 27) == 13
    query_blocks = to_blocks(proj_own.reshape(field)).reshape(-1, cube, D)
    value_blocks = to_blocks(vals_own.reshape(field)).reshape(-1, cube, D)
    upstream_blocks = to_blocks(grad_z.reshape(field)).reshape(-1, cube, D)
    key_pad = padded_blocks(proj_halo)
    value_pad = padded_blocks(vals_halo)

    def locate(number):
        plane = number // (height_blocks * across_blocks)
        row_at = number // across_blocks % height_blocks
        column = number % across_blocks
        return (plane, row_at, column)

    def window(padded, number):
        plane, row_at, column = locate(number)
        piece = lax.dynamic_slice(
            padded, (plane, row_at, column, 0, 0), (3, 3, 3) + padded.shape[3:]
        )
        return piece.reshape(27 * cube, padded.shape[4])

    def unblock(stacked):
        return from_blocks(
            stacked.reshape(depth_blocks, height_blocks, across_blocks, cube, stacked.shape[-1])
        )

    def query_block(number):
        plane, row_at, column = locate(number)
        keys = window(key_pad, number).reshape(-1, HEADS, HEAD_DIM)
        values = window(value_pad, number).reshape(-1, HEADS, HEAD_DIM)
        near = lax.dynamic_slice(near_other, (plane, row_at, column), (3, 3, 3)).reshape(27)
        valid = jnp.repeat((near > 0) | center, cube)
        query = query_blocks[number].reshape(cube, HEADS, HEAD_DIM)
        upstream = upstream_blocks[number].reshape(cube, HEADS, HEAD_DIM)
        raw_scores = (
            jnp.einsum("qhd,khd->hqk", query, keys, preferred_element_type=jnp.float32) * scale
        )
        scores = jnp.where(valid[None, None, :], raw_scores, -jnp.inf)
        top = jnp.max(scores, axis=2, keepdims=True)
        expd = jnp.exp(scores - top)
        total_weight = jnp.sum(expd, axis=2, keepdims=True)
        weights = expd / total_weight
        rounded = weights.astype(jnp.bfloat16)
        attended = jnp.einsum(
            "hqk,khd->qhd", rounded, values, preferred_element_type=jnp.float32
        ).astype(jnp.bfloat16)
        delta = jnp.sum(upstream.astype(jnp.float32) * attended.astype(jnp.float32), axis=2)
        pushed = jnp.einsum("qhd,khd->hqk", upstream, values, preferred_element_type=jnp.float32)
        slopes = (weights * (pushed - delta.T[:, :, None]) * scale).astype(jnp.bfloat16)
        query_grad = jnp.einsum("hqk,khd->qhd", slopes, keys, preferred_element_type=jnp.float32)
        log_total = (top + jnp.log(total_weight))[:, :, 0].T
        return (
            attended.reshape(cube, D),
            log_total,
            delta,
            query_grad.reshape(cube, D),
            raw_scores,
        )

    attended, log_total, delta, query_grad, kept_scores = lax.map(
        query_block, jnp.arange(total_blocks, dtype=jnp.int32)
    )
    attended_field = unblock(attended)
    lse_field = unblock(log_total)
    delta_field = unblock(delta)
    query_field = unblock(query_grad)
    upstream_field = grad_z.reshape(field)
    upstream_partner = swapped(upstream_field, "scan", 0)
    upstream_halo = padded_2(upstream_partner, (("gz", 0), ("gy", 1)), BLK)
    stats_partner = swapped((lse_field, delta_field), "scan", 0)
    lse_halo, delta_halo = (
        padded_2(stats_partner[0], (("gz", 0), ("gy", 1)), BLK),
        padded_2(stats_partner[1], (("gz", 0), ("gy", 1)), BLK),
    )
    upstream_pad = padded_blocks(upstream_halo)
    lse_pad = padded_blocks(lse_halo)
    delta_pad = padded_blocks(delta_halo)

    def key_block(inputs):
        number, block_scores = inputs
        plane, row_at, column = locate(number)
        queries = window(key_pad, number).reshape(-1, HEADS, HEAD_DIM)
        upstream = window(upstream_pad, number).reshape(-1, HEADS, HEAD_DIM)
        lse_window = window(lse_pad, number)
        delta_window = window(delta_pad, number)
        exists = lax.dynamic_slice(near_inside, (plane, row_at, column), (3, 3, 3)).reshape(27) > 0
        own_flag = lax.dynamic_slice(
            near_own, (plane + 1, row_at + 1, column + 1), (1, 1, 1)
        ).reshape(())
        valid = jnp.repeat(exists & ((own_flag > 0) | center), cube)
        values = value_blocks[number].reshape(cube, HEADS, HEAD_DIM)
        shifted = jnp.where(valid[None, None, :], block_scores - lse_window.T[:, None, :], -jnp.inf)
        weights = jnp.exp(shifted)
        rounded = weights.astype(jnp.bfloat16)
        pushed = jnp.einsum("qhd,khd->hkq", upstream, values, preferred_element_type=jnp.float32)
        slopes = (weights * (pushed - delta_window.T[:, None, :]) * scale).astype(jnp.bfloat16)
        key_grad = jnp.einsum("hkq,qhd->khd", slopes, queries, preferred_element_type=jnp.float32)
        value_grad = jnp.einsum(
            "hkq,qhd->khd", rounded, upstream, preferred_element_type=jnp.float32
        )
        return (key_grad.reshape(cube, D), value_grad.reshape(cube, D))

    key_grad, value_grad = lax.map(
        key_block, (jnp.arange(total_blocks, dtype=jnp.int32), kept_scores)
    )
    proj_grad = (query_field + unblock(key_grad)).astype(jnp.bfloat16).reshape(-1, D)
    vals_grad = unblock(value_grad).astype(jnp.bfloat16).reshape(-1, D)
    attended_flat = attended_field.reshape(-1, D)
    mixed = (
        jnp.dot(attended_flat, out_weight, preferred_element_type=jnp.float32)
        .astype(jnp.bfloat16)
        .reshape(scans.shape)
    )
    grad_scans = (
        (
            jnp.dot(proj_grad, proj_weight.T, preferred_element_type=jnp.float32)
            + jnp.dot(vals_grad, value_weight.T, preferred_element_type=jnp.float32)
        )
        .astype(jnp.bfloat16)
        .reshape(scans.shape)
    )
    local_proj = jnp.dot(flat.T, proj_grad, preferred_element_type=jnp.float32)
    local_value = jnp.dot(flat.T, vals_grad, preferred_element_type=jnp.float32)
    local_out = jnp.dot(attended_flat.T, cot_flat, preferred_element_type=jnp.float32)
    summed = lax.psum((local_proj, local_value, local_out), ("scan", "gz", "gy"))
    return (mixed, grad_scans, summed[0], summed[1], summed[2])


def solution(mesh):
    return jax.shard_map(
        on_device,
        mesh=mesh,
        in_specs=(
            P("scan", "gz", "gy", None, None),
            P(),
            P(),
            P(),
            P(),
            P("scan", "gz", "gy", None, None),
        ),
        out_specs=(
            P("scan", "gz", "gy", None, None),
            P("scan", "gz", "gy", None, None),
            P(),
            P(),
            P(),
        ),
        check_vma=False,
    )
```

profile of v0, /device:TPU:1, one launch (start us, length us, event | category | flops | bytes accessed | tf_op | source)
XLA Modules:
  0.0 766.9 jit_solution(13792516813963944112)
XLA Ops:
  9.3 3.3 collective-permute-start
  22.9 4.1 collective-permute-start.6
  28.4 4.2 collective-permute-start.16
  35.4 5.5 collective-permute-start.3
  43.3 7.1 collective-permute-start.8
  53.0 3.4 collective-permute-done.4
  56.3 3.0 collective-permute-start.18
  59.4 20.1 %collective-permute-done.3 = bf16[12,4,16,256]{3,2,1,0:T(8,128)(2,1)S(1)} collective-permute-done((bf16[12,4,16,256]{3,2,1,0:T(8,128)(2,1)S(1)}, bf16[12,4,16,256]{3,2,1,0:T(8,128)(2,1)S(1)}, u32[]{:S(2)}, u32[]{:S(2)}) %collective-permute-start.3) | collective-permute-done | bytes 393248 | tf_op jit(solution)/shard_map/ppermute | solution.py:30
  82.4 5.6 collective-permute-done.8
  96.4 179.0 %while.38 = (s32[]{:T(128)}, bf16[8,64,256]{2,1,0:T(8,128)(2,1)S(1)}, f32[8,64,4]{1,2,0:T(4,128)S(1)}, f32[8,64,4]{1,2,0:T(4,128)}, f32[8,64,256]{1,2,0:T(8,128)...) while((s32[]{:T(128)}, ...), condition=%wide.region_4.5_spmd.clone, body=%wide.region_0.4_spmd.clone.sunk | while | flops 234094208 | bytes 29196008 | solution.py:148
  103.8 2.9 copy.159
  286.9 4.0 collective-permute-start.21
  294.5 6.5 collective-permute-start.13
  303.9 7.0 collective-permute-start.23
  320.1 167.4 %while.39 = (s32[]{:T(128)}, f32[8,64,256]{1,2,0:T(8,128)}, bf16[8,64,256]{1,2,0:T(8,128)(2,1)S(1)}, s32[8]{0:T(128)S(1)}, bf16[3,4,6,64,256]{4,3,2,1,0:T(8,128)...) while((s32[]{:T(128)}, f32[8,64,256]{1,2,0:T(8,128)}, ...), condition=%wide.region_6.7_spmd.clone, body=%wide.region_5.6_spmd.clone.sunk | while | flops 173850784 | bytes 20642436 | solution.py:191
  334.9 3.4 fusion.106
  355.8 3.4 fusion.106
  376.7 3.4 fusion.106
  397.6 3.4 fusion.106
  418.6 3.4 fusion.106
  439.5 3.4 fusion.106
  460.4 3.4 fusion.106
  481.3 3.4 fusion.106
  493.3 261.5 %all-reduce.10.cloned.1.call-done = (f32[256,256]{0,1:T(8,128)}, f32[256,256]{0,1:T(8,128)}, f32[256,256]{1,0:T(8,128)}) async-done(((f32[256,256]{0,1:T(8,128)}, f32[256,256]{0,1:T(8,128)}, f32[256,256]{1,0:T(8,128)}), (f32[256,256]{0,1:T(8,128)}, f32[256,256]{0,1:T(8,128)}, f32[256,256]{1,0:T(8,128)})) %all-reduce.10.cloned.1.call-update) | async-done | bytes 786448 | tf_op jit(solution)/shard_map/psum | solution.py:213
  (567 shorter events, 318.6 us)
Async XLA Ops:
  7.2 747.6 %all-reduce.10.cloned.1.call-start = ((), (), s32[]{:S(2)}) async-start(), calls=%async_computation | async-start | bytes 1572864 | tf_op jit(solution)/shard_map/psum | solution.py:213
  13.7 9.2 %collective-permute-start.5 = (bf16[4,8,16,256]{3,2,1,0:T(8,128)(2,1)S(1)}, bf16[4,8,16,256]{3,2,1,0:T(8,128)(2,1)S(1)}, u32[]{:S(2)}, u32[]{:S(2)}) collective-permute-start(bf16[4,8,16,256]{3,2,1,0:T(8,128)(2,1)S(1)} %bitcast.208), channel_id=1, source_target_pairs={{0,128},{128,0},{1,129},{129,1},{2,130},{130,2},{3,131},{131,3},{4... | collective-permute-start | bytes 786440 | tf_op jit(solution)/shard_map/ppermute | solution.py:22
  15.1 13.3 %collective-permute-start.15 = (bf16[4,8,16,256]{3,2,1,0:T(8,128)(2,1)S(1)}, bf16[4,8,16,256]{3,2,1,0:T(8,128)(2,1)S(1)}, u32[]{:S(2)}, u32[]{:S(2)}) collective-permute-start(bf16[4,8,16,256]{3,2,1,0:T(8,128)(2,1)S(1)} %bitcast.207), channel_id=1, source_target_pairs={{0,128},{128,0},{1,129},{129,1},{2,130},{130,2},{3,131},{131,3},{4... | collective-permute-start | bytes 786440 | tf_op jit(solution)/shard_map/ppermute | solution.py:22
  15.6 16.9 %collective-permute-start.1 = (bf16[4,8,16,256]{3,2,1,0:T(8,128)(2,1)S(1)}, bf16[4,8,16,256]{3,2,1,0:T(8,128)(2,1)S(1)}, u32[]{:S(2)}, u32[]{:S(2)}) collective-permute-start(bf16[4,8,16,256]{3,2,1,0:T(8,128)(2,1)S(1)} %collective-permute-done), channel_id=1, source_target_pairs={{0,8},{8,16},{16,24},{24,32},{32,40},{40,48},{48,56},{56,64},{64,7... | collective-permute-start | bytes 786440 | tf_op jit(solution)/shard_map/ppermute | solution.py:30
  18.5 15.5 %collective-permute-start.2 = (bf16[4,8,16,256]{3,2,1,0:T(8,128)(2,1)S(1)}, bf16[4,8,16,256]{3,2,1,0:T(8,128)(2,1)S(1)}, u32[]{:S(2)}, u32[]{:S(2)}) collective-permute-start(bf16[4,8,16,256]{3,2,1,0:T(8,128)(2,1)S(1)} %collective-permute-done), channel_id=1, source_target_pairs={{8,0},{16,8},{24,16},{32,24},{40,32},{48,40},{56,48},{64,56},{72,6... | collective-permute-start | bytes 786440 | tf_op jit(solution)/shard_map/ppermute | solution.py:33
  22.9 12.4 %collective-permute-start.6 = (bf16[4,8,16,256]{3,2,1,0:T(8,128)(2,1)S(1)}, bf16[4,8,16,256]{3,2,1,0:T(8,128)(2,1)S(1)}, u32[]{:S(2)}, u32[]{:S(2)}) collective-permute-start(bf16[4,8,16,256]{3,2,1,0:T(8,128)(2,1)S(1)} %collective-permute-done.5), channel_id=1, source_target_pairs={{0,8},{8,16},{16,24},{24,32},{32,40},{40,48},{48,56},{56,64},{64,7... | collective-permute-start | bytes 786440 | tf_op jit(solution)/shard_map/ppermute | solution.py:30
  27.1 13.9 %collective-permute-start.7 = (bf16[4,8,16,256]{3,2,1,0:T(8,128)(2,1)S(1)}, bf16[4,8,16,256]{3,2,1,0:T(8,128)(2,1)S(1)}, u32[]{:S(2)}, u32[]{:S(2)}) collective-permute-start(bf16[4,8,16,256]{3,2,1,0:T(8,128)(2,1)S(1)} %collective-permute-done.5), channel_id=1, source_target_pairs={{8,0},{16,8},{24,16},{32,24},{40,32},{48,40},{56,48},{64,56},{72,6... | collective-permute-start | bytes 786440 | tf_op jit(solution)/shard_map/ppermute | solution.py:33
  28.4 15.0 %collective-permute-start.16 = (bf16[4,8,16,256]{3,2,1,0:T(8,128)(2,1)S(1)}, bf16[4,8,16,256]{3,2,1,0:T(8,128)(2,1)S(1)}, u32[]{:S(2)}, u32[]{:S(2)}) collective-permute-start(bf16[4,8,16,256]{3,2,1,0:T(8,128)(2,1)S(1)} %collective-permute-done.15), channel_id=1, source_target_pairs={{0,8},{8,16},{16,24},{24,32},{32,40},{40,48},{48,56},{56,64},{64,7... | collective-permute-start | bytes 786440 | tf_op jit(solution)/shard_map/ppermute | solution.py:30
  32.6 17.9 %collective-permute-start.17 = (bf16[4,8,16,256]{3,2,1,0:T(8,128)(2,1)S(1)}, bf16[4,8,16,256]{3,2,1,0:T(8,128)(2,1)S(1)}, u32[]{:S(2)}, u32[]{:S(2)}) collective-permute-start(bf16[4,8,16,256]{3,2,1,0:T(8,128)(2,1)S(1)} %collective-permute-done.15), channel_id=1, source_target_pairs={{8,0},{16,8},{24,16},{32,24},{40,32},{48,40},{56,48},{64,56},{72,6... | collective-permute-start | bytes 786440 | tf_op jit(solution)/shard_map/ppermute | solution.py:33
  34.0 22.3 %collective-permute-start.4 = (bf16[12,4,16,256]{3,2,1,0:T(8,128)(2,1)S(1)}, bf16[12,4,16,256]{3,2,1,0:T(8,128)(2,1)S(1)}, u32[]{:S(2)}, u32[]{:S(2)}) collective-permute-start(bf16[12,4,16,256]{3,2,1,0:T(8,128)(2,1)S(1)} %get-tuple-element.652), channel_id=1, source_target_pairs={{1,0},{2,1},{3,2},{4,3},{5,4},{6,5},{7,6},{9,8},{10,9},{11,10},{12... | collective-permute-start | bytes 1179656 | tf_op jit(solution)/shard_map/ppermute | solution.py:33
  35.4 44.1 %collective-permute-start.3 = (bf16[12,4,16,256]{3,2,1,0:T(8,128)(2,1)S(1)}, bf16[12,4,16,256]{3,2,1,0:T(8,128)(2,1)S(1)}, u32[]{:S(2)}, u32[]{:S(2)}) collective-permute-start(bf16[12,4,16,256]{3,2,1,0:T(8,128)(2,1)S(1)} %get-tuple-element.651), channel_id=1, source_target_pairs={{0,1},{1,2},{2,3},{3,4},{4,5},{5,6},{6,7},{8,9},{9,10},{10,11},{11... | collective-permute-start | bytes 1179656 | tf_op jit(solution)/shard_map/ppermute | solution.py:30
  42.0 40.3 %collective-permute-start.9 = (bf16[12,4,16,256]{3,2,1,0:T(8,128)(2,1)}, bf16[12,4,16,256]{3,2,1,0:T(8,128)(2,1)}, u32[]{:S(2)}, u32[]{:S(2)}) collective-permute-start(bf16[12,4,16,256]{3,2,1,0:T(8,128)(2,1)} %get-tuple-element.650), channel_id=1, source_target_pairs={{1,0},{2,1},{3,2},{4,3},{5,4},{6,5},{7,6},{9,8},{10,9},{11,10},{12... | collective-permute-start | bytes 1179656 | tf_op jit(solution)/shard_map/ppermute | solution.py:33
  43.3 44.7 %collective-permute-start.8 = (bf16[12,4,16,256]{3,2,1,0:T(8,128)(2,1)}, bf16[12,4,16,256]{3,2,1,0:T(8,128)(2,1)}, u32[]{:S(2)}, u32[]{:S(2)}) collective-permute-start(bf16[12,4,16,256]{3,2,1,0:T(8,128)(2,1)} %get-tuple-element.649), channel_id=1, source_target_pairs={{0,1},{1,2},{2,3},{3,4},{4,5},{5,6},{6,7},{8,9},{9,10},{10,11},{11... | collective-permute-start | bytes 1179656 | tf_op jit(solution)/shard_map/ppermute | solution.py:30
  51.7 229.4 %collective-permute-start.19 = (bf16[12,4,16,256]{3,2,1,0:T(8,128)(2,1)}, bf16[12,4,16,256]{3,2,1,0:T(8,128)(2,1)}, u32[]{:S(2)}, u32[]{:S(2)}) collective-permute-start(bf16[12,4,16,256]{3,2,1,0:T(8,128)(2,1)} %get-tuple-element.648), channel_id=1, source_target_pairs={{1,0},{2,1},{3,2},{4,3},{5,4},{6,5},{7,6},{9,8},{10,9},{11,10},{12... | collective-permute-start | bytes 1179656 | tf_op jit(solution)/shard_map/ppermute | solution.py:33
  56.3 224.8 %collective-permute-start.18 = (bf16[12,4,16,256]{3,2,1,0:T(8,128)(2,1)}, bf16[12,4,16,256]{3,2,1,0:T(8,128)(2,1)}, u32[]{:S(2)}, u32[]{:S(2)}) collective-permute-start(bf16[12,4,16,256]{3,2,1,0:T(8,128)(2,1)} %get-tuple-element.647), channel_id=1, source_target_pairs={{0,1},{1,2},{2,3},{3,4},{4,5},{5,6},{6,7},{8,9},{9,10},{10,11},{11... | collective-permute-start | bytes 1179656 | tf_op jit(solution)/shard_map/ppermute | solution.py:30
  279.7 7.3 collective-permute-start.20
  279.8 12.5 %collective-permute-start.11 = (f32[4,8,16,4]{2,1,3,0:T(8,128)}, f32[4,8,16,4]{2,1,3,0:T(8,128)S(1)}, u32[]{:S(2)}, u32[]{:S(2)}) collective-permute-start(f32[4,8,16,4]{2,1,3,0:T(8,128)} %collective-permute-done.10), channel_id=1, source_target_pairs={{0,8},{8,16},{16,24},{24,32},{32,40},{40,48},{48,56},{56,64},{64,7... | collective-permute-start | bytes 24584 | tf_op jit(solution)/shard_map/ppermute | solution.py:30
  285.6 7.5 collective-permute-start.12
  286.9 14.0 %collective-permute-start.21 = (f32[4,8,16,4]{2,1,3,0:T(8,128)}, f32[4,8,16,4]{2,1,3,0:T(8,128)S(1)}, u32[]{:S(2)}, u32[]{:S(2)}) collective-permute-start(f32[4,8,16,4]{2,1,3,0:T(8,128)} %collective-permute-done.20), channel_id=1, source_target_pairs={{0,8},{8,16},{16,24},{24,32},{32,40},{40,48},{48,56},{56,64},{64,7... | collective-permute-start | bytes 24584 | tf_op jit(solution)/shard_map/ppermute | solution.py:30
  290.9 10.9 %collective-permute-start.22 = (f32[4,8,16,4]{2,1,3,0:T(8,128)}, f32[4,8,16,4]{2,1,3,0:T(8,128)S(1)}, u32[]{:S(2)}, u32[]{:S(2)}) collective-permute-start(f32[4,8,16,4]{2,1,3,0:T(8,128)} %collective-permute-done.20), channel_id=1, source_target_pairs={{8,0},{16,8},{24,16},{32,24},{40,32},{48,40},{56,48},{64,56},{72,6... | collective-permute-start | bytes 24584 | tf_op jit(solution)/shard_map/ppermute | solution.py:33
  293.2 17.7 %collective-permute-start.14 = (f32[12,4,16,4]{2,1,3,0:T(4,128)S(1)}, f32[12,4,16,4]{2,1,3,0:T(4,128)S(1)}, u32[]{:S(2)}, u32[]{:S(2)}) collective-permute-start(f32[12,4,16,4]{2,1,3,0:T(4,128)S(1)} %get-tuple-element.656), channel_id=1, source_target_pairs={{1,0},{2,1},{3,2},{4,3},{5,4},{6,5},{7,6},{9,8},{10,9},{11,10},{12... | collective-permute-start | bytes 36872 | tf_op jit(solution)/shard_map/ppermute | solution.py:33
  294.5 16.4 %collective-permute-start.13 = (f32[12,4,16,4]{2,1,3,0:T(4,128)S(1)}, f32[12,4,16,4]{2,1,3,0:T(4,128)S(1)}, u32[]{:S(2)}, u32[]{:S(2)}) collective-permute-start(f32[12,4,16,4]{2,1,3,0:T(4,128)S(1)} %get-tuple-element.655), channel_id=1, source_target_pairs={{0,1},{1,2},{2,3},{3,4},{4,5},{5,6},{6,7},{8,9},{9,10},{10,11},{11... | collective-permute-start | bytes 36872 | tf_op jit(solution)/shard_map/ppermute | solution.py:30
  302.6 11.2 %collective-permute-start.24 = (f32[12,4,16,4]{2,1,3,0:T(4,128)}, f32[12,4,16,4]{2,1,3,0:T(4,128)}, u32[]{:S(2)}, u32[]{:S(2)}) collective-permute-start(f32[12,4,16,4]{2,1,3,0:T(4,128)} %get-tuple-element.654), channel_id=1, source_target_pairs={{1,0},{2,1},{3,2},{4,3},{5,4},{6,5},{7,6},{9,8},{10,9},{11,10},{12... | collective-permute-start | bytes 36872 | tf_op jit(solution)/shard_map/ppermute | solution.py:33
  303.9 9.9 %collective-permute-start.23 = (f32[12,4,16,4]{2,1,3,0:T(4,128)}, f32[12,4,16,4]{2,1,3,0:T(4,128)}, u32[]{:S(2)}, u32[]{:S(2)}) collective-permute-start(f32[12,4,16,4]{2,1,3,0:T(4,128)} %get-tuple-element.653), channel_id=1, source_target_pairs={{0,1},{1,2},{2,3},{3,4},{4,5},{5,6},{6,7},{8,9},{9,10},{10,11},{11... | collective-permute-start | bytes 36872 | tf_op jit(solution)/shard_map/ppermute | solution.py:30
  (33 other events, 124.8 us)
Sparse Core Ops, SparseCore 0:
  492.2 262.5 all-reduce.9
where the time goes:
time: 773 us; the launch traced here: 767 us
  waiting for transfers between devices  291 us (38%)
  local copies, waits for them, and re-layouts  236 us (31%)
  matrix products  78.6 us (10%)
  loops' own time  67.8 us (9%)
  starting transfers between devices  62.3 us (8%)
  other arithmetic  16.2 us (2%)
  between operations  14.8 us (2%)
    psum x1, waiting for transfers between devices, on_device(): lax.psum((local_proj, local_value, local_out), ('scan', 'gz', 'gy'))  262 us
    ppermute x10, starting transfers between devices, padded_2(): lax.ppermute(lax.slice_in_dim(block, block.shape[dim] - width, None, axis...  44.6 us
    dynamic_slice x48, local copies, waits for them, and re-layouts, window(): lax.dynamic_slice(padded, (plane, row_at, column, 0, 0), (3, 3, 3) + padd...  39.4 us
    another operation x1, loops' own time, on_device(): lax.map(key_block, (jnp.arange(total_blocks, dtype=jnp.int32), kept_scores))  35.7 us
    another operation x1, loops' own time, on_device(): lax.map(query_block, jnp.arange(total_blocks, dtype=jnp.int32))  32.1 us
    reshape x16, local copies, waits for them, and re-layouts, query_block(): values = window(value_pad, number).reshape(-1, HEADS, HEAD_DIM)  29.4 us
    reshape x16, local copies, waits for them, and re-layouts, key_block(): upstream = window(upstream_pad, number).reshape(-1, HEADS, HEAD_DIM)  28.9 us
    dot_general x8, matrix products, key_block(): jnp.einsum('hkq,qhd->khd', slopes, queries, preferred_element_type=jnp.fl...  27.3 us
  transfers between devices with their start and end apart: 26, of which 4 were waited for; matrix products, arithmetic and copies ran while one was open for 23% of the time, Pallas kernels for 0%

commit v1 on v0

v1 whole, which is shorter than its diff:
```python
import functools

import jax
import jax.numpy as jnp
import numpy as np
from jax import lax
from jax.experimental import pallas as pl
from jax.experimental.pallas import tpu as pltpu
from jax.sharding import PartitionSpec as P

D = 256
HEADS = 4
HEAD_DIM = 64
BLK = 4
CUBE = 64
ROW = 256
NEG = -1e30
AXES = ("scan", "gz", "gy")
F32 = jnp.float32
BF16 = jnp.bfloat16
NN = (((1,), (0,)), ((), ()))
NT = (((1,), (1,)), ((), ()))
TN = (((0,), (0,)), ((), ()))


def dot(a, b, dims=NN):
    return lax.dot_general(a, b, dims, preferred_element_type=F32)


def natural_of(t):
    return ((t >> 4) & 3) * 64 + ((t >> 2) & 3) * 16 + (t >> 6) * 4 + (t & 3)


def iota2(shape, axis):
    return lax.broadcasted_iota(jnp.int32, shape, axis)


def to_blocks_matrix():
    shape = (ROW, ROW)
    return (natural_of(iota2(shape, 0)) == iota2(shape, 1)).astype(F32).astype(BF16)


def from_blocks_matrix():
    shape = (ROW, ROW)
    return (natural_of(iota2(shape, 1)) == iota2(shape, 0)).astype(F32).astype(BF16)


def head_mask():
    shape = (ROW, D)
    return (iota2(shape, 0) // HEAD_DIM == iota2(shape, 1) // HEAD_DIM).astype(F32)


def spread(block, mask, scale=1.0):
    wide = jnp.concatenate([block.astype(F32)] * HEADS, axis=0)
    return wide * (mask * scale)


def collect(wide, mask):
    kept = wide * mask
    return (kept[0:64] + kept[64:128]) + (kept[128:192] + kept[192:256])


def chunks(rows, width):
    if width == ROW:
        return [(j, 1) for j in range(rows)]
    return [(j, min(2, rows - j)) for j in range(0, rows, 2)]


def take(ref, lead, j, count, start, width):
    return ref[(*lead, pl.ds(j, count), pl.ds(start, width))].reshape(count * width, D)


def blocks_of(i):
    y, xx = i // 2, i % 2
    return y, (
        (y * 4 + 3 * xx, 3 * xx, pl.multiple_of(xx * 128, 128), 128),
        (y * 4 + 1 + xx, 1 + xx, 0, 256),
    )


def own_rows(ref, y, x):
    return ref[y, pl.ds(pl.multiple_of(x * CUBE, CUBE), CUBE), :]


def lane_max(s):
    out = s[:, 0:128]
    for k in range(128, s.shape[1], 128):
        out = jnp.maximum(out, s[:, k : k + 128])
    return out


def lane_sum(s):
    out = s[:, 0:128]
    for k in range(128, s.shape[1], 128):
        out = out + s[:, k : k + 128]
    return out


def own_kernel(scans, cot, wp, wv, wo, xs, cs, p0, v0, g0):
    shuffle = to_blocks_matrix()
    for y in range(2):
        x = dot(shuffle, scans[:, 4 * y : 4 * y + 4].reshape(ROW, D)).astype(BF16)
        c = dot(shuffle, cot[:, 4 * y : 4 * y + 4].reshape(ROW, D)).astype(BF16)
        xs[y] = x
        cs[y] = c
        p0[y] = dot(x, wp[...]).astype(BF16)
        v0[y] = dot(x, wv[...]).astype(BF16)
        g0[y] = dot(c, wo[...], NT).astype(BF16)


def mid_kernel(zl, zm, zh, wp, wv, p0, bias_a, bias_b, pm, vm, a1, ml, s_scr, e_scr):
    shuffle = to_blocks_matrix()
    mask = head_mask()
    for z, slab in enumerate((zl, zm, zh)):
        for y in range(2):
            x = dot(shuffle, slab[:, 4 * y : 4 * y + 4].reshape(ROW, D)).astype(BF16)
            pm[2 * z + y] = dot(x, wp[...]).astype(BF16)
            vm[2 * z + y] = dot(x, wv[...]).astype(BF16)

    def step(i, carry):
        y, pair = blocks_of(i)
        for which, (b, x, start, width) in enumerate(pair):
            bias = (bias_a, bias_b)[which]
            q = spread(own_rows(p0, y, x), mask, 0.125).astype(BF16)
            top = None
            for j, count in chunks(6, width):
                cols = slice(j * width, (j + count) * width)
                s = dot(q, take(pm, (), j, count, start, width), NT) + bias[i, :, cols]
                s_scr[which, :, cols] = s
                part = lane_max(s)
                top = part if top is None else jnp.maximum(top, part)
            top = jnp.max(top, axis=1, keepdims=True)
            total = None
            for j, count in chunks(6, width):
                cols = slice(j * width, (j + count) * width)
                e = jnp.exp(s_scr[which, :, cols] - top)
                e_scr[which, :, cols] = e.astype(BF16)
                part = lane_sum(e)
                total = part if total is None else total + part
            total = jnp.sum(total, axis=1, keepdims=True)
            wide = dot(e_scr[which, :, 0 : 6 * width], take(vm, (), 0, 6, start, width))
            a1[b] = collect(wide, mask)
            ml[b] = jnp.where(iota2((ROW, 128), 1) < 64, top, total)
        return carry

    lax.fori_loop(0, 4, step, 0)


def edge_kernel(
    lo, hi, wp, wv, wo, p0, g0, cs, bias_a, bias_b, a1, ml,
    pe, ve, cols_out, rows_out, mixed, gout, s_scr, e_scr, att,
):
    shuffle = to_blocks_matrix()
    back = from_blocks_matrix()
    mask = head_mask()
    for side, rows in enumerate((lo, hi)):
        for z in range(3):
            x = dot(shuffle, rows[z].reshape(ROW, D)).astype(BF16)
            pe[side, z] = dot(x, wp[...]).astype(BF16)
            ve[side, z] = dot(x, wv[...]).astype(BF16)

    def step(i, carry):
        y, pair = blocks_of(i)
        for which, (b, x, start, width) in enumerate(pair):
            bias = (bias_a, bias_b)[which]
            q = spread(own_rows(p0, y, x), mask, 0.125).astype(BF16)
            top1 = ml[b, :, 0:1]
            total1 = ml[b, :, 64:65]
            top = None
            for j, count in chunks(3, width):
                cols = slice(j * width, (j + count) * width)
                wide_cols = slice((6 + j) * width, (6 + j + count) * width)
                s = dot(q, take(pe, (y,), j, count, start, width), NT) + bias[i, :, wide_cols]
                s_scr[which, :, cols] = s
                part = lane_max(s)
                top = part if top is None else jnp.maximum(top, part)
            top = jnp.maximum(jnp.max(top, axis=1, keepdims=True), top1)
            total = None
            for j, count in chunks(3, width):
                cols = slice(j * width, (j + count) * width)
                e = jnp.exp(s_scr[which, :, cols] - top)
                e_scr[which, :, cols] = e.astype(BF16)
                part = lane_sum(e)
                total = part if total is None else total + part
            keep = jnp.exp(top1 - top)
            total = jnp.sum(total, axis=1, keepdims=True) + total1 * keep
            wide = dot(e_scr[which, :, 0 : 3 * width], take(ve, (y,), 0, 3, start, width))
            inverse = 1.0 / total
            attended = a1[b] * collect(jnp.broadcast_to(keep * inverse, (ROW, D)), mask)
            attended = (attended + collect(wide * inverse, mask)).astype(BF16)
            att[y, pl.ds(pl.multiple_of(x * CUBE, CUBE), CUBE), :] = attended
            product = own_rows(g0, y, x).astype(F32) * attended.astype(F32)
            delta = jnp.sum(spread(product, mask), axis=1, keepdims=True)
            log_total = top + jnp.log(total)
            both = jnp.where(iota2((ROW, 128), 1) < 64, log_total, delta)
            cols_out[b] = both
            turned = jnp.transpose(both)
            rows_out[b, 0:1] = turned[0:1]
            rows_out[b, 1:2] = turned[64:65]
        return carry

    lax.fori_loop(0, 4, step, 0)
    for y in range(2):
        out = dot(att[y], wo[...]).astype(BF16)
        mixed[:, 4 * y : 4 * y + 4] = dot(back, out).astype(BF16).reshape(4, 4, 16, D)
    gout[...] = dot(att[0], cs[0], TN) + dot(att[1], cs[1], TN)


def query_kernel(p0, g0, pm, vm, pe, ve, stats, bias_a, bias_b, qg, w_scr):
    mask = head_mask()

    def step(i, carry):
        y, pair = blocks_of(i)
        for which, (b, x, start, width) in enumerate(pair):
            bias = (bias_a, bias_b)[which]
            q = spread(own_rows(p0, y, x), mask, 0.125).astype(BF16)
            g = spread(own_rows(g0, y, x), mask).astype(BF16)
            lse = stats[b, :, 0:1]
            delta = stats[b, :, 64:65]
            for rows, base, k_ref, v_ref, lead in (
                (6, 0, pm, vm, ()),
                (3, 6, pe, ve, (y,)),
            ):
                for j, count in chunks(rows, width):
                    cols = slice((base + j) * width, (base + j + count) * width)
                    s = dot(q, take(k_ref, lead, j, count, start, width), NT)
                    pushed = dot(g, take(v_ref, lead, j, count, start, width), NT)
                    w = jnp.exp((s - lse) + bias[i, :, cols])
                    w_scr[which, :, cols] = (w * (pushed - delta)).astype(BF16)
            wide = dot(w_scr[which, :, 0 : 6 * width], take(pm, (), 0, 6, start, width))
            wide = wide + dot(
                w_scr[which, :, 6 * width : 9 * width], take(pe, (y,), 0, 3, start, width)
            )
            qg[b] = collect(wide, mask)
        return carry

    lax.fori_loop(0, 4, step, 0)


def key_kernel(
    zl, zm, zh, lo, hi, wp, wv, wo, p0, v0, xs, pm, pe, smid, sedge, bias_a, bias_b, qg, gout,
    grad, part, gm, ge, w_scr, s_scr, pg, vg,
):
    shuffle = to_blocks_matrix()
    back = from_blocks_matrix()
    mask = head_mask()
    for z, slab in enumerate((zl, zm, zh)):
        for y in range(2):
            c = dot(shuffle, slab[:, 4 * y : 4 * y + 4].reshape(ROW, D)).astype(BF16)
            gm[2 * z + y] = dot(c, wo[...], NT).astype(BF16)
    for side, rows in enumerate((lo, hi)):
        for z in range(3):
            c = dot(shuffle, rows[z].reshape(ROW, D)).astype(BF16)
            ge[side, z] = dot(c, wo[...], NT).astype(BF16)

    def step(i, carry):
        y, pair = blocks_of(i)
        for which, (b, x, start, width) in enumerate(pair):
            bias = (bias_a, bias_b)[which]
            k = spread(own_rows(p0, y, x), mask, 0.125).astype(BF16)
            v = spread(own_rows(v0, y, x), mask).astype(BF16)
            for rows, base, q_ref, g_ref, s_ref, lead in (
                (6, 0, pm, gm, smid, ()),
                (3, 6, pe, ge, sedge, (y,)),
            ):
                for j, count in chunks(rows, width):
                    cols = slice((base + j) * width, (base + j + count) * width)
                    s = dot(k, take(q_ref, lead, j, count, start, width), NT)
                    pushed = dot(v, take(g_ref, lead, j, count, start, width), NT)
                    stat = [s_ref[(*lead, j + n, slice(None), pl.ds(start, width))] for n in range(count)]
                    stat = stat[0] if count == 1 else jnp.concatenate(stat, axis=1)
                    lse = stat[0:4] - bias[i, :, cols]
                    delta = stat[4:8]
                    for h in range(HEADS):
                        hs = slice(64 * h, 64 * h + 64)
                        w = jnp.exp(s[hs] - lse[h : h + 1])
                        w_scr[which, hs, cols] = w.astype(BF16)
                        s_scr[which, hs, cols] = (w * (pushed[hs] - delta[h : h + 1])).astype(BF16)
            mid = slice(0, 6 * width)
            far = slice(6 * width, 9 * width)
            here = pl.ds(pl.multiple_of(x * CUBE, CUBE), CUBE)
            kg = dot(s_scr[which, :, mid], take(pm, (), 0, 6, start, width))
            kg = kg + dot(s_scr[which, :, far], take(pe, (y,), 0, 3, start, width))
            pg[y, here, :] = ((collect(kg, mask) + qg[b]) * 0.125).astype(BF16)
            val = dot(w_scr[which, :, mid], take(gm, (), 0, 6, start, width))
            val = val + dot(w_scr[which, :, far], take(ge, (y,), 0, 3, start, width))
            vg[y, here, :] = collect(val, mask).astype(BF16)
        return carry

    lax.fori_loop(0, 4, step, 0)
    for y in range(2):
        out = (dot(pg[y], wp[...], NT) + dot(vg[y], wv[...], NT)).astype(BF16)
        grad[:, 4 * y : 4 * y + 4] = dot(back, out).astype(BF16).reshape(4, 4, 16, D)
    part[:, 0:256] = (dot(xs[0], pg[0], TN) + dot(xs[1], pg[1], TN)).astype(BF16)
    part[:, 256:512] = (dot(xs[0], vg[0], TN) + dot(xs[1], vg[1], TN)).astype(BF16)
    part[:, 512:768] = gout[...].astype(BF16)


def call(body, outs, scratch=(), flops=0, name=None):
    return pl.pallas_call(
        body,
        out_shape=tuple(jax.ShapeDtypeStruct(shape, dtype) for shape, dtype in outs),
        scratch_shapes=list(scratch),
        compiler_params=pltpu.CompilerParams(vmem_limit_bytes=48 * 1024 * 1024),
        cost_estimate=pl.CostEstimate(flops=flops, bytes_accessed=4 * 1024 * 1024, transcendentals=0),
        name=name,
    )


def shift(block, other, dz, dy):
    scans, depth, height = (lax.axis_size(axis) for axis in AXES)
    route = []
    for s in range(scans):
        for z in range(depth):
            for y in range(height):
                if 0 <= z + dz < depth and 0 <= y + dy < height:
                    target = s ^ other
                    route.append(
                        (
                            (s * depth + z) * height + y,
                            (target * depth + z + dz) * height + y + dy,
                        )
                    )
    return lax.ppermute(block, AXES, route)


def slabs(own):
    return shift(own, 1, 1, 0), shift(own, 1, 0, 0), shift(own, 1, -1, 0)


def window_biases(flags):
    depth, height = lax.axis_size("gz"), lax.axis_size("gy")
    side = lax.axis_index("scan")
    plane = lax.axis_index("gz")
    row = lax.axis_index("gy") * 2
    near = jnp.pad(flags, ((0, 0), (1, 1), (1, 1), (0, 0)))
    near_other = lax.dynamic_slice(near, (1 - side, plane, row, 0), (1, 3, 4, 4))[0]
    near_own = lax.dynamic_slice(flags, (side, plane, row, 0), (1, 1, 2, 4))[0, 0]
    inside = jnp.pad(jnp.ones((depth, 2 * height), jnp.int32), 1)
    near_inside = lax.dynamic_slice(inside, (plane, row), (3, 4))

    def nine(window):
        middle = window[:, 1:3].reshape((6,) + window.shape[2:])
        return jnp.stack(
            [jnp.concatenate([middle, window[:, 0]]), jnp.concatenate([middle, window[:, 3]])]
        )

    xs = np.arange(4)
    adjacent = np.abs(xs[:, None] - xs[None, :]) <= 1
    center = np.zeros((2, 4, 9, 4), bool)
    for y in range(2):
        for x in range(4):
            center[y, x, 2 + y, x] = True
    adjacent = adjacent[None, :, None, :]
    query = adjacent & ((nine(near_other)[:, None] > 0) | center)
    key = adjacent & (nine(near_inside)[:, None, :, None] > 0)
    key = key & ((near_own[:, :, None, None] > 0) | center)
    result = []
    for valid in (query, key):
        bias = jnp.where(valid, 0.0, NEG).astype(F32)
        a = jnp.stack([bias[:, 0, :, 0:2], bias[:, 3, :, 2:4]], axis=1)
        b = bias[:, 1:3]
        result.append(jnp.repeat(a.reshape(4, 1, 18), CUBE, axis=2))
        result.append(jnp.repeat(b.reshape(4, 1, 36), CUBE, axis=2))
    return result


def total_of(part):
    depth, height = lax.axis_size("gz"), lax.axis_size("gy")
    half = part.shape[0] // 2
    side = lax.axis_index("scan")
    mine = lax.dynamic_slice_in_dim(part, side * half, half, 0)
    other = lax.dynamic_slice_in_dim(part, (1 - side) * half, half, 0)
    mine = (mine.astype(F32) + shift(other, 1, 0, 0).astype(F32)).astype(BF16)
    places = depth * height
    got = lax.all_to_all(
        mine.reshape(places, -1), ("gz", "gy"), 0, 0, tiled=True
    )
    total = jnp.sum(got.astype(F32), axis=0).astype(BF16)
    full = lax.all_to_all(
        jnp.broadcast_to(total[None], got.shape), ("gz", "gy"), 0, 0, tiled=True
    ).reshape(half, -1)
    away = shift(full, 1, 0, 0)
    first = jnp.where(side == 0, full, away)
    second = jnp.where(side == 0, away, full)
    return jnp.concatenate([first, second], axis=0).astype(F32)


def on_device(scans, proj_weight, value_weight, out_weight, flags, cotangent):
    own = scans[0]
    cot = cotangent[0]
    weights = (proj_weight, value_weight, out_weight)
    wide = (ROW, D)
    unit = 2 * ROW * ROW * D

    zl, zm, zh = slabs(own)
    lo = shift(jnp.stack([zl[:, 4:], zm[:, 4:], zh[:, 4:]]), 0, 0, 1)
    hi = shift(jnp.stack([zl[:, :4], zm[:, :4], zh[:, :4]]), 0, 0, -1)
    query_a, query_b, key_a, key_b = window_biases(flags)
    xs, cs, p0, v0, g0 = call(own_kernel, [((2,) + wide, BF16)] * 5, flops=10 * unit, name="own")(
        own, cot, *weights
    )
    pm, vm, a1, ml = call(
        mid_kernel,
        [((6,) + wide, BF16)] * 2 + [((8, CUBE, D), F32), ((8, ROW, 128), F32)],
        [pltpu.VMEM((2, ROW, 1536), F32), pltpu.VMEM((2, ROW, 1536), BF16)],
        flops=300 * unit,
        name="mid",
    )(zl, zm, zh, proj_weight, value_weight, p0, query_a, query_b)
    czl, czm, czh = slabs(cot)
    clo = shift(jnp.stack([czl[:, 4:], czm[:, 4:], czh[:, 4:]]), 0, 0, 1)
    chi = shift(jnp.stack([czl[:, :4], czm[:, :4], czh[:, :4]]), 0, 0, -1)
    pe, ve, stat_cols, stat_rows, mixed, gout = call(
        edge_kernel,
        [((2, 3) + wide, BF16)] * 2
        + [((8, ROW, 128), F32), ((8, 2, ROW), F32), (own.shape, BF16), (wide, F32)],
        [
            pltpu.VMEM((2, ROW, 768), F32),
            pltpu.VMEM((2, ROW, 768), BF16),
            pltpu.VMEM((2,) + wide, BF16),
        ],
        flops=200 * unit,
        name="edge",
    )(lo, hi, *weights, p0, g0, cs, query_a, query_b, a1, ml)
    stat_rows = stat_rows.reshape(2, 4, 2, HEADS, CUBE).transpose(0, 2, 3, 1, 4).reshape(2, 8, ROW)
    szl, szm, szh = slabs(stat_rows)
    slo = shift(jnp.stack([szl[1], szm[1], szh[1]]), 0, 0, 1)
    shi = shift(jnp.stack([szl[0], szm[0], szh[0]]), 0, 0, -1)
    smid = jnp.concatenate([szl, szm, szh])
    sedge = jnp.stack([slo, shi])
    (qg,) = call(
        query_kernel,
        [((8, CUBE, D), F32)],
        [pltpu.VMEM((2, ROW, 2304), BF16)],
        flops=400 * unit,
        name="query",
    )(p0, g0, pm, vm, pe, ve, stat_cols, query_a, query_b)
    grad, part = call(
        key_kernel,
        [(own.shape, BF16), ((ROW, 3 * D), BF16)],
        [
            pltpu.VMEM((6,) + wide, BF16),
            pltpu.VMEM((2, 3) + wide, BF16),
            pltpu.VMEM((2, ROW, 2304), BF16),
            pltpu.VMEM((2, ROW, 2304), BF16),
            pltpu.VMEM((2,) + wide, BF16),
            pltpu.VMEM((2,) + wide, BF16),
        ],
        flops=500 * unit,
        name="key",
    )(czl, czm, czh, clo, chi, *weights, p0, v0, xs, pm, pe, smid, sedge, key_a, key_b, qg, gout)
    summed = total_of(part)
    return (
        mixed[None],
        grad[None],
        summed[:, 0:256],
        summed[:, 256:512],
        summed[:, 512:768],
    )


def solution(mesh):
    field = P("scan", "gz", "gy", None, None)
    return jax.shard_map(
        on_device,
        mesh=mesh,
        in_specs=(field, P(), P(), P(), P(), field),
        out_specs=(field, field, P(), P(), P()),
        check_vma=False,
    )
```

time: 773 us -> 171 us (0.22)
  waiting for transfers between devices: 291 us -> 11.4 us
  local copies, waits for them, and re-layouts: 236 us -> 19.3 us
  matrix products: 78.6 us -> 0 us
  loops' own time: 67.8 us -> 0 us
  blocking collectives: 0 us -> 48.9 us
  Pallas kernels: 0 us -> 39.4 us
  starting transfers between devices: 62.3 us -> 44.2 us
  between operations: 14.8 us -> 1.25 us
  other arithmetic: 16.2 us -> 5.81 us
    psum x1 -> x0, waiting for transfers between devices: 262 us -> none  [on_device(): lax.psum((local_proj, local_value, local_out), ('scan', 'gz', 'gy'))]
    reshape x81 -> x12, local copies, waits for them, and re-layouts: 102 us -> 0.95 us  [the longest x4 0.4 us: window_biases(): result.append(jnp.repeat(a.reshape(4, 1, 18), CUBE, axis=2))]
    dot_general x49 -> x0, matrix products: 78.6 us -> none  [the longest x8 27.3 us: key_block(): jnp.einsum('hkq,qhd->khd', slopes, queries, preferred_element_type=jnp.fl...]
    dynamic_slice x108 -> x4, local copies, waits for them, and re-layouts: 73 us -> 0.98 us  [the longest x2 0.87 us: window_biases(): lax.dynamic_slice(near, (1 - side, plane, row, 0), (1, 3, 4, 4))[0]]
    another operation x2 -> x0, loops' own time: 67.8 us -> none  [the longest x1 35.7 us: on_device(): lax.map(key_block, (jnp.arange(total_blocks, dtype=jnp.int32), kept_scores))]
    all_to_all x0 -> x2, blocking collectives: none -> 48.9 us  [the longest x1 30.5 us: total_of(): lax.all_to_all(mine.reshape(places, -1), ('gz', 'gy'), 0, 0, tiled=True)]
    pallas_call x0 -> x5, Pallas kernels: none -> 39.4 us  [the longest x1 11.3 us: on_device(): call(key_kernel, [(own.shape, BF16), ((ROW, 3 * D), BF16)], [pltpu.VMEM((...]
    dynamic_update_slice x48 -> x0, local copies, waits for them, and re-layouts: 23 us -> none  [on_device(): lax.map(query_block, jnp.arange(total_blocks, dtype=jnp.int32))]
  transfers between devices with their start and end apart: 26 -> 17, of which waited for: 4 -> 5; matrix products, arithmetic and copies ran while one was open for 23% -> 4% of each run, Pallas kernels for 0% -> 17%
where the time goes in v1:
time: 171 us; the launch traced here: 170 us
  blocking collectives  48.9 us (29%)
  starting transfers between devices  44.2 us (26%)
  Pallas kernels  39.4 us (23%)
  local copies, waits for them, and re-layouts  19.3 us (11%)
  waiting for transfers between devices  11.4 us (7%)
  other arithmetic  5.81 us (3%)
    ppermute x17, starting transfers between devices, shift(): return lax.ppermute(block, AXES, route)  44.2 us
    all_to_all x1, blocking collectives, total_of(): lax.all_to_all(mine.reshape(places, -1), ('gz', 'gy'), 0, 0, tiled=True)  30.5 us
    all_to_all x1, blocking collectives, total_of(): lax.all_to_all(jnp.broadcast_to(total[None], got.shape), ('gz', 'gy'), 0,...  18.3 us
    unnamed x51, local copies, waits for them, and re-layouts  14.2 us
    ppermute x17, waiting for transfers between devices, shift(): return lax.ppermute(block, AXES, route)  11.4 us
    pallas_call x1, Pallas kernels, on_device(): call(key_kernel, [(own.shape, BF16), ((ROW, 3 * D), BF16)], [pltpu.VMEM((...  11.3 us
    pallas_call x1, Pallas kernels, on_device(): call(edge_kernel, [((2, 3) + wide, BF16)] * 2 + [((8, ROW, 128), F32), ((...  10.4 us
    pallas_call x1, Pallas kernels, on_device(): call(query_kernel, [((8, CUBE, D), F32)], [pltpu.VMEM((2, ROW, 2304), BF1...  9.06 us
  transfers between devices with their start and end apart: 17, of which 5 were waited for; matrix products, arithmetic and copies ran while one was open for 4% of the time, Pallas kernels for 17%

profile of v1, /device:TPU:1, one launch (start us, length us, event | category | flops | bytes accessed | tf_op | source)
XLA Modules:
  0.0 170.3 jit_solution(2650963560943229888)
XLA Ops:
  0.6 4.9 %collective-permute-start = (bf16[4,8,16,256]{3,2,1,0:T(8,128)(2,1)}, bf16[4,8,16,256]{3,2,1,0:T(8,128)(2,1)S(1)}, u32[]{:S(2)}, u32[]{:S(2)}) collective-permute-start(bf16[4,8,16,256]{3,2,1,0:T(8,128)(2,1)} %bitcast.56), channel_id=1, source_target_pairs={{0,136},{1,137},{2,138},{3,139},{4,140},{5,141},{6,142},{7,143},{8... | collective-permute-start | bytes 786440 | tf_op jit(solution)/shard_map/ppermute | solution.py:324
  5.7 1.3 collective-permute-start.2
  7.0 4.5 %collective-permute-start.5 = (bf16[4,8,16,256]{3,2,1,0:T(8,128)(2,1)}, bf16[4,8,16,256]{3,2,1,0:T(8,128)(2,1)S(1)}, u32[]{:S(2)}, u32[]{:S(2)}) collective-permute-start(bf16[4,8,16,256]{3,2,1,0:T(8,128)(2,1)} %bitcast.60), channel_id=1, source_target_pairs={{0,136},{1,137},{2,138},{3,139},{4,140},{5,141},{6,142},{7,143},{8... | collective-permute-start | bytes 786440 | tf_op jit(solution)/shard_map/ppermute | solution.py:324
  18.3 1.3 collective-permute-start.7
  19.8 4.8 %collective-permute-start.3 = (bf16[3,4,4,16,256]{4,3,2,1,0:T(8,128)(2,1)S(1)}, bf16[3,4,4,16,256]{4,3,2,1,0:T(8,128)(2,1)S(1)}, u32[]{:S(2)}, u32[]{:S(2)}) collective-permute-start(bf16[3,4,4,16,256]{4,3,2,1,0:T(8,128)(2,1)S(1)} %pad_maximum_fusion), channel_id=1, source_target_pairs={{0,1},{1,2},{2,3},{3,4},{4,5},{5,6},{6,7},{8,9},{9,10},{10,11},{11... | collective-permute-start | bytes 1179656 | tf_op jit(solution)/shard_map/ppermute | solution.py:324
  24.7 1.3 collective-permute-start.4
  26.0 2.4 %collective-permute-done.7.zh = bf16[4,8,16,256]{3,2,1,0:T(8,128)(2,1)S(1)} collective-permute-done((bf16[4,8,16,256]{3,2,1,0:T(8,128)(2,1)S(1)}, bf16[4,8,16,256]{3,2,1,0:T(8,128)(2,1)S(1)}, u32[]{:S(2)}, u32[]{:S(2)}) %collective-permute-start.7) | collective-permute-done | bytes 262176 | tf_op jit(solution)/shard_map/ppermute | solution.py:324
  29.2 5.1 %collective-permute-start.8 = (bf16[3,4,4,16,256]{4,3,2,1,0:T(8,128)(2,1)}, bf16[3,4,4,16,256]{4,3,2,1,0:T(8,128)(2,1)S(1)}, u32[]{:S(2)}, u32[]{:S(2)}) collective-permute-start(bf16[3,4,4,16,256]{4,3,2,1,0:T(8,128)(2,1)} %pad_maximum_fusion.2), channel_id=1, source_target_pairs={{0,1},{1,2},{2,3},{3,4},{4,5},{5,6},{6,7},{8,9},{9,10},{10,11},{11... | collective-permute-start | bytes 1179656 | tf_op jit(solution)/shard_map/ppermute | solution.py:324
  35.2 1.3 collective-permute-start.9
  36.5 8.1 %mid.1 = (bf16[6,256,256]{2,1,0:T(8,128)(2,1)S(1)}, bf16[6,256,256]{2,1,0:T(8,128)(2,1)S(1)}, f32[8,64,256]{2,1,0:T(8,128)S(1)}, f32[8,256,128]{2,1,0:T(8,128)S(1)}) custom-call(bf16[4,8,16,256]{3,2,1,0:T(8,128)(2,1)S(1)} %collective-permute-done.zl, bf16[4,8,16,256]{3,2,1,0:T(8,128)(2,1)S(1)} %collective-permute-done.1.zm, ...), custom_call_target="tpu_custom_call" | custom-call | flops 10066329600 | bytes 4194304 | tf_op jit(solution)/shard_map/mid/pallas_call | solution.py:403
  47.3 2.3 %collective-permute-done.3.lo = bf16[3,4,4,16,256]{4,3,2,1,0:T(8,128)(2,1)S(1)} collective-permute-done((bf16[3,4,4,16,256]{4,3,2,1,0:T(8,128)(2,1)S(1)}, bf16[3,4,4,16,256]{4,3,2,1,0:T(8,128)(2,1)S(1)}, u32[]{:S(2)}, u32[]{:S(2)}) %collective-permute-start.3) | collective-permute-done | bytes 393248 | tf_op jit(solution)/shard_map/ppermute | solution.py:324
  49.7 10.4 %edge.1 = (bf16[2,3,256,256]{3,2,1,0:T(8,128)(2,1)S(1)}, bf16[2,3,256,256]{3,2,1,0:T(8,128)(2,1)S(1)}, f32[8,256,128]{2,1,0:T(8,128)S(1)}, f32[8,2,256]{2,1,0:T(...) custom-call(bf16[3,4,4,16,256]{4,3,2,1,0:T(8,128)(2,1)S(1)} %collective-permute-done.3.lo, ...), custom_call_target="tpu_custom_call" | custom-call | flops 6710886400 | bytes 4194304 | tf_op jit(solution)/shard_map/edge/pallas_call | solution.py:413
  63.0 5.8 %collective-permute-start.10 = (f32[2,8,256]{2,1,0:T(8,128)S(1)}, f32[2,8,256]{2,1,0:T(8,128)S(1)}, u32[]{:S(2)}, u32[]{:S(2)}) collective-permute-start(f32[2,8,256]{2,1,0:T(8,128)S(1)} %reshape.115), channel_id=1, source_target_pairs={{0,136},{1,137},{2,138},{3,139},{4,140},{5,141},{6,142},{7,143},{8... | collective-permute-start | bytes 49160 | tf_op jit(solution)/shard_map/ppermute | solution.py:324
  69.0 1.3 collective-permute-start.12
  77.0 9.1 %query.1.qg = f32[8,64,256]{2,1,0:T(8,128)S(1)} custom-call(bf16[2,256,256]{2,1,0:T(8,128)(2,1)S(1)} %get-tuple-element.22.p0, bf16[2,256,256]{2,1,0:T(8,128)(2,1)S(1)} %copy-done.8, bf16[6,256,256]{2,1,0:T(8,128)(2,1)S(1)} %copy-done.18, bf16[6,256,256]{2,1,0:T(8,128)(2,1)S(1)} %copy-done.20, bf16[2,3,256,256]{3,2,1,0:T(8,128)(2,1)S(1)} %copy-done.13, ...), custom_call_target="tpu_custom_call" | custom-call | flops 13421772800 | bytes 4194304 | tf_op jit(solution)/shard_map/query/pallas_call | solution.py:431
  86.1 5.6 %collective-permute-start.13 = (f32[3,8,256]{2,1,0:T(8,128)S(1)}, f32[3,8,256]{2,1,0:T(8,128)S(1)}, u32[]{:S(2)}, u32[]{:S(2)}) collective-permute-start(f32[3,8,256]{2,1,0:T(8,128)S(1)} %pad_maximum_fusion.6), channel_id=1, source_target_pairs={{0,1},{1,2},{2,3},{3,4},{4,5},{5,6},{6,7},{8,9},{9,10},{10,11},{11... | collective-permute-start | bytes 73736 | tf_op jit(solution)/shard_map/ppermute | solution.py:324
  91.8 1.5 collective-permute-start.14
  93.3 4.6 %collective-permute-done.14 = f32[3,8,256]{2,1,0:T(8,128)S(1)} collective-permute-done((f32[3,8,256]{2,1,0:T(8,128)S(1)}, f32[3,8,256]{2,1,0:T(8,128)S(1)}, u32[]{:S(2)}, u32[]{:S(2)}) %collective-permute-start.14) | collective-permute-done | bytes 24608 | tf_op jit(solution)/shard_map/ppermute | solution.py:324
  97.9 11.3 %key.1 = (bf16[4,8,16,256]{3,2,1,0:T(8,128)(2,1)}, bf16[256,768]{1,0:T(8,128)(2,1)S(1)}) custom-call(bf16[4,8,16,256]{3,2,1,0:T(8,128)(2,1)S(1)} %collective-permute-done.5.zl, bf16[4,8,16,256]{3,2,1,0:T(8,128)(2,1)S(1)} %collective-permute-done.6.zm, bf16[4,8,16,256]{3,2,1,0:T(8,128)(2,1)S(1)} %collective-permute-done.7.zh, ...), custom_call_target="tpu_custom_call" | custom-call | flops 16777216000 | bytes 4194304 | tf_op jit(solution)/shard_map/key/pallas_call | solution.py:438
  109.2 2.0 %collective-permute-start.15 = (bf16[128,768]{1,0:T(8,128)(2,1)S(1)}, bf16[128,768]{1,0:T(8,128)(2,1)S(1)}, u32[]{:S(2)}, u32[]{:S(2)}) collective-permute-start(bf16[128,768]{1,0:T(8,128)(2,1)S(1)} %constant_dynamic-slice_fusion), channel_id=1, source_target_pairs={{0,128},{1,129},{2,130},{3,131},{4,132},{5,133},{6,134},{7,135},{8... | collective-permute-start | bytes 589832 | tf_op jit(solution)/shard_map/ppermute | solution.py:324
  113.6 30.5 %all_to_all.18 = bf16[128,2,384]{2,1,0:T(2,128)(2,1)S(1)} all-to-all(bf16[128,2,384]{2,1,0:T(2,128)(2,1)S(1)} %reshape.121), channel_id=1, replica_groups=mesh['scan'=2,'gz'=16,'gy'=8] {'gz','gy'}, dimensions={0} | all-to-all | bytes 393216 | tf_op jit(solution)/shard_map/all_to_all | solution.py:376
  144.9 1.8 %reduce.3 = bf16[128,768]{1,0:T(8,128)(2,1)S(1)} reduce(bf16[128,1,768]{2,1,0:T(2,128)(2,1)S(1)} %broadcast_in_dim.60, bf16[]{:T(256)} %broadcast.46), dimensions={1}, to_apply=%broadcast_in_dim.60.reduce_sub_computation | reduce | bytes 393218 | tf_op jit(solution)/shard_map/broadcast_in_dim | solution.py:381
  146.8 18.3 %all_to_all.19 = bf16[128,2,384]{2,1,0:T(2,128)(2,1)S(1)} all-to-all(bf16[128,2,384]{2,1,0:T(2,128)(2,1)S(1)} %reshape.123), channel_id=1, replica_groups=mesh['scan'=2,'gz'=16,'gy'=8] {'gz','gy'}, dimensions={0} | all-to-all | bytes 393216 | tf_op jit(solution)/shard_map/all_to_all | solution.py:380
  165.3 2.9 %collective-permute-start.16 = (bf16[128,768]{1,0:T(8,128)(2,1)S(1)}, bf16[128,768]{1,0:T(8,128)(2,1)S(1)}, u32[]{:S(2)}, u32[]{:S(2)}) collective-permute-start(bf16[128,768]{1,0:T(8,128)(2,1)S(1)} %bitcast.64), channel_id=1, source_target_pairs={{0,128},{1,129},{2,130},{3,131},{4,132},{5,133},{6,134},{7,135},{8... | collective-permute-start | bytes 589832 | tf_op jit(solution)/shard_map/ppermute | solution.py:324
  (140 shorter events, 26.6 us)
Async XLA Ops:
  0.6 17.7 %collective-permute-start = (bf16[4,8,16,256]{3,2,1,0:T(8,128)(2,1)}, bf16[4,8,16,256]{3,2,1,0:T(8,128)(2,1)S(1)}, u32[]{:S(2)}, u32[]{:S(2)}) collective-permute-start(bf16[4,8,16,256]{3,2,1,0:T(8,128)(2,1)} %bitcast.56), channel_id=1, source_target_pairs={{0,136},{1,137},{2,138},{3,139},{4,140},{5,141},{6,142},{7,143},{8... | collective-permute-start | bytes 786440 | tf_op jit(solution)/shard_map/ppermute | solution.py:324
  5.6 14.1 %collective-permute-start.1 = (bf16[4,8,16,256]{3,2,1,0:T(8,128)(2,1)}, bf16[4,8,16,256]{3,2,1,0:T(8,128)(2,1)S(1)}, u32[]{:S(2)}, u32[]{:S(2)}) collective-permute-start(bf16[4,8,16,256]{3,2,1,0:T(8,128)(2,1)} %bitcast.57), channel_id=1, source_target_pairs={{0,128},{1,129},{2,130},{3,131},{4,132},{5,133},{6,134},{7,135},{8... | collective-permute-start | bytes 786440 | tf_op jit(solution)/shard_map/ppermute | solution.py:324
  5.7 14.0 %collective-permute-start.2 = (bf16[4,8,16,256]{3,2,1,0:T(8,128)(2,1)}, bf16[4,8,16,256]{3,2,1,0:T(8,128)(2,1)S(1)}, u32[]{:S(2)}, u32[]{:S(2)}) collective-permute-start(bf16[4,8,16,256]{3,2,1,0:T(8,128)(2,1)} %bitcast.58), channel_id=1, source_target_pairs={{8,128},{9,129},{10,130},{11,131},{12,132},{13,133},{14,134},{15,1... | collective-permute-start | bytes 786440 | tf_op jit(solution)/shard_map/ppermute | solution.py:324
  7.0 19.0 %collective-permute-start.5 = (bf16[4,8,16,256]{3,2,1,0:T(8,128)(2,1)}, bf16[4,8,16,256]{3,2,1,0:T(8,128)(2,1)S(1)}, u32[]{:S(2)}, u32[]{:S(2)}) collective-permute-start(bf16[4,8,16,256]{3,2,1,0:T(8,128)(2,1)} %bitcast.60), channel_id=1, source_target_pairs={{0,136},{1,137},{2,138},{3,139},{4,140},{5,141},{6,142},{7,143},{8... | collective-permute-start | bytes 786440 | tf_op jit(solution)/shard_map/ppermute | solution.py:324
  11.5 14.5 %collective-permute-start.6 = (bf16[4,8,16,256]{3,2,1,0:T(8,128)(2,1)}, bf16[4,8,16,256]{3,2,1,0:T(8,128)(2,1)S(1)}, u32[]{:S(2)}, u32[]{:S(2)}) collective-permute-start(bf16[4,8,16,256]{3,2,1,0:T(8,128)(2,1)} %bitcast.61), channel_id=1, source_target_pairs={{0,128},{1,129},{2,130},{3,131},{4,132},{5,133},{6,134},{7,135},{8... | collective-permute-start | bytes 786440 | tf_op jit(solution)/shard_map/ppermute | solution.py:324
  15.3 1.5 copy-start.4
  15.5 1.3 copy-start.3
  18.3 31.3 %copy-start.7 = (bf16[2,256,256]{2,1,0:T(8,128)(2,1)}, bf16[2,256,256]{2,1,0:T(8,128)(2,1)S(1)}, u32[]{:S(2)}) copy-start(bf16[2,256,256]{2,1,0:T(8,128)(2,1)S(1)} %get-tuple-element.23.g0) | copy-start | bytes 786436
  18.3 10.1 %collective-permute-start.7 = (bf16[4,8,16,256]{3,2,1,0:T(8,128)(2,1)S(1)}, bf16[4,8,16,256]{3,2,1,0:T(8,128)(2,1)S(1)}, u32[]{:S(2)}, u32[]{:S(2)}) collective-permute-start(bf16[4,8,16,256]{3,2,1,0:T(8,128)(2,1)S(1)} %bitcast.63), channel_id=1, source_target_pairs={{8,128},{9,129},{10,130},{11,131},{12,132},{13,133},{14,134},{15,1... | collective-permute-start | bytes 786440 | tf_op jit(solution)/shard_map/ppermute | solution.py:324
  19.8 29.9 %collective-permute-start.3 = (bf16[3,4,4,16,256]{4,3,2,1,0:T(8,128)(2,1)S(1)}, bf16[3,4,4,16,256]{4,3,2,1,0:T(8,128)(2,1)S(1)}, u32[]{:S(2)}, u32[]{:S(2)}) collective-permute-start(bf16[3,4,4,16,256]{4,3,2,1,0:T(8,128)(2,1)S(1)} %pad_maximum_fusion), channel_id=1, source_target_pairs={{0,1},{1,2},{2,3},{3,4},{4,5},{5,6},{6,7},{8,9},{9,10},{10,11},{11... | collective-permute-start | bytes 1179656 | tf_op jit(solution)/shard_map/ppermute | solution.py:324
  24.7 25.0 %collective-permute-start.4 = (bf16[3,4,4,16,256]{4,3,2,1,0:T(8,128)(2,1)S(1)}, bf16[3,4,4,16,256]{4,3,2,1,0:T(8,128)(2,1)S(1)}, u32[]{:S(2)}, u32[]{:S(2)}) collective-permute-start(bf16[3,4,4,16,256]{4,3,2,1,0:T(8,128)(2,1)S(1)} %pad_maximum_fusion.1), channel_id=1, source_target_pairs={{1,0},{2,1},{3,2},{4,3},{5,4},{6,5},{7,6},{9,8},{10,9},{11,10},{12... | collective-permute-start | bytes 1179656 | tf_op jit(solution)/shard_map/ppermute | solution.py:324
  29.2 68.6 %collective-permute-start.8 = (bf16[3,4,4,16,256]{4,3,2,1,0:T(8,128)(2,1)}, bf16[3,4,4,16,256]{4,3,2,1,0:T(8,128)(2,1)S(1)}, u32[]{:S(2)}, u32[]{:S(2)}) collective-permute-start(bf16[3,4,4,16,256]{4,3,2,1,0:T(8,128)(2,1)} %pad_maximum_fusion.2), channel_id=1, source_target_pairs={{0,1},{1,2},{2,3},{3,4},{4,5},{5,6},{6,7},{8,9},{9,10},{10,11},{11... | collective-permute-start | bytes 1179656 | tf_op jit(solution)/shard_map/ppermute | solution.py:324
  35.2 62.7 %collective-permute-start.9 = (bf16[3,4,4,16,256]{4,3,2,1,0:T(8,128)(2,1)}, bf16[3,4,4,16,256]{4,3,2,1,0:T(8,128)(2,1)S(1)}, u32[]{:S(2)}, u32[]{:S(2)}) collective-permute-start(bf16[3,4,4,16,256]{4,3,2,1,0:T(8,128)(2,1)} %pad_maximum_fusion.3), channel_id=1, source_target_pairs={{1,0},{2,1},{3,2},{4,3},{5,4},{6,5},{7,6},{9,8},{10,9},{11,10},{12... | collective-permute-start | bytes 1179656 | tf_op jit(solution)/shard_map/ppermute | solution.py:324
  63.0 23.0 %collective-permute-start.10 = (f32[2,8,256]{2,1,0:T(8,128)S(1)}, f32[2,8,256]{2,1,0:T(8,128)S(1)}, u32[]{:S(2)}, u32[]{:S(2)}) collective-permute-start(f32[2,8,256]{2,1,0:T(8,128)S(1)} %reshape.115), channel_id=1, source_target_pairs={{0,136},{1,137},{2,138},{3,139},{4,140},{5,141},{6,142},{7,143},{8... | collective-permute-start | bytes 49160 | tf_op jit(solution)/shard_map/ppermute | solution.py:324
  68.9 17.2 %collective-permute-start.11 = (f32[2,8,256]{2,1,0:T(8,128)S(1)}, f32[2,8,256]{2,1,0:T(8,128)S(1)}, u32[]{:S(2)}, u32[]{:S(2)}) collective-permute-start(f32[2,8,256]{2,1,0:T(8,128)S(1)} %reshape.115), channel_id=1, source_target_pairs={{0,128},{1,129},{2,130},{3,131},{4,132},{5,133},{6,134},{7,135},{8... | collective-permute-start | bytes 49160 | tf_op jit(solution)/shard_map/ppermute | solution.py:324
  69.0 17.1 %collective-permute-start.12 = (f32[2,8,256]{2,1,0:T(8,128)S(1)}, f32[2,8,256]{2,1,0:T(8,128)S(1)}, u32[]{:S(2)}, u32[]{:S(2)}) collective-permute-start(f32[2,8,256]{2,1,0:T(8,128)S(1)} %reshape.115), channel_id=1, source_target_pairs={{8,128},{9,129},{10,130},{11,131},{12,132},{13,133},{14,134},{15,1... | collective-permute-start | bytes 49160 | tf_op jit(solution)/shard_map/ppermute | solution.py:324
  71.2 1.2 copy-start.10
  72.5 1.1 copy-start.13
  77.0 20.9 %copy-start.14 = (bf16[2,3,256,256]{3,2,1,0:T(8,128)(2,1)S(1)}, bf16[2,3,256,256]{3,2,1,0:T(8,128)(2,1)}, u32[]{:S(2)}) copy-start(bf16[2,3,256,256]{3,2,1,0:T(8,128)(2,1)} %copy-done.12) | copy-start | bytes 2359300
  86.1 11.8 %copy-start.6 = (bf16[2,256,256]{2,1,0:T(8,128)(2,1)S(1)}, bf16[2,256,256]{2,1,0:T(8,128)(2,1)}, u32[]{:S(2)}) copy-start(bf16[2,256,256]{2,1,0:T(8,128)(2,1)} %copy-done.5) | copy-start | bytes 786436
  86.1 7.1 %collective-permute-start.13 = (f32[3,8,256]{2,1,0:T(8,128)S(1)}, f32[3,8,256]{2,1,0:T(8,128)S(1)}, u32[]{:S(2)}, u32[]{:S(2)}) collective-permute-start(f32[3,8,256]{2,1,0:T(8,128)S(1)} %pad_maximum_fusion.6), channel_id=1, source_target_pairs={{0,1},{1,2},{2,3},{3,4},{4,5},{5,6},{6,7},{8,9},{9,10},{10,11},{11... | collective-permute-start | bytes 73736 | tf_op jit(solution)/shard_map/ppermute | solution.py:324
  91.8 6.1 %collective-permute-start.14 = (f32[3,8,256]{2,1,0:T(8,128)S(1)}, f32[3,8,256]{2,1,0:T(8,128)S(1)}, u32[]{:S(2)}, u32[]{:S(2)}) collective-permute-start(f32[3,8,256]{2,1,0:T(8,128)S(1)} %pad_maximum_fusion.7), channel_id=1, source_target_pairs={{1,0},{2,1},{3,2},{4,3},{5,4},{6,5},{7,6},{9,8},{10,9},{11,10},{12... | collective-permute-start | bytes 73736 | tf_op jit(solution)/shard_map/ppermute | solution.py:324
  109.2 3.1 %collective-permute-start.15 = (bf16[128,768]{1,0:T(8,128)(2,1)S(1)}, bf16[128,768]{1,0:T(8,128)(2,1)S(1)}, u32[]{:S(2)}, u32[]{:S(2)}) collective-permute-start(bf16[128,768]{1,0:T(8,128)(2,1)S(1)} %constant_dynamic-slice_fusion), channel_id=1, source_target_pairs={{0,128},{1,129},{2,130},{3,131},{4,132},{5,133},{6,134},{7,135},{8... | collective-permute-start | bytes 589832 | tf_op jit(solution)/shard_map/ppermute | solution.py:324
  165.3 4.0 %collective-permute-start.16 = (bf16[128,768]{1,0:T(8,128)(2,1)S(1)}, bf16[128,768]{1,0:T(8,128)(2,1)S(1)}, u32[]{:S(2)}, u32[]{:S(2)}) collective-permute-start(bf16[128,768]{1,0:T(8,128)(2,1)S(1)} %bitcast.64), channel_id=1, source_target_pairs={{0,128},{1,129},{2,130},{3,131},{4,132},{5,133},{6,134},{7,135},{8... | collective-permute-start | bytes 589832 | tf_op jit(solution)/shard_map/ppermute | solution.py:324
  (16 other events, 15.0 us)

commit v2 on v1

--- a/solution.py
+++ b/solution.py
@@ -96,6 +96,23 @@
     return out
 
 
+def lanes(column, width):
+    return column if width == 128 else jnp.concatenate([column] * (width // 128), axis=1)
+
+
+def filled(column):
+    return jnp.broadcast_to(column, (ROW, 128))
+
+
+def turned(column):
+    keep = iota2((CUBE, 128), 0) == (iota2((CUBE, 128), 1) & 63)
+    rows = [
+        jnp.sum(jnp.where(keep, column[64 * h : 64 * h + 64], 0.0), axis=0, keepdims=True)
+        for h in range(HEADS)
+    ]
+    return jnp.concatenate(rows, axis=0)
+
+
 def own_kernel(scans, cot, wp, wv, wo, xs, cs, p0, v0, g0):
     shuffle = to_blocks_matrix()
     for y in range(2):
@@ -108,7 +125,7 @@
         g0[y] = dot(c, wo[...], NT).astype(BF16)
 
 
-def mid_kernel(zl, zm, zh, wp, wv, p0, bias_a, bias_b, pm, vm, a1, ml, s_scr, e_scr):
+def mid_kernel(zl, zm, zh, wp, wv, p0, bias_a, bias_b, pm, vm, a1, top_out, sum_out, s_scr, e_scr):
     shuffle = to_blocks_matrix()
     mask = head_mask()
     for z, slab in enumerate((zl, zm, zh)):
@@ -129,33 +146,34 @@
                 s_scr[which, :, cols] = s
                 part = lane_max(s)
                 top = part if top is None else jnp.maximum(top, part)
-            top = jnp.max(top, axis=1, keepdims=True)
+            top = filled(jnp.max(top, axis=1, keepdims=True))
             total = None
             for j, count in chunks(6, width):
                 cols = slice(j * width, (j + count) * width)
-                e = jnp.exp(s_scr[which, :, cols] - top)
+                e = jnp.exp(s_scr[which, :, cols] - lanes(top, count * width))
                 e_scr[which, :, cols] = e.astype(BF16)
                 part = lane_sum(e)
                 total = part if total is None else total + part
-            total = jnp.sum(total, axis=1, keepdims=True)
+            total = filled(jnp.sum(total, axis=1, keepdims=True))
             wide = dot(e_scr[which, :, 0 : 6 * width], take(vm, (), 0, 6, start, width))
             a1[b] = collect(wide, mask)
-            ml[b] = jnp.where(iota2((ROW, 128), 1) < 64, top, total)
+            top_out[b] = top
+            sum_out[b] = total
         return carry
 
     lax.fori_loop(0, 4, step, 0)
 
 
 def edge_kernel(
-    lo, hi, wp, wv, wo, p0, g0, cs, bias_a, bias_b, a1, ml,
-    pe, ve, cols_out, rows_out, mixed, gout, s_scr, e_scr, att,
+    mid_y, low_y, high_y, wp, wv, wo, p0, g0, cs, bias_a, bias_b, a1, top_in, sum_in,
+    pe, ve, lse_out, delta_out, first_out, second_out, mixed, gout, s_scr, e_scr, att, rows_scr,
 ):
     shuffle = to_blocks_matrix()
     back = from_blocks_matrix()
     mask = head_mask()
-    for side, rows in enumerate((lo, hi)):
-        for z in range(3):
-            x = dot(shuffle, rows[z].reshape(ROW, D)).astype(BF16)
+    for z, slab in enumerate((low_y, mid_y, high_y)):
+        for side in range(2):
+            x = dot(shuffle, slab[side].reshape(ROW, D)).astype(BF16)
             pe[side, z] = dot(x, wp[...]).astype(BF16)
             ve[side, z] = dot(x, wv[...]).astype(BF16)
 
@@ -164,8 +182,8 @@
         for which, (b, x, start, width) in enumerate(pair):
             bias = (bias_a, bias_b)[which]
             q = spread(own_rows(p0, y, x), mask, 0.125).astype(BF16)
-            top1 = ml[b, :, 0:1]
-            total1 = ml[b, :, 64:65]
+            top1 = top_in[b]
+            total1 = sum_in[b]
             top = None
             for j, count in chunks(3, width):
                 cols = slice(j * width, (j + count) * width)
@@ -174,49 +192,53 @@
                 s_scr[which, :, cols] = s
                 part = lane_max(s)
                 top = part if top is None else jnp.maximum(top, part)
-            top = jnp.maximum(jnp.max(top, axis=1, keepdims=True), top1)
+            top = jnp.maximum(filled(jnp.max(top, axis=1, keepdims=True)), top1)
             total = None
             for j, count in chunks(3, width):
                 cols = slice(j * width, (j + count) * width)
-                e = jnp.exp(s_scr[which, :, cols] - top)
+                e = jnp.exp(s_scr[which, :, cols] - lanes(top, count * width))
                 e_scr[which, :, cols] = e.astype(BF16)
                 part = lane_sum(e)
                 total = part if total is None else total + part
             keep = jnp.exp(top1 - top)
-            total = jnp.sum(total, axis=1, keepdims=True) + total1 * keep
+            total = filled(jnp.sum(total, axis=1, keepdims=True)) + total1 * keep
             wide = dot(e_scr[which, :, 0 : 3 * width], take(ve, (y,), 0, 3, start, width))
             inverse = 1.0 / total
-            attended = a1[b] * collect(jnp.broadcast_to(keep * inverse, (ROW, D)), mask)
-            attended = (attended + collect(wide * inverse, mask)).astype(BF16)
+            attended = a1[b] * collect(lanes(keep * inverse, D), mask)
+            attended = (attended + collect(wide * lanes(inverse, D), mask)).astype(BF16)
             att[y, pl.ds(pl.multiple_of(x * CUBE, CUBE), CUBE), :] = attended
             product = own_rows(g0, y, x).astype(F32) * attended.astype(F32)
-            delta = jnp.sum(spread(product, mask), axis=1, keepdims=True)
+            delta = filled(jnp.sum(lane_sum(spread(product, mask)), axis=1, keepdims=True))
             log_total = top + jnp.log(total)
-            both = jnp.where(iota2((ROW, 128), 1) < 64, log_total, delta)
-            cols_out[b] = both
-            turned = jnp.transpose(both)
-            rows_out[b, 0:1] = turned[0:1]
-            rows_out[b, 1:2] = turned[64:65]
+            lse_out[b] = log_total
+            delta_out[b] = delta
+            rows_scr[b] = jnp.concatenate([turned(log_total), turned(delta)], axis=0)
         return carry
 
     lax.fori_loop(0, 4, step, 0)
+    left = iota2((8, 128), 1) < 64
+    for y, out in enumerate((first_out, second_out)):
+        for k in range(2):
+            at = 4 * y + 2 * k
+            out[:, 128 * k : 128 * k + 128] = jnp.where(left, rows_scr[at], rows_scr[at + 1])
     for y in range(2):
         out = dot(att[y], wo[...]).astype(BF16)
         mixed[:, 4 * y : 4 * y + 4] = dot(back, out).astype(BF16).reshape(4, 4, 16, D)
     gout[...] = dot(att[0], cs[0], TN) + dot(att[1], cs[1], TN)
 
 
-def query_kernel(p0, g0, pm, vm, pe, ve, stats, bias_a, bias_b, qg, w_scr):
+def query_kernel(y, p0, g0, pm, vm, pe, ve, lse_in, delta_in, bias_a, bias_b, qg, w_scr):
     mask = head_mask()
 
-    def step(i, carry):
-        y, pair = blocks_of(i)
+    def step(xx, carry):
+        i = 2 * y + xx
+        _, pair = blocks_of(i)
         for which, (b, x, start, width) in enumerate(pair):
             bias = (bias_a, bias_b)[which]
             q = spread(own_rows(p0, y, x), mask, 0.125).astype(BF16)
             g = spread(own_rows(g0, y, x), mask).astype(BF16)
-            lse = stats[b, :, 0:1]
-            delta = stats[b, :, 64:65]
+            lse = lse_in[b]
+            delta = delta_in[b]
             for rows, base, k_ref, v_ref, lead in (
                 (6, 0, pm, vm, ()),
                 (3, 6, pe, ve, (y,)),
@@ -225,33 +247,36 @@
                     cols = slice((base + j) * width, (base + j + count) * width)
                     s = dot(q, take(k_ref, lead, j, count, start, width), NT)
                     pushed = dot(g, take(v_ref, lead, j, count, start, width), NT)
-                    w = jnp.exp((s - lse) + bias[i, :, cols])
-                    w_scr[which, :, cols] = (w * (pushed - delta)).astype(BF16)
+                    w = jnp.exp((s - lanes(lse, count * width)) + bias[i, :, cols])
+                    slopes = w * (pushed - lanes(delta, count * width))
+                    w_scr[which, :, cols] = slopes.astype(BF16)
             wide = dot(w_scr[which, :, 0 : 6 * width], take(pm, (), 0, 6, start, width))
             wide = wide + dot(
                 w_scr[which, :, 6 * width : 9 * width], take(pe, (y,), 0, 3, start, width)
             )
-            qg[b] = collect(wide, mask)
+            qg[b - 4 * y] = collect(wide, mask)
         return carry
 
-    lax.fori_loop(0, 4, step, 0)
+    lax.fori_loop(0, 2, step, 0)
 
 
 def key_kernel(
-    zl, zm, zh, lo, hi, wp, wv, wo, p0, v0, xs, pm, pe, smid, sedge, bias_a, bias_b, qg, gout,
-    grad, part, gm, ge, w_scr, s_scr, pg, vg,
+    zl, zm, zh, sl, sm, sh, wp, wv, wo, p0, v0, xs, pm, pe, bias_a, bias_b, qg0, qg1, gout,
+    grad, part, gm, ge, smid, sedge, w_scr, s_scr, pg, vg,
 ):
     shuffle = to_blocks_matrix()
     back = from_blocks_matrix()
     mask = head_mask()
-    for z, slab in enumerate((zl, zm, zh)):
-        for y in range(2):
-            c = dot(shuffle, slab[:, 4 * y : 4 * y + 4].reshape(ROW, D)).astype(BF16)
-            gm[2 * z + y] = dot(c, wo[...], NT).astype(BF16)
-    for side, rows in enumerate((lo, hi)):
-        for z in range(3):
-            c = dot(shuffle, rows[z].reshape(ROW, D)).astype(BF16)
-            ge[side, z] = dot(c, wo[...], NT).astype(BF16)
+    for z, (slab, stat) in enumerate(((zl, sl), (zm, sm), (zh, sh))):
+        for r in range(4):
+            c = dot(shuffle, slab[:, 4 * r : 4 * r + 4].reshape(ROW, D)).astype(BF16)
+            g = dot(c, wo[...], NT).astype(BF16)
+            if r in (1, 2):
+                gm[2 * z + r - 1] = g
+                smid[2 * z + r - 1] = stat[r]
+            else:
+                ge[r // 3, z] = g
+                sedge[r // 3, z] = stat[r]
 
     def step(i, carry):
         y, pair = blocks_of(i)
@@ -281,7 +306,8 @@
             here = pl.ds(pl.multiple_of(x * CUBE, CUBE), CUBE)
             kg = dot(s_scr[which, :, mid], take(pm, (), 0, 6, start, width))
             kg = kg + dot(s_scr[which, :, far], take(pe, (y,), 0, 3, start, width))
-            pg[y, here, :] = ((collect(kg, mask) + qg[b]) * 0.125).astype(BF16)
+            qg = jnp.where(i < 2, qg0[b % 4], qg1[b % 4])
+            pg[y, here, :] = ((collect(kg, mask) + qg) * 0.125).astype(BF16)
             val = dot(w_scr[which, :, mid], take(gm, (), 0, 6, start, width))
             val = val + dot(w_scr[which, :, far], take(ge, (y,), 0, 3, start, width))
             vg[y, here, :] = collect(val, mask).astype(BF16)
@@ -301,7 +327,7 @@
         body,
         out_shape=tuple(jax.ShapeDtypeStruct(shape, dtype) for shape, dtype in outs),
         scratch_shapes=list(scratch),
-        compiler_params=pltpu.CompilerParams(vmem_limit_bytes=48 * 1024 * 1024),
+        compiler_params=pltpu.CompilerParams(vmem_limit_bytes=20 * 1024 * 1024),
         cost_estimate=pl.CostEstimate(flops=flops, bytes_accessed=4 * 1024 * 1024, transcendentals=0),
         name=name,
     )
@@ -386,61 +412,78 @@
     return jnp.concatenate([first, second], axis=0).astype(F32)
 
 
+def after(value, token):
+    return lax.optimization_barrier((value, token))[0]
+
+
 def on_device(scans, proj_weight, value_weight, out_weight, flags, cotangent):
     own = scans[0]
     cot = cotangent[0]
     weights = (proj_weight, value_weight, out_weight)
     wide = (ROW, D)
+    columns = ((8, ROW, 128), F32)
     unit = 2 * ROW * ROW * D
 
+    low_y = shift(own[:, 4:], 1, 0, 1)
+    high_y = shift(own[:, :4], 1, 0, -1)
     zl, zm, zh = slabs(own)
-    lo = shift(jnp.stack([zl[:, 4:], zm[:, 4:], zh[:, 4:]]), 0, 0, 1)
-    hi = shift(jnp.stack([zl[:, :4], zm[:, :4], zh[:, :4]]), 0, 0, -1)
     query_a, query_b, key_a, key_b = window_biases(flags)
     xs, cs, p0, v0, g0 = call(own_kernel, [((2,) + wide, BF16)] * 5, flops=10 * unit, name="own")(
         own, cot, *weights
     )
-    pm, vm, a1, ml = call(
+    mid_y = jnp.stack([low_y, high_y])
+    low_zy = shift(mid_y, 0, 1, 0)
+    high_zy = shift(mid_y, 0, -1, 0)
+    pm, vm, a1, top, total = call(
         mid_kernel,
-        [((6,) + wide, BF16)] * 2 + [((8, CUBE, D), F32), ((8, ROW, 128), F32)],
+        [((6,) + wide, BF16)] * 2 + [((8, CUBE, D), F32), columns, columns],
         [pltpu.VMEM((2, ROW, 1536), F32), pltpu.VMEM((2, ROW, 1536), BF16)],
         flops=300 * unit,
         name="mid",
     )(zl, zm, zh, proj_weight, value_weight, p0, query_a, query_b)
-    czl, czm, czh = slabs(cot)
-    clo = shift(jnp.stack([czl[:, 4:], czm[:, 4:], czh[:, 4:]]), 0, 0, 1)
-    chi = shift(jnp.stack([czl[:, :4], czm[:, :4], czh[:, :4]]), 0, 0, -1)
-    pe, ve, stat_cols, stat_rows, mixed, gout = call(
+    cot_y = after(cot, mid_y)
+    cot_y = (shift(cot_y[:, 4:], 0, 0, 1), shift(cot_y[:, :4], 0, 0, -1))
+    cot_y = jnp.concatenate([cot_y[0], cot, cot_y[1]], axis=1)
+    czl, czm, czh = slabs(after(cot_y, total))
+    pe, ve, lse, delta, first, second, mixed, gout = call(
         edge_kernel,
         [((2, 3) + wide, BF16)] * 2
-        + [((8, ROW, 128), F32), ((8, 2, ROW), F32), (own.shape, BF16), (wide, F32)],
+        + [columns, columns, ((8, ROW), F32), ((8, ROW), F32), (own.shape, BF16), (wide, F32)],
         [
             pltpu.VMEM((2, ROW, 768), F32),
             pltpu.VMEM((2, ROW, 768), BF16),
             pltpu.VMEM((2,) + wide, BF16),
+            pltpu.VMEM((8, 8, 128), F32),
         ],
         flops=200 * unit,
         name="edge",
-    )(lo, hi, *weights, p0, g0, cs, query_a, query_b, a1, ml)
-    stat_rows = stat_rows.reshape(2, 4, 2, HEADS, CUBE).transpose(0, 2, 3, 1, 4).reshape(2, 8, ROW)
-    szl, szm, szh = slabs(stat_rows)
-    slo = shift(jnp.stack([szl[1], szm[1], szh[1]]), 0, 0, 1)
-    shi = shift(jnp.stack([szl[0], szm[0], szh[0]]), 0, 0, -1)
-    smid = jnp.concatenate([szl, szm, szh])
-    sedge = jnp.stack([slo, shi])
-    (qg,) = call(
-        query_kernel,
-        [((8, CUBE, D), F32)],
-        [pltpu.VMEM((2, ROW, 2304), BF16)],
-        flops=400 * unit,
-        name="query",
-    )(p0, g0, pm, vm, pe, ve, stat_cols, query_a, query_b)
+    )(mid_y, low_zy, high_zy, *weights, after(p0, cot_y), g0, cs, query_a, query_b, a1, top, total)
+    stat_low = shift(second, 0, 0, 1)
+    stat_high = shift(first, 0, 0, -1)
+
+    def query(y, p):
+        (out,) = call(
+            functools.partial(query_kernel, y),
+            [((4, CUBE, D), F32)],
+            [pltpu.VMEM((2, ROW, 2304), BF16)],
+            flops=200 * unit,
+            name="query",
+        )(p, g0, pm, vm, pe, ve, lse, delta, query_a, query_b)
+        return out
+
+    qg0 = query(0, after(p0, (czl, czm, czh)))
+    stat_low = after(stat_low, qg0)
+    stat_y = jnp.stack([stat_low, first, second, stat_high])
+    szl, szm, szh = slabs(stat_y)
+    qg1 = query(1, after(p0, stat_y))
     grad, part = call(
         key_kernel,
         [(own.shape, BF16), ((ROW, 3 * D), BF16)],
         [
             pltpu.VMEM((6,) + wide, BF16),
             pltpu.VMEM((2, 3) + wide, BF16),
+            pltpu.VMEM((6, 8, ROW), F32),
+            pltpu.VMEM((2, 3, 8, ROW), F32),
             pltpu.VMEM((2, ROW, 2304), BF16),
             pltpu.VMEM((2, ROW, 2304), BF16),
             pltpu.VMEM((2,) + wide, BF16),
@@ -448,7 +491,7 @@
         ],
         flops=500 * unit,
         name="key",
-    )(czl, czm, czh, clo, chi, *weights, p0, v0, xs, pm, pe, smid, sedge, key_a, key_b, qg, gout)
+    )(czl, czm, czh, szl, szm, szh, *weights, p0, v0, xs, pm, pe, key_a, key_b, qg0, qg1, gout)
     summed = total_of(part)
     return (
         mixed[None],

time: 171 us -> 154 us (0.901)
  local copies, waits for them, and re-layouts: 19.3 us -> 6.34 us
  waiting for transfers between devices: 11.4 us -> 6.13 us
  starting transfers between devices: 44.2 us -> 48.8 us
  other arithmetic: 5.81 us -> 3.51 us
  Pallas kernels: 39.4 us -> 37.2 us
    unnamed x51 -> x21, local copies, waits for them, and re-layouts: 14.2 us -> 1.3 us
    ppermute x17 -> x19, waiting for transfers between devices: 11.4 us -> 6.13 us  [shift(): return lax.ppermute(block, AXES, route)]
    ppermute x17 -> x19, starting transfers between devices: 44.2 us -> 48.8 us  [shift(): return lax.ppermute(block, AXES, route)]
    pallas_call x3 -> x4, Pallas kernels: 27.5 us -> 25.3 us  [the longest x2 9.4 us: query(): call(functools.partial(query_kernel, y), [((4, CUBE, D), F32)], [pltpu.VM...]
    all_to_all x1, blocking collectives: 30.5 us -> 32.3 us  [total_of(): lax.all_to_all(mine.reshape(places, -1), ('gz', 'gy'), 0, 0, tiled=True)]
  transfers between devices with their start and end apart: 17 -> 19, of which waited for: 5 -> 6; matrix products, arithmetic and copies ran while one was open for 4% -> 3% of each run, Pallas kernels for 17% -> 17%
where the time goes in v2:
time: 154 us
  blocking collectives  50.6 us (33%)
  starting transfers between devices  48.8 us (32%)
  Pallas kernels  37.2 us (24%)
  local copies, waits for them, and re-layouts  6.34 us (4%)
  waiting for transfers between devices  6.13 us (4%)
  other arithmetic  3.51 us (2%)
    ppermute x19, starting transfers between devices, shift(): return lax.ppermute(block, AXES, route)  48.8 us
    all_to_all x1, blocking collectives, total_of(): lax.all_to_all(mine.reshape(places, -1), ('gz', 'gy'), 0, 0, tiled=True)  32.3 us
    all_to_all x1, blocking collectives, total_of(): lax.all_to_all(jnp.broadcast_to(total[None], got.shape), ('gz', 'gy'), 0,...  18.2 us
    pallas_call x1, Pallas kernels, on_device(): call(key_kernel, [(own.shape, BF16), ((ROW, 3 * D), BF16)], [pltpu.VMEM((...  11.3 us
    pallas_call x2, Pallas kernels, query(): call(functools.partial(query_kernel, y), [((4, CUBE, D), F32)], [pltpu.VM...  9.4 us
    pallas_call x1, Pallas kernels, on_device(): call(mid_kernel, [((6,) + wide, BF16)] * 2 + [((8, CUBE, D), F32), column...  8.26 us
    pallas_call x1, Pallas kernels, on_device(): call(edge_kernel, [((2, 3) + wide, BF16)] * 2 + [columns, columns, ((8, R...  7.61 us
    ppermute x19, waiting for transfers between devices, shift(): return lax.ppermute(block, AXES, route)  6.13 us
  transfers between devices with their start and end apart: 19, of which 6 were waited for; matrix products, arithmetic and copies ran while one was open for 3% of the time, Pallas kernels for 17%

profile of v2, /device:TPU:1, one launch (start us, length us, event | category | flops | bytes accessed | tf_op | source)
XLA Modules:
  0.0 153.7 jit_solution(10430796691107373549)
XLA Ops:
  0.6 4.9 %collective-permute-start.6 = (bf16[4,8,16,256]{3,2,1,0:T(8,128)(2,1)}, bf16[4,8,16,256]{3,2,1,0:T(8,128)(2,1)S(1)}, u32[]{:S(2)}, u32[]{:S(2)}) collective-permute-start(bf16[4,8,16,256]{3,2,1,0:T(8,128)(2,1)} %bitcast.36), channel_id=1, source_target_pairs={{0,136},{1,137},{2,138},{3,139},{4,140},{5,141},{6,142},{7,143},{8... | collective-permute-start | bytes 786440 | tf_op jit(solution)/shard_map/ppermute | solution.py:350
  5.7 1.3 collective-permute-start.8
  8.0 1.4 collective-permute-start.1
  9.4 5.8 %collective-permute-start = (bf16[4,4,16,256]{3,2,1,0:T(8,128)(2,1)S(1)}, bf16[4,4,16,256]{3,2,1,0:T(8,128)(2,1)S(1)}, u32[]{:S(2)}, u32[]{:S(2)}) collective-permute-start(bf16[4,4,16,256]{3,2,1,0:T(8,128)(2,1)S(1)} %get-tuple-element.64), channel_id=1, source_target_pairs={{0,129},{1,130},{2,131},{3,132},{4,133},{5,134},{6,135},{8,137},{9... | collective-permute-start | bytes 393224 | tf_op jit(solution)/shard_map/ppermute | solution.py:350
  19.7 1.7 %collective-permute-done.1 = bf16[4,4,16,256]{3,2,1,0:T(8,128)(2,1)S(1)} collective-permute-done((bf16[4,4,16,256]{3,2,1,0:T(8,128)(2,1)S(1)}, bf16[4,4,16,256]{3,2,1,0:T(8,128)(2,1)S(1)}, u32[]{:S(2)}, u32[]{:S(2)}) %collective-permute-start.1) | collective-permute-done | bytes 131104 | tf_op jit(solution)/shard_map/ppermute | solution.py:350
  21.5 3.0 %collective-permute-start.2 = (bf16[2,4,4,16,256]{4,3,2,1,0:T(8,128)(2,1)S(1)}, bf16[2,4,4,16,256]{4,3,2,1,0:T(8,128)(2,1)S(1)}, u32[]{:S(2)}, u32[]{:S(2)}) collective-permute-start(bf16[2,4,4,16,256]{4,3,2,1,0:T(8,128)(2,1)S(1)} %pad_maximum_fusion.1.mid_y), channel_id=1, source_target_pairs={{0,8},{1,9},{2,10},{3,11},{4,12},{5,13},{6,14},{7,15},{8,16},{9,17... | collective-permute-start | bytes 786440 | tf_op jit(solution)/shard_map/ppermute | solution.py:350
  24.5 1.3 collective-permute-start.3
  25.8 1.3 collective-permute-start.5
  27.2 6.2 %collective-permute-start.4 = (bf16[4,4,16,256]{3,2,1,0:T(8,128)(2,1)S(1)}, bf16[4,4,16,256]{3,2,1,0:T(8,128)(2,1)S(1)}, u32[]{:S(2)}, u32[]{:S(2)}) collective-permute-start(bf16[4,4,16,256]{3,2,1,0:T(8,128)(2,1)S(1)} %get-tuple-element.62), channel_id=1, source_target_pairs={{0,1},{1,2},{2,3},{3,4},{4,5},{5,6},{6,7},{8,9},{9,10},{10,11},{11... | collective-permute-start | bytes 393224 | tf_op jit(solution)/shard_map/ppermute | solution.py:350
  33.4 8.3 %mid.1 = (bf16[6,256,256]{2,1,0:T(8,128)(2,1)S(1)}, bf16[6,256,256]{2,1,0:T(8,128)(2,1)S(1)}, f32[8,64,256]{2,1,0:T(8,128)S(1)}, f32[8,256,128]{2,1,0:T(8,128)S(1)}, f32[8,256,128]{2,1,0:T(8,128)S(1)}) custom-call(bf16[4,8,16,256]{3,2,1,0:T(8,128)(2,1)S(1)} %collective-permute-done.6.zl, bf16[4,8,16,256]{3,2,1,0:T(8,128)(2,1)S(1)} %collective-permute-done.7.zm, ...), custom_call_target="tpu_custom_call" | custom-call | flops 10066329600 | bytes 4194304 | tf_op jit(solution)/shard_map/mid/pallas_call | solution.py:437
  41.8 5.1 %collective-permute-start.9 = (bf16[4,16,16,256]{3,2,1,0:T(8,128)(2,1)S(1)}, bf16[4,16,16,256]{3,2,1,0:T(8,128)(2,1)S(1)}, u32[]{:S(2)}, u32[]{:S(2)}) collective-permute-start(bf16[4,16,16,256]{3,2,1,0:T(8,128)(2,1)S(1)} %pad_maximum_fusion), channel_id=1, source_target_pairs={{0,136},{1,137},{2,138},{3,139},{4,140},{5,141},{6,142},{7,143},{8... | collective-permute-start | bytes 1572872 | tf_op jit(solution)/shard_map/ppermute | solution.py:350
  47.0 1.3 collective-permute-start.11
  48.3 7.6 %edge.1 = (bf16[2,3,256,256]{3,2,1,0:T(8,128)(2,1)S(1)}, bf16[2,3,256,256]{3,2,1,0:T(8,128)(2,1)S(1)}, f32[8,256,128]{2,1,0:T(8,128)S(1)}, f32[8,256,128]{2,1,0:...) custom-call(bf16[2,4,4,16,256]{4,3,2,1,0:T(8,128)(2,1)S(1)} %pad_max, ...), custom_call_target="tpu_custom_call" | custom-call | flops 6710886400 | bytes 4194304 | tf_op jit(solution)/shard_map/edge/pallas_call | solution.py:448
  57.2 6.7 %collective-permute-start.12 = (f32[8,256]{1,0:T(8,128)S(1)}, f32[8,256]{1,0:T(8,128)S(1)}, u32[]{:S(2)}, u32[]{:S(2)}) collective-permute-start(f32[8,256]{1,0:T(8,128)S(1)} %get-tuple-element.41), channel_id=1, source_target_pairs={{0,1},{1,2},{2,3},{3,4},{4,5},{5,6},{6,7},{8,9},{9,10},{10,11},{11... | collective-permute-start | bytes 24584 | tf_op jit(solution)/shard_map/ppermute | solution.py:350
  64.1 4.7 %query.2.qg0 = f32[4,64,256]{2,1,0:T(8,128)S(1)} custom-call(bf16[2,256,256]{2,1,0:T(8,128)(2,1)S(1)} %get-tuple-element.53.p0, bf16[2,256,256]{2,1,0:T(8,128)(2,1)S(1)} %get-tuple-element.34.g0, bf16[6,256,256]{2,1,0:T(8,128)(2,1)S(1)} %get-tuple-element.43.pm, bf16[6,256,256]{2,1,0:T(8,128)(2,1)S(1)} %get-tuple-element.44.vm, ...), custom_call_target="tpu_custom_call" | custom-call | flops 6710886400 | bytes 4194304 | tf_op jit(solution)/shard_map/query/pallas_call | solution.py:465
  68.8 1.6 %collective-permute-done.13 = f32[8,256]{1,0:T(8,128)S(1)} collective-permute-done((f32[8,256]{1,0:T(8,128)S(1)}, f32[8,256]{1,0:T(8,128)S(1)}, u32[]{:S(2)}, u32[]{:S(2)}) %collective-permute-start.13) | collective-permute-done | bytes 8224 | tf_op jit(solution)/shard_map/ppermute | solution.py:350
  70.4 4.1 %collective-permute-start.14 = (f32[4,8,256]{2,1,0:T(8,128)S(1)}, f32[4,8,256]{2,1,0:T(8,128)S(1)}, u32[]{:S(2)}, u32[]{:S(2)}) collective-permute-start(f32[4,8,256]{2,1,0:T(8,128)S(1)} %pad_maximum_fusion.2), channel_id=1, source_target_pairs={{0,136},{1,137},{2,138},{3,139},{4,140},{5,141},{6,142},{7,143},{8... | collective-permute-start | bytes 98312 | tf_op jit(solution)/shard_map/ppermute | solution.py:350
  74.7 1.5 collective-permute-start.16
  76.1 4.7 %query.3.qg1 = f32[4,64,256]{2,1,0:T(8,128)S(1)} custom-call(bf16[2,256,256]{2,1,0:T(8,128)(2,1)S(1)} %get-tuple-element.53.p0, bf16[2,256,256]{2,1,0:T(8,128)(2,1)S(1)} %get-tuple-element.34.g0, bf16[6,256,256]{2,1,0:T(8,128)(2,1)S(1)} %get-tuple-element.43.pm, bf16[6,256,256]{2,1,0:T(8,128)(2,1)S(1)} %get-tuple-element.44.vm, ...), custom_call_target="tpu_custom_call" | custom-call | flops 6710886400 | bytes 4194304 | tf_op jit(solution)/shard_map/query/pallas_call | solution.py:465
  81.2 11.3 %key.1 = (bf16[4,8,16,256]{3,2,1,0:T(8,128)(2,1)}, bf16[256,768]{1,0:T(8,128)(2,1)S(1)}) custom-call(bf16[4,16,16,256]{3,2,1,0:T(8,128)(2,1)S(1)} %collective-permute-done.9.zl, bf16[4,16,16,256]{3,2,1,0:T(8,128)(2,1)S(1)} %collective-permute-done.10.zm, bf16[4,16,16,256]{3,2,1,0:T(8,128)(2,1)S(1)} %collective-permute-done.11.zh, ...), custom_call_target="tpu_custom_call" | custom-call | flops 16777216000 | bytes 4194304 | tf_op jit(solution)/shard_map/key/pallas_call | solution.py:479
  95.3 32.3 %all_to_all.18 = bf16[128,2,384]{2,1,0:T(2,128)(2,1)S(1)} all-to-all(bf16[128,2,384]{2,1,0:T(2,128)(2,1)S(1)} %reshape.113), channel_id=1, replica_groups=mesh['scan'=2,'gz'=16,'gy'=8] {'gz','gy'}, dimensions={0} | all-to-all | bytes 393216 | tf_op jit(solution)/shard_map/all_to_all | solution.py:402
  128.5 1.8 %reduce.3 = bf16[128,768]{1,0:T(8,128)(2,1)S(1)} reduce(bf16[128,1,768]{2,1,0:T(2,128)(2,1)S(1)} %broadcast_in_dim.60, bf16[]{:T(256)} %broadcast.46), dimensions={1}, to_apply=%broadcast_in_dim.60.reduce_sub_computation | reduce | bytes 393218 | tf_op jit(solution)/shard_map/broadcast_in_dim | solution.py:407
  130.3 18.2 %all_to_all.19 = bf16[128,2,384]{2,1,0:T(2,128)(2,1)S(1)} all-to-all(bf16[128,2,384]{2,1,0:T(2,128)(2,1)S(1)} %reshape.115), channel_id=1, replica_groups=mesh['scan'=2,'gz'=16,'gy'=8] {'gz','gy'}, dimensions={0} | all-to-all | bytes 393216 | tf_op jit(solution)/shard_map/all_to_all | solution.py:406
  148.7 2.9 %collective-permute-start.18 = (bf16[128,768]{1,0:T(8,128)(2,1)S(1)}, bf16[128,768]{1,0:T(8,128)(2,1)S(1)}, u32[]{:S(2)}, u32[]{:S(2)}) collective-permute-start(bf16[128,768]{1,0:T(8,128)(2,1)S(1)} %bitcast.43), channel_id=1, source_target_pairs={{0,128},{1,129},{2,130},{3,131},{4,132},{5,133},{6,134},{7,135},{8... | collective-permute-start | bytes 589832 | tf_op jit(solution)/shard_map/ppermute | solution.py:350
  (100 shorter events, 13.3 us)
Async XLA Ops:
  0.6 25.2 %collective-permute-start.6 = (bf16[4,8,16,256]{3,2,1,0:T(8,128)(2,1)}, bf16[4,8,16,256]{3,2,1,0:T(8,128)(2,1)S(1)}, u32[]{:S(2)}, u32[]{:S(2)}) collective-permute-start(bf16[4,8,16,256]{3,2,1,0:T(8,128)(2,1)} %bitcast.36), channel_id=1, source_target_pairs={{0,136},{1,137},{2,138},{3,139},{4,140},{5,141},{6,142},{7,143},{8... | collective-permute-start | bytes 786440 | tf_op jit(solution)/shard_map/ppermute | solution.py:350
  5.6 21.6 %collective-permute-start.7 = (bf16[4,8,16,256]{3,2,1,0:T(8,128)(2,1)}, bf16[4,8,16,256]{3,2,1,0:T(8,128)(2,1)S(1)}, u32[]{:S(2)}, u32[]{:S(2)}) collective-permute-start(bf16[4,8,16,256]{3,2,1,0:T(8,128)(2,1)} %bitcast.37), channel_id=1, source_target_pairs={{0,128},{1,129},{2,130},{3,131},{4,132},{5,133},{6,134},{7,135},{8... | collective-permute-start | bytes 786440 | tf_op jit(solution)/shard_map/ppermute | solution.py:350
  5.7 27.7 %collective-permute-start.8 = (bf16[4,8,16,256]{3,2,1,0:T(8,128)(2,1)}, bf16[4,8,16,256]{3,2,1,0:T(8,128)(2,1)S(1)}, u32[]{:S(2)}, u32[]{:S(2)}) collective-permute-start(bf16[4,8,16,256]{3,2,1,0:T(8,128)(2,1)} %bitcast.38), channel_id=1, source_target_pairs={{8,128},{9,129},{10,130},{11,131},{12,132},{13,133},{14,134},{15,1... | collective-permute-start | bytes 786440 | tf_op jit(solution)/shard_map/ppermute | solution.py:350
  8.0 7.4 %copy-start.5 = (s32[2,16,16,4]{2,3,1,0:T(4,128)S(1)}, s32[2,16,16,4]{2,3,1,0:T(4,128)}, u32[]{:S(2)}) copy-start(s32[2,16,16,4]{2,3,1,0:T(4,128)} %param.12) | copy-start | bytes 24580
  8.0 13.4 %collective-permute-start.1 = (bf16[4,4,16,256]{3,2,1,0:T(8,128)(2,1)S(1)}, bf16[4,4,16,256]{3,2,1,0:T(8,128)(2,1)S(1)}, u32[]{:S(2)}, u32[]{:S(2)}) collective-permute-start(bf16[4,4,16,256]{3,2,1,0:T(8,128)(2,1)S(1)} %get-tuple-element.65), channel_id=1, source_target_pairs={{1,128},{2,129},{3,130},{4,131},{5,132},{6,133},{7,134},{9,136},{1... | collective-permute-start | bytes 393224 | tf_op jit(solution)/shard_map/ppermute | solution.py:350
  9.4 12.0 %collective-permute-start = (bf16[4,4,16,256]{3,2,1,0:T(8,128)(2,1)S(1)}, bf16[4,4,16,256]{3,2,1,0:T(8,128)(2,1)S(1)}, u32[]{:S(2)}, u32[]{:S(2)}) collective-permute-start(bf16[4,4,16,256]{3,2,1,0:T(8,128)(2,1)S(1)} %get-tuple-element.64), channel_id=1, source_target_pairs={{0,129},{1,130},{2,131},{3,132},{4,133},{5,134},{6,135},{8,137},{9... | collective-permute-start | bytes 393224 | tf_op jit(solution)/shard_map/ppermute | solution.py:350
  17.4 1.5 copy-start.4
  17.5 1.3 copy-start.3
  17.8 1.0 copy-start.2
  18.0 1.0 copy-start
  21.5 26.9 %collective-permute-start.2 = (bf16[2,4,4,16,256]{4,3,2,1,0:T(8,128)(2,1)S(1)}, bf16[2,4,4,16,256]{4,3,2,1,0:T(8,128)(2,1)S(1)}, u32[]{:S(2)}, u32[]{:S(2)}) collective-permute-start(bf16[2,4,4,16,256]{4,3,2,1,0:T(8,128)(2,1)S(1)} %pad_maximum_fusion.1.mid_y), channel_id=1, source_target_pairs={{0,8},{1,9},{2,10},{3,11},{4,12},{5,13},{6,14},{7,15},{8,16},{9,17... | collective-permute-start | bytes 786440 | tf_op jit(solution)/shard_map/ppermute | solution.py:350
  24.5 23.8 %collective-permute-start.3 = (bf16[2,4,4,16,256]{4,3,2,1,0:T(8,128)(2,1)S(1)}, bf16[2,4,4,16,256]{4,3,2,1,0:T(8,128)(2,1)S(1)}, u32[]{:S(2)}, u32[]{:S(2)}) collective-permute-start(bf16[2,4,4,16,256]{4,3,2,1,0:T(8,128)(2,1)S(1)} %pad_maximum_fusion.1.mid_y), channel_id=1, source_target_pairs={{8,0},{9,1},{10,2},{11,3},{12,4},{13,5},{14,6},{15,7},{16,8},{17,9... | collective-permute-start | bytes 786440 | tf_op jit(solution)/shard_map/ppermute | solution.py:350
  25.8 15.8 %collective-permute-start.5 = (bf16[4,4,16,256]{3,2,1,0:T(8,128)(2,1)S(1)}, bf16[4,4,16,256]{3,2,1,0:T(8,128)(2,1)S(1)}, u32[]{:S(2)}, u32[]{:S(2)}) collective-permute-start(bf16[4,4,16,256]{3,2,1,0:T(8,128)(2,1)S(1)} %get-tuple-element.63), channel_id=1, source_target_pairs={{1,0},{2,1},{3,2},{4,3},{5,4},{6,5},{7,6},{9,8},{10,9},{11,10},{12... | collective-permute-start | bytes 393224 | tf_op jit(solution)/shard_map/ppermute | solution.py:350
  27.2 14.5 %collective-permute-start.4 = (bf16[4,4,16,256]{3,2,1,0:T(8,128)(2,1)S(1)}, bf16[4,4,16,256]{3,2,1,0:T(8,128)(2,1)S(1)}, u32[]{:S(2)}, u32[]{:S(2)}) collective-permute-start(bf16[4,4,16,256]{3,2,1,0:T(8,128)(2,1)S(1)} %get-tuple-element.62), channel_id=1, source_target_pairs={{0,1},{1,2},{2,3},{3,4},{4,5},{5,6},{6,7},{8,9},{9,10},{10,11},{11... | collective-permute-start | bytes 393224 | tf_op jit(solution)/shard_map/ppermute | solution.py:350
  41.8 22.1 %collective-permute-start.9 = (bf16[4,16,16,256]{3,2,1,0:T(8,128)(2,1)S(1)}, bf16[4,16,16,256]{3,2,1,0:T(8,128)(2,1)S(1)}, u32[]{:S(2)}, u32[]{:S(2)}) collective-permute-start(bf16[4,16,16,256]{3,2,1,0:T(8,128)(2,1)S(1)} %pad_maximum_fusion), channel_id=1, source_target_pairs={{0,136},{1,137},{2,138},{3,139},{4,140},{5,141},{6,142},{7,143},{8... | collective-permute-start | bytes 1572872 | tf_op jit(solution)/shard_map/ppermute | solution.py:350
  46.9 17.0 %collective-permute-start.10 = (bf16[4,16,16,256]{3,2,1,0:T(8,128)(2,1)S(1)}, bf16[4,16,16,256]{3,2,1,0:T(8,128)(2,1)S(1)}, u32[]{:S(2)}, u32[]{:S(2)}) collective-permute-start(bf16[4,16,16,256]{3,2,1,0:T(8,128)(2,1)S(1)} %pad_maximum_fusion), channel_id=1, source_target_pairs={{0,128},{1,129},{2,130},{3,131},{4,132},{5,133},{6,134},{7,135},{8... | collective-permute-start | bytes 1572872 | tf_op jit(solution)/shard_map/ppermute | solution.py:350
  47.0 17.1 %collective-permute-start.11 = (bf16[4,16,16,256]{3,2,1,0:T(8,128)(2,1)S(1)}, bf16[4,16,16,256]{3,2,1,0:T(8,128)(2,1)S(1)}, u32[]{:S(2)}, u32[]{:S(2)}) collective-permute-start(bf16[4,16,16,256]{3,2,1,0:T(8,128)(2,1)S(1)} %pad_maximum_fusion), channel_id=1, source_target_pairs={{8,128},{9,129},{10,130},{11,131},{12,132},{13,133},{14,134},{15,1... | collective-permute-start | bytes 1572872 | tf_op jit(solution)/shard_map/ppermute | solution.py:350
  55.9 14.5 %collective-permute-start.13 = (f32[8,256]{1,0:T(8,128)S(1)}, f32[8,256]{1,0:T(8,128)S(1)}, u32[]{:S(2)}, u32[]{:S(2)}) collective-permute-start(f32[8,256]{1,0:T(8,128)S(1)} %get-tuple-element.50), channel_id=1, source_target_pairs={{1,0},{2,1},{3,2},{4,3},{5,4},{6,5},{7,6},{9,8},{10,9},{11,10},{12... | collective-permute-start | bytes 24584 | tf_op jit(solution)/shard_map/ppermute | solution.py:350
  57.2 11.6 %collective-permute-start.12 = (f32[8,256]{1,0:T(8,128)S(1)}, f32[8,256]{1,0:T(8,128)S(1)}, u32[]{:S(2)}, u32[]{:S(2)}) collective-permute-start(f32[8,256]{1,0:T(8,128)S(1)} %get-tuple-element.41), channel_id=1, source_target_pairs={{0,1},{1,2},{2,3},{3,4},{4,5},{5,6},{6,7},{8,9},{9,10},{10,11},{11... | collective-permute-start | bytes 24584 | tf_op jit(solution)/shard_map/ppermute | solution.py:350
  70.4 10.4 %collective-permute-start.14 = (f32[4,8,256]{2,1,0:T(8,128)S(1)}, f32[4,8,256]{2,1,0:T(8,128)S(1)}, u32[]{:S(2)}, u32[]{:S(2)}) collective-permute-start(f32[4,8,256]{2,1,0:T(8,128)S(1)} %pad_maximum_fusion.2), channel_id=1, source_target_pairs={{0,136},{1,137},{2,138},{3,139},{4,140},{5,141},{6,142},{7,143},{8... | collective-permute-start | bytes 98312 | tf_op jit(solution)/shard_map/ppermute | solution.py:350
  74.6 6.3 %collective-permute-start.15 = (f32[4,8,256]{2,1,0:T(8,128)S(1)}, f32[4,8,256]{2,1,0:T(8,128)S(1)}, u32[]{:S(2)}, u32[]{:S(2)}) collective-permute-start(f32[4,8,256]{2,1,0:T(8,128)S(1)} %pad_maximum_fusion.2), channel_id=1, source_target_pairs={{0,128},{1,129},{2,130},{3,131},{4,132},{5,133},{6,134},{7,135},{8... | collective-permute-start | bytes 98312 | tf_op jit(solution)/shard_map/ppermute | solution.py:350
  74.7 6.5 %collective-permute-start.16 = (f32[4,8,256]{2,1,0:T(8,128)S(1)}, f32[4,8,256]{2,1,0:T(8,128)S(1)}, u32[]{:S(2)}, u32[]{:S(2)}) collective-permute-start(f32[4,8,256]{2,1,0:T(8,128)S(1)} %pad_maximum_fusion.2), channel_id=1, source_target_pairs={{8,128},{9,129},{10,130},{11,131},{12,132},{13,133},{14,134},{15,1... | collective-permute-start | bytes 98312 | tf_op jit(solution)/shard_map/ppermute | solution.py:350
  92.5 1.5 collective-permute-start.17
  148.7 4.0 %collective-permute-start.18 = (bf16[128,768]{1,0:T(8,128)(2,1)S(1)}, bf16[128,768]{1,0:T(8,128)(2,1)S(1)}, u32[]{:S(2)}, u32[]{:S(2)}) collective-permute-start(bf16[128,768]{1,0:T(8,128)(2,1)S(1)} %bitcast.43), channel_id=1, source_target_pairs={{0,128},{1,129},{2,130},{3,131},{4,132},{5,133},{6,134},{7,135},{8... | collective-permute-start | bytes 589832 | tf_op jit(solution)/shard_map/ppermute | solution.py:350
  (3 other events, 2.4 us)

commit v3 on v2

v3 whole, which is shorter than its diff:
```python
import functools

import jax
import jax.numpy as jnp
import numpy as np
from jax import lax
from jax.experimental import pallas as pl
from jax.experimental.pallas import tpu as pltpu
from jax.sharding import PartitionSpec as P

D = 256
HEADS = 4
HEAD_DIM = 64
BLK = 4
CUBE = 64
ROW = 256
NEG = -1e30
AXES = ("scan", "gz", "gy")
F32 = jnp.float32
BF16 = jnp.bfloat16
NN = (((1,), (0,)), ((), ()))
NT = (((1,), (1,)), ((), ()))
TN = (((0,), (0,)), ((), ()))


def dot(a, b, dims=NN):
    return lax.dot_general(a, b, dims, preferred_element_type=F32)


def natural_of(t):
    return ((t >> 4) & 3) * 64 + ((t >> 2) & 3) * 16 + (t >> 6) * 4 + (t & 3)


def iota2(shape, axis):
    return lax.broadcasted_iota(jnp.int32, shape, axis)


def to_blocks_matrix():
    shape = (ROW, ROW)
    return (natural_of(iota2(shape, 0)) == iota2(shape, 1)).astype(F32).astype(BF16)


def from_blocks_matrix():
    shape = (ROW, ROW)
    return (natural_of(iota2(shape, 1)) == iota2(shape, 0)).astype(F32).astype(BF16)


def head_mask():
    shape = (ROW, D)
    return (iota2(shape, 0) // HEAD_DIM == iota2(shape, 1) // HEAD_DIM).astype(F32)


def spread(block, mask, scale=1.0):
    wide = jnp.concatenate([block.astype(F32)] * HEADS, axis=0)
    return wide * (mask * scale)


def collect(wide, mask):
    kept = wide * mask
    return (kept[0:64] + kept[64:128]) + (kept[128:192] + kept[192:256])


def chunks(rows, width):
    if width == ROW:
        return [(j, 1) for j in range(rows)]
    return [(j, min(2, rows - j)) for j in range(0, rows, 2)]


def take(ref, lead, j, count, start, width):
    return ref[(*lead, pl.ds(j, count), pl.ds(start, width))].reshape(count * width, D)


def span(x):
    return {0: (0, 128), 1: (0, 256), 2: (0, 256), 3: (128, 128)}[x]


def own_rows(ref, y, x):
    return ref[y, CUBE * x : CUBE * x + CUBE, :]


def bias_of(bias_a, bias_b, y, x, cols):
    return bias_b[2 * y + x - 1, :, cols] if x in (1, 2) else bias_a[2 * y + x // 3, :, cols]


def store(ref, lead, rows, j, count, x, value):
    start, width = span(x)
    for n in range(count):
        at = (j + n) * ROW + start
        ref[(*lead, rows, slice(at, at + width))] = value[:, n * width : n * width + width]


def lane_max(s):
    out = s[:, 0:128]
    for k in range(128, s.shape[1], 128):
        out = jnp.maximum(out, s[:, k : k + 128])
    return out


def lane_sum(s):
    out = s[:, 0:128]
    for k in range(128, s.shape[1], 128):
        out = out + s[:, k : k + 128]
    return out


def lanes(column, width):
    return column if width == 128 else jnp.concatenate([column] * (width // 128), axis=1)


def filled(column):
    return jnp.broadcast_to(column, (ROW, 128))


def turned(column):
    keep = iota2((CUBE, 128), 0) == (iota2((CUBE, 128), 1) & 63)
    rows = [
        jnp.sum(jnp.where(keep, column[64 * h : 64 * h + 64], 0.0), axis=0, keepdims=True)
        for h in range(HEADS)
    ]
    return jnp.concatenate(rows, axis=0)


def own_kernel(scans, cot, wp, wo, xs, cs, p0, g0):
    shuffle = to_blocks_matrix()
    for y in range(2):
        x = dot(shuffle, scans[:, 4 * y : 4 * y + 4].reshape(ROW, D)).astype(BF16)
        c = dot(shuffle, cot[:, 4 * y : 4 * y + 4].reshape(ROW, D)).astype(BF16)
        xs[y] = x
        cs[y] = c
        p0[y] = dot(x, wp[...]).astype(BF16)
        g0[y] = dot(c, wo[...], NT).astype(BF16)


def mid_kernel(
    zl, zm, zh, wp, wv, p0, bias_a, bias_b, xm, pm, vm, em, a1, top_out, sum_out, s_scr,
):
    shuffle = to_blocks_matrix()
    mask = head_mask()
    for z, slab in enumerate((zl, zm, zh)):
        for y in range(2):
            x = dot(shuffle, slab[:, 4 * y : 4 * y + 4].reshape(ROW, D)).astype(BF16)
            xm[2 * z + y] = x
            pm[2 * z + y] = dot(x, wp[...]).astype(BF16)
            vm[2 * z + y] = dot(x, wv[...]).astype(BF16)

    def step(y, carry):
        for x in range(4):
            start, width = span(x)
            rows = slice(ROW * x, ROW * x + ROW)
            q = spread(own_rows(p0, y, x), mask, 0.125).astype(BF16)
            top = None
            for j, count in chunks(6, width):
                cols = slice(j * width, (j + count) * width)
                s = dot(q, take(pm, (), j, count, start, width), NT)
                s = s + bias_of(bias_a, bias_b, y, x, cols)
                s_scr[x, :, cols] = s
                part = lane_max(s)
                top = part if top is None else jnp.maximum(top, part)
            top = filled(jnp.max(top, axis=1, keepdims=True))
            total = None
            for j, count in chunks(6, width):
                cols = slice(j * width, (j + count) * width)
                e = jnp.exp(s_scr[x, :, cols] - lanes(top, count * width))
                store(em, (y,), rows, j, count, x, e.astype(BF16))
                if width == 128:
                    store(em, (y,), rows, j, count, 3 - x, jnp.zeros((ROW, count * width), BF16))
                part = lane_sum(e)
                total = part if total is None else total + part
            wide = dot(em[y, rows, :], pm_rows(vm))
            a1[y, CUBE * x : CUBE * x + CUBE, :] = collect(wide, mask)
            top_out[y, rows, :] = top
            sum_out[y, rows, :] = filled(jnp.sum(total, axis=1, keepdims=True))
        return carry

    lax.fori_loop(0, 2, step, 0)


def pm_rows(ref, *lead):
    return ref[(*lead, slice(None), slice(None), slice(None))].reshape(-1, D)


def main_kernel(
    mid_y, low_y, high_y, wp, wv, wo, p0, g0, xs, cs, bias_a, bias_b, xm, pm, vm, em, a1,
    top_in, sum_in,
    back_low, back_mid, back_high, own_back, part, mixed,
    xe, pe, ve, s_scr, ee, slopes, pf_mid, pf_edge, gf_mid, gf_edge, kg, vg, kge, vge, att, qg,
):
    shuffle = to_blocks_matrix()
    back = from_blocks_matrix()
    mask = head_mask()
    for z, slab in enumerate((low_y, mid_y, high_y)):
        for side in range(2):
            x = dot(shuffle, slab[side].reshape(ROW, D)).astype(BF16)
            xe[side, z] = x
            pe[side, z] = dot(x, wp[...]).astype(BF16)
            ve[side, z] = dot(x, wv[...]).astype(BF16)
    kg[...] = jnp.zeros_like(kg)
    vg[...] = jnp.zeros_like(vg)
    for x in (0, 3):
        rows = slice(ROW * x, ROW * x + ROW)
        for j in range(9):
            store(slopes, (), rows, j, 1, 3 - x, jnp.zeros((ROW, 128), BF16))
        for j in range(3):
            store(ee, (), rows, j, 1, 3 - x, jnp.zeros((ROW, 128), BF16))

    def step(y, carry):
        for x in range(4):
            start, width = span(x)
            rows = slice(ROW * x, ROW * x + ROW)
            here = slice(CUBE * x, CUBE * x + CUBE)
            q32 = spread(own_rows(p0, y, x), mask, 0.125)
            g32 = spread(own_rows(g0, y, x), mask)
            q = q32.astype(BF16)
            g = g32.astype(BF16)
            top1 = top_in[y, rows, :]
            top = None
            for j, count in chunks(3, width):
                cols = slice(j * width, (j + count) * width)
                wide_cols = slice((6 + j) * width, (6 + j + count) * width)
                s = dot(q, take(pe, (y,), j, count, start, width), NT)
                s = s + bias_of(bias_a, bias_b, y, x, wide_cols)
                s_scr[x, :, cols] = s
                part_top = lane_max(s)
                top = part_top if top is None else jnp.maximum(top, part_top)
            top = jnp.maximum(filled(jnp.max(top, axis=1, keepdims=True)), top1)
            total = None
            for j, count in chunks(3, width):
                cols = slice(j * width, (j + count) * width)
                e = jnp.exp(s_scr[x, :, cols] - lanes(top, count * width))
                store(ee, (), rows, j, count, x, e.astype(BF16))
                part_sum = lane_sum(e)
                total = part_sum if total is None else total + part_sum
            keep = jnp.exp(top1 - top)
            total = filled(jnp.sum(total, axis=1, keepdims=True)) + sum_in[y, rows, :] * keep
            inverse = 1.0 / total
            f_edge = lanes(inverse, D)
            f_mid = lanes(keep * inverse, D)
            wide = dot(ee[rows, :], pm_rows(ve, y))
            attended = a1[y, here, :] * collect(f_mid, mask) + collect(wide * f_edge, mask)
            attended = attended.astype(BF16)
            att[y, here, :] = attended
            product = own_rows(g0, y, x).astype(F32) * attended.astype(F32)
            delta = filled(jnp.sum(lane_sum(spread(product, mask)), axis=1, keepdims=True))
            pf_mid[rows, :] = (q32 * f_mid).astype(BF16)
            pf_edge[rows, :] = (q32 * f_edge).astype(BF16)
            gf_mid[rows, :] = (g32 * f_mid).astype(BF16)
            gf_edge[rows, :] = (g32 * f_edge).astype(BF16)
            for number, base, v_ref, lead in ((6, 0, vm, ()), (3, 6, ve, (y,))):
                for j, count in chunks(number, width):
                    pushed = dot(g, take(v_ref, lead, j, count, start, width), NT)
                    pushed = pushed - lanes(delta, count * width)
                    for n in range(count):
                        at = (j + n) * ROW + start
                        cols = slice(at, at + width)
                        e = em[y, rows, cols] if base == 0 else ee[rows, cols]
                        value = e.astype(F32) * pushed[:, n * width : n * width + width]
                        store(slopes, (), rows, base + j + n, 1, x, value.astype(BF16))
            wide = dot(slopes[rows, 0:1536], pm_rows(pm)) * f_mid
            wide = wide + dot(slopes[rows, 1536:2304], pm_rows(pe, y)) * f_edge
            qg[y, here, :] = (collect(wide, mask) * 0.125).astype(BF16)
        for n in range(6):
            cols = slice(n * ROW, n * ROW + ROW)
            kg[n] += dot(slopes[:, cols], pf_mid[...], TN)
            vg[n] += dot(em[y, :, cols], gf_mid[...], TN)
        for z in range(3):
            cols = slice(z * ROW, z * ROW + ROW)
            wide_cols = slice((6 + z) * ROW, (7 + z) * ROW)
            kge[y, z] = dot(slopes[:, wide_cols], pf_edge[...], TN).astype(BF16)
            vge[y, z] = dot(ee[:, cols], gf_edge[...], TN).astype(BF16)
        return carry

    lax.fori_loop(0, 2, step, 0)
    gp = dot(xs[0], qg[0], TN) + dot(xs[1], qg[1], TN)
    gv = jnp.zeros((D, D), F32)
    for z, out in enumerate((back_low, back_mid, back_high)):
        for r in range(4):
            if r in (1, 2):
                x, k, v = xm[2 * z + r - 1], kg[2 * z + r - 1].astype(BF16), vg[2 * z + r - 1].astype(BF16)
            else:
                x, k, v = xe[r // 3, z], kge[r // 3, z], vge[r // 3, z]
            out[r] = (dot(k, wp[...], NT) + dot(v, wv[...], NT)).astype(BF16)
            gp = gp + dot(x, k, TN)
            gv = gv + dot(x, v, TN)
    part[:, 0:256] = gp.astype(BF16)
    part[:, 256:512] = gv.astype(BF16)
    gout = dot(att[0], cs[0], TN) + dot(att[1], cs[1], TN)
    part[:, 512:768] = gout.astype(BF16)
    for y in range(2):
        own_back[y] = dot(qg[y], wp[...], NT)
        out = dot(att[y], wo[...]).astype(BF16)
        mixed[:, 4 * y : 4 * y + 4] = dot(back, out).astype(BF16).reshape(4, 4, 16, D)


def finish_kernel(own_back, summed, from_low, from_high, grad):
    back = from_blocks_matrix()
    for y, side in enumerate((from_low, from_high)):
        out = (own_back[y] + summed[y] + side[...].astype(F32)).astype(BF16)
        grad[:, 4 * y : 4 * y + 4] = dot(back, out).astype(BF16).reshape(4, 4, 16, D)


def call(body, outs, scratch=(), flops=0, name=None, limit=16):
    return pl.pallas_call(
        body,
        out_shape=tuple(jax.ShapeDtypeStruct(shape, dtype) for shape, dtype in outs),
        scratch_shapes=list(scratch),
        compiler_params=pltpu.CompilerParams(vmem_limit_bytes=limit * 1024 * 1024),
        cost_estimate=pl.CostEstimate(flops=flops, bytes_accessed=4 * 1024 * 1024, transcendentals=0),
        name=name,
    )


def shift(block, other, dz, dy):
    scans, depth, height = (lax.axis_size(axis) for axis in AXES)
    route = []
    for s in range(scans):
        for z in range(depth):
            for y in range(height):
                if 0 <= z + dz < depth and 0 <= y + dy < height:
                    target = s ^ other
                    route.append(
                        (
                            (s * depth + z) * height + y,
                            (target * depth + z + dz) * height + y + dy,
                        )
                    )
    return lax.ppermute(block, AXES, route)


def slabs(own):
    return shift(own, 1, 1, 0), shift(own, 1, 0, 0), shift(own, 1, -1, 0)


def window_bias(flags):
    side = lax.axis_index("scan")
    plane = lax.axis_index("gz")
    row = lax.axis_index("gy") * 2
    near = jnp.pad(flags, ((0, 0), (1, 1), (1, 1), (0, 0)))
    near_other = lax.dynamic_slice(near, (1 - side, plane, row, 0), (1, 3, 4, 4))[0]

    def nine(window):
        middle = window[:, 1:3].reshape((6,) + window.shape[2:])
        return jnp.stack(
            [jnp.concatenate([middle, window[:, 0]]), jnp.concatenate([middle, window[:, 3]])]
        )

    xs = np.arange(4)
    adjacent = np.abs(xs[:, None] - xs[None, :]) <= 1
    center = np.zeros((2, 4, 9, 4), bool)
    for y in range(2):
        for x in range(4):
            center[y, x, 2 + y, x] = True
    adjacent = adjacent[None, :, None, :]
    valid = adjacent & ((nine(near_other)[:, None] > 0) | center)
    bias = jnp.where(valid, 0.0, NEG).astype(F32)
    a = jnp.stack([bias[:, 0, :, 0:2], bias[:, 3, :, 2:4]], axis=1)
    b = bias[:, 1:3]
    return (
        jnp.repeat(a.reshape(4, 1, 18), CUBE, axis=2),
        jnp.repeat(b.reshape(4, 1, 36), CUBE, axis=2),
    )


def summed_share(part):
    half = part.shape[0] // 2
    side = lax.axis_index("scan")
    mine = lax.dynamic_slice_in_dim(part, side * half, half, 0)
    other = lax.dynamic_slice_in_dim(part, (1 - side) * half, half, 0)
    mine = (mine.astype(F32) + shift(other, 1, 0, 0).astype(F32)).astype(BF16)
    places = lax.axis_size("gz") * lax.axis_size("gy")
    got = lax.all_to_all(mine.reshape(places, -1), ("gz", "gy"), 0, 0, tiled=True)
    return jnp.sum(got.astype(F32), axis=0).astype(BF16)


def all_shares(total):
    places = lax.axis_size("gz") * lax.axis_size("gy")
    full = lax.all_to_all(
        jnp.broadcast_to(total[None], (places,) + total.shape), ("gz", "gy"), 0, 0, tiled=True
    )
    return full


def both_halves(full, half):
    side = lax.axis_index("scan")
    full = full.reshape(half, -1)
    away = shift(full, 1, 0, 0)
    first = jnp.where(side == 0, full, away)
    second = jnp.where(side == 0, away, full)
    return jnp.concatenate([first, second], axis=0).astype(F32)


def after(value, token):
    return lax.optimization_barrier((value, token))[0]


def on_device(scans, proj_weight, value_weight, out_weight, flags, cotangent):
    own = scans[0]
    cot = cotangent[0]
    weights = (proj_weight, value_weight, out_weight)
    wide = (ROW, D)
    columns = ((2, 4 * ROW, 128), F32)
    unit = 2 * ROW * ROW * D

    low_y = shift(own[:, 4:], 1, 0, 1)
    high_y = shift(own[:, :4], 1, 0, -1)
    zl, zm, zh = slabs(own)
    bias = window_bias(flags)
    xs, cs, p0, g0 = call(own_kernel, [((2,) + wide, BF16)] * 4, flops=10 * unit, name="own")(
        own, cot, proj_weight, out_weight
    )
    mid_y = jnp.stack([low_y, high_y])
    low_zy = shift(mid_y, 0, 1, 0)
    high_zy = shift(mid_y, 0, -1, 0)
    xm, pm, vm, em, a1, top, total = call(
        mid_kernel,
        [((6,) + wide, BF16)] * 3
        + [((2, 4 * ROW, 6 * ROW), BF16), ((2,) + wide, F32), columns, columns],
        [pltpu.VMEM((4, ROW, 6 * ROW), F32)],
        flops=300 * unit,
        name="mid",
        limit=20,
    )(zl, zm, zh, proj_weight, value_weight, after(p0, mid_y), *bias)
    back_low, back_mid, back_high, own_back, part, mixed = call(
        main_kernel,
        [((4,) + wide, BF16)] * 3
        + [((2,) + wide, F32), ((ROW, 3 * D), BF16), (own.shape, BF16)],
        [pltpu.VMEM((2, 3) + wide, BF16)] * 3
        + [
            pltpu.VMEM((4, ROW, 3 * ROW), F32),
            pltpu.VMEM((4 * ROW, 3 * ROW), BF16),
            pltpu.VMEM((4 * ROW, 9 * ROW), BF16),
        ]
        + [pltpu.VMEM((4 * ROW, D), BF16)] * 4
        + [pltpu.VMEM((6,) + wide, F32)] * 2
        + [pltpu.VMEM((2, 3) + wide, BF16)] * 2
        + [pltpu.VMEM((2,) + wide, BF16)] * 2,
        flops=900 * unit,
        name="main",
        limit=36,
    )(mid_y, low_zy, high_zy, *weights, p0, g0, xs, cs, *bias, xm, pm, vm, em, a1, top, total)

    got = (
        shift(back_low, 1, -1, 0).astype(F32)
        + shift(back_mid, 1, 0, 0).astype(F32)
        + shift(back_high, 1, 1, 0).astype(F32)
    )
    to_low = got[0].astype(BF16)
    to_high = got[3].astype(BF16)
    share = summed_share(part)
    from_high = shift(to_low, 0, 0, -1)
    from_low = shift(to_high, 0, 0, 1)
    shares = all_shares(after(share, (to_low, to_high)))
    (grad,) = call(finish_kernel, [(own.shape, BF16)], flops=4 * unit, name="finish")(
        own_back, got[1:3], from_low, from_high
    )
    sums = both_halves(after(shares, grad), part.shape[0] // 2)
    return (
        mixed[None],
        grad[None],
        sums[:, 0:256],
        sums[:, 256:512],
        sums[:, 512:768],
    )


def solution(mesh):
    field = P("scan", "gz", "gy", None, None)
    return jax.shard_map(
        on_device,
        mesh=mesh,
        in_specs=(field, P(), P(), P(), P(), field),
        out_specs=(field, field, P(), P(), P()),
        check_vma=False,
    )
```

time: 154 us -> 126 us (0.82)
  blocking collectives: 50.6 us -> 0 us
  waiting for transfers between devices: 6.13 us -> 19.4 us
  starting transfers between devices: 48.8 us -> 59.4 us
  Pallas kernels: 37.2 us -> 28.1 us
  local copies, waits for them, and re-layouts: 6.34 us -> 11.9 us
  other arithmetic: 3.51 us -> 5.37 us
    all_to_all x2 -> x0, blocking collectives: 50.6 us -> none  [the longest x1 32.3 us: total_of(): lax.all_to_all(mine.reshape(places, -1), ('gz', 'gy'), 0, 0, tiled=True)]
    all_to_all x0 -> x2, starting transfers between devices: none -> 23.9 us  [the longest x1 17.1 us: summed_share(): lax.all_to_all(mine.reshape(places, -1), ('gz', 'gy'), 0, 0, tiled=True)]
    ppermute x19 -> x14, starting transfers between devices: 48.8 us -> 35.4 us  [shift(): return lax.ppermute(block, AXES, route)]
    all_to_all x0 -> x2, waiting for transfers between devices: none -> 10.5 us  [the longest x1 10.5 us: summed_share(): lax.all_to_all(mine.reshape(places, -1), ('gz', 'gy'), 0, 0, tiled=True)]
    pallas_call x6 -> x4, Pallas kernels: 37.2 us -> 28.1 us  [the longest x1 20 us: on_device(): call(main_kernel, [((4,) + wide, BF16)] * 3 + [((2,) + wide, F32), ((ROW,...]
    unnamed x21 -> x23, local copies, waits for them, and re-layouts: 1.3 us -> 7.29 us
    ppermute x19 -> x14, waiting for transfers between devices: 6.13 us -> 8.84 us  [shift(): return lax.ppermute(block, AXES, route)]
  transfers between devices with their start and end apart: 19 -> 16, of which waited for: 6 -> 6; matrix products, arithmetic and copies ran while one was open for 3% -> 6% of each run, Pallas kernels for 17% -> 6%
where the time goes in v3:
time: 126 us; the launch traced here: 125 us
  starting transfers between devices  59.4 us (47%)
  Pallas kernels  28.1 us (22%)
  waiting for transfers between devices  19.4 us (15%)
  local copies, waits for them, and re-layouts  11.9 us (9%)
  other arithmetic  5.37 us (4%)
    ppermute x14, starting transfers between devices, shift(): return lax.ppermute(block, AXES, route)  35.4 us
    pallas_call x1, Pallas kernels, on_device(): call(main_kernel, [((4,) + wide, BF16)] * 3 + [((2,) + wide, F32), ((ROW,...  20 us
    all_to_all x1, starting transfers between devices, summed_share(): lax.all_to_all(mine.reshape(places, -1), ('gz', 'gy'), 0, 0, tiled=True)  17.1 us
    all_to_all x1, waiting for transfers between devices, summed_share(): lax.all_to_all(mine.reshape(places, -1), ('gz', 'gy'), 0, 0, tiled=True)  10.5 us
    ppermute x14, waiting for transfers between devices, shift(): return lax.ppermute(block, AXES, route)  8.84 us
    unnamed x23, local copies, waits for them, and re-layouts  7.29 us
    all_to_all x1, starting transfers between devices, all_shares(): lax.all_to_all(jnp.broadcast_to(total[None], (places,) + total.shape), ('...  6.82 us
    pallas_call x1, Pallas kernels, on_device(): call(mid_kernel, [((6,) + wide, BF16)] * 3 + [((2, 4 * ROW, 6 * ROW), BF1...  6.5 us
  transfers between devices with their start and end apart: 16, of which 6 were waited for; matrix products, arithmetic and copies ran while one was open for 6% of the time, Pallas kernels for 6%

profile of v3, /device:TPU:1, one launch (start us, length us, event | category | flops | bytes accessed | tf_op | source)
XLA Modules:
  0.0 125.1 jit_solution(684510038079408360)
XLA Ops:
  0.6 4.9 %collective-permute-start.4 = (bf16[4,8,16,256]{3,2,1,0:T(8,128)(2,1)}, bf16[4,8,16,256]{3,2,1,0:T(8,128)(2,1)S(1)}, u32[]{:S(2)}, u32[]{:S(2)}) collective-permute-start(bf16[4,8,16,256]{3,2,1,0:T(8,128)(2,1)} %bitcast.22), channel_id=1, source_target_pairs={{0,136},{1,137},{2,138},{3,139},{4,140},{5,141},{6,142},{7,143},{8... | collective-permute-start | bytes 786440 | tf_op jit(solution)/shard_map/ppermute | solution.py:326
  5.7 1.3 %collective-permute-start.6 = (bf16[4,8,16,256]{3,2,1,0:T(8,128)(2,1)}, bf16[4,8,16,256]{3,2,1,0:T(8,128)(2,1)S(1)}, u32[]{:S(2)}, u32[]{:S(2)}) collective-permute-start(bf16[4,8,16,256]{3,2,1,0:T(8,128)(2,1)} %bitcast.24), channel_id=1, source_target_pairs={{8,128},{9,129},{10,130},{11,131},{12,132},{13,133},{14,134},{15,1... | collective-permute-start | bytes 786440 | tf_op jit(solution)/shard_map/ppermute | solution.py:326
  7.0 1.0 fusion.3
  8.0 5.2 %collective-permute-start = (bf16[4,4,16,256]{3,2,1,0:T(8,128)(2,1)S(1)}, bf16[4,4,16,256]{3,2,1,0:T(8,128)(2,1)S(1)}, u32[]{:S(2)}, u32[]{:S(2)}) collective-permute-start(bf16[4,4,16,256]{3,2,1,0:T(8,128)(2,1)S(1)} %get-tuple-element.54), channel_id=1, source_target_pairs={{0,129},{1,130},{2,131},{3,132},{4,133},{5,134},{6,135},{8,137},{9... | collective-permute-start | bytes 393224 | tf_op jit(solution)/shard_map/ppermute | solution.py:326
  13.2 1.3 %collective-permute-start.1 = (bf16[4,4,16,256]{3,2,1,0:T(8,128)(2,1)S(1)}, bf16[4,4,16,256]{3,2,1,0:T(8,128)(2,1)S(1)}, u32[]{:S(2)}, u32[]{:S(2)}) collective-permute-start(bf16[4,4,16,256]{3,2,1,0:T(8,128)(2,1)S(1)} %get-tuple-element.55), channel_id=1, source_target_pairs={{1,128},{2,129},{3,130},{4,131},{5,132},{6,133},{7,134},{9,136},{1... | collective-permute-start | bytes 393224 | tf_op jit(solution)/shard_map/ppermute | solution.py:326
  21.8 4.4 %collective-permute-start.2 = (bf16[2,4,4,16,256]{4,3,2,1,0:T(8,128)(2,1)S(1)}, bf16[2,4,4,16,256]{4,3,2,1,0:T(8,128)(2,1)S(1)}, u32[]{:S(2)}, u32[]{:S(2)}) collective-permute-start(bf16[2,4,4,16,256]{4,3,2,1,0:T(8,128)(2,1)S(1)} %pad_maximum_fusion.mid_y), channel_id=1, source_target_pairs={{0,8},{1,9},{2,10},{3,11},{4,12},{5,13},{6,14},{7,15},{8,16},{9,17... | collective-permute-start | bytes 786440 | tf_op jit(solution)/shard_map/ppermute | solution.py:326
  26.1 1.3 %collective-permute-start.3 = (bf16[2,4,4,16,256]{4,3,2,1,0:T(8,128)(2,1)S(1)}, bf16[2,4,4,16,256]{4,3,2,1,0:T(8,128)(2,1)S(1)}, u32[]{:S(2)}, u32[]{:S(2)}) collective-permute-start(bf16[2,4,4,16,256]{4,3,2,1,0:T(8,128)(2,1)S(1)} %pad_maximum_fusion.mid_y), channel_id=1, source_target_pairs={{8,0},{9,1},{10,2},{11,3},{12,4},{13,5},{14,6},{15,7},{16,8},{17,9... | collective-permute-start | bytes 786440 | tf_op jit(solution)/shard_map/ppermute | solution.py:326
  29.3 6.5 %mid.1 = (bf16[6,256,256]{2,1,0:T(8,128)(2,1)S(1)}, bf16[6,256,256]{2,1,0:T(8,128)(2,1)S(1)}, bf16[6,256,256]{2,1,0:T(8,128)(2,1)S(1)}, bf16[2,1024,1536]{2,1,0:...) custom-call(bf16[4,8,16,256]{3,2,1,0:T(8,128)(2,1)S(1)} %collective-permute-, ...), custom_call_target="tpu_custom_call" | custom-call | flops 10066329600 | bytes 4194304 | tf_op jit(solution)/shard_map/mid/pallas_call | solution.py:413
  35.8 20.0 %main.1 = (bf16[4,256,256]{2,1,0:T(8,128)(2,1)S(1)}, bf16[4,256,256]{2,1,0:T(8,128)(2,1)S(1)}, bf16[4,256,256]{2,1,0:T(8,128)(2,1)S(1)}, f32[2,256,256]{2,1,0:T(...) custom-call(bf16[2,4,4,16,256]{4,3,2,1,0:T(8,128)(2,1)S(1)} %pad_maximum_fusion.mid_y, ...), custom_call_target="tpu_custom_call" | custom-call | flops 30198988800 | bytes 4194304 | tf_op jit(solution)/shard_map/main/pallas_call | solution.py:422
  55.9 1.3 %collective-permute-start.7 = (bf16[4,256,256]{2,1,0:T(8,128)(2,1)S(1)}, bf16[4,256,256]{2,1,0:T(8,128)(2,1)S(1)}, u32[]{:S(2)}, u32[]{:S(2)}) collective-permute-start(bf16[4,256,256]{2,1,0:T(8,128)(2,1)S(1)} %get-tuple-element.39), channel_id=1, source_target_pairs={{8,128},{9,129},{10,130},{11,131},{12,132},{13,133},{14,134},{15,1... | collective-permute-start | bytes 1572872 | tf_op jit(solution)/shard_map/ppermute | solution.py:326
  57.2 1.2 collective-permute-start.8
  58.3 5.9 %collective-permute-start.9 = (bf16[4,256,256]{2,1,0:T(8,128)(2,1)S(1)}, bf16[4,256,256]{2,1,0:T(8,128)(2,1)}, u32[]{:S(2)}, u32[]{:S(2)}) collective-permute-start(bf16[4,256,256]{2,1,0:T(8,128)(2,1)S(1)} %get-tuple-element.41), channel_id=1, source_target_pairs={{0,136},{1,137},{2,138},{3,139},{4,140},{5,141},{6,142},{7,143},{8... | collective-permute-start | bytes 1572872 | tf_op jit(solution)/shard_map/ppermute | solution.py:326
  64.8 1.1 collective-permute-done.12
  67.9 17.1 %all-to-all-start = ((bf16[128,2,384]{2,1,0:T(2,128)(2,1)}), bf16[128,2,384]{2,1,0:T(2,128)(2,1)S(1)}, u32[]{:S(2)}, u32[]{:S(2)}) async-start(bf16[128,2,384]{2,1,0:T(2,128)(2,1)} %reshape.63), calls=%async_computation | async-start | bytes 393216 | tf_op jit(solution)/shard_map/all_to_all | solution.py:370
  85.1 1.4 %fusion.1 = (bf16[4,256,256]{2,1,0:T(8,128)(2,1)S(1)}, f32[4,256,256]{2,1,0:T(8,128)S(1)}) fusion(bf16[4,256,256]{2,1,0:T(8,128)(2,1)} %collective-permute-done.9, bf16[4,256,256]{2,1,0:T(8,128)(2,1)} %collective-permute-done.8, bf16[4,256,256]{2,1,0:T(8,128)(2,1)S(1)} %collective-permute-done.7), kind=kLoop, calls=%fused_computation.17 | loop fusion | flops 1572864 | bytes 3145728 | tf_op jit(solution)/shard_map/convert.2
  86.5 10.5 %all-to-all-done = bf16[128,2,384]{2,1,0:T(2,128)(2,1)S(1)} async-done(((bf16[128,2,384]{2,1,0:T(2,128)(2,1)}), bf16[128,2,384]{2,1,0:T(2,128)(2,1)S(1)}, u32[]{:S(2)}, u32[]{:S(2)}) %all-to-all-start) | async-done | bytes 196640 | tf_op jit(solution)/shard_map/all_to_all | solution.py:370
  97.8 1.8 %reduce.3 = bf16[128,768]{1,0:T(8,128)(2,1)S(1)} reduce(bf16[128,1,768]{2,1,0:T(2,128)(2,1)S(1)} %broadcast_in_dim.39, bf16[]{:T(256)} %broadcast.16), dimensions={1}, to_apply=%broadcast_in_dim.39.reduce_sub_computation | reduce | bytes 393218 | tf_op jit(solution)/shard_map/broadcast_in_dim | solution.py:377
  100.4 6.8 %all-to-all-start.1 = ((bf16[128,2,384]{2,1,0:T(2,128)(2,1)}), bf16[128,2,384]{2,1,0:T(2,128)(2,1)S(1)}, u32[]{:S(2)}, u32[]{:S(2)}) async-start(bf16[128,2,384]{2,1,0:T(2,128)(2,1)} %reshape.65), calls=%async_computation.1 | async-start | bytes 393216 | tf_op jit(solution)/shard_map/all_to_all | solution.py:376
  107.2 4.0 %collective-permute-start.10 = (bf16[256,256]{1,0:T(8,128)(2,1)S(1)}, bf16[256,256]{1,0:T(8,128)(2,1)S(1)}, u32[]{:S(2)}, u32[]{:S(2)}) collective-permute-start(bf16[256,256]{1,0:T(8,128)(2,1)S(1)} %get-tuple-element.51), channel_id=1, source_target_pairs={{0,1},{1,2},{2,3},{3,4},{4,5},{5,6},{6,7},{8,9},{9,10},{10,11},{11... | collective-permute-start | bytes 393224 | tf_op jit(solution)/shard_map/ppermute | solution.py:326
  111.2 1.3 %collective-permute-start.11 = (bf16[256,256]{1,0:T(8,128)(2,1)S(1)}, bf16[256,256]{1,0:T(8,128)(2,1)S(1)}, u32[]{:S(2)}, u32[]{:S(2)}) collective-permute-start(bf16[256,256]{1,0:T(8,128)(2,1)S(1)} %get-tuple-element.50), channel_id=1, source_target_pairs={{1,0},{2,1},{3,2},{4,3},{5,4},{6,5},{7,6},{9,8},{10,9},{11,10},{12... | collective-permute-start | bytes 393224 | tf_op jit(solution)/shard_map/ppermute | solution.py:326
  112.5 1.1 collective-permute-done.10.from_low
  113.6 5.5 %collective-permute-done.11.from_high = bf16[256,256]{1,0:T(8,128)(2,1)S(1)} collective-permute-done((bf16[256,256]{1,0:T(8,128)(2,1)S(1)}, bf16[256,256]{1,0:T(8,128)(2,1)S(1)}, u32[]{:S(2)}, u32[]{:S(2)}) %collective-permute-start.11) | collective-permute-done | bytes 131104 | tf_op jit(solution)/shard_map/ppermute | solution.py:326
  120.3 2.8 %collective-permute-start.13 = (bf16[128,768]{1,0:T(8,128)(2,1)S(1)}, bf16[128,768]{1,0:T(8,128)(2,1)S(1)}, u32[]{:S(2)}, u32[]{:S(2)}) collective-permute-start(bf16[128,768]{1,0:T(8,128)(2,1)S(1)} %bitcast.28), channel_id=1, source_target_pairs={{0,128},{1,129},{2,130},{3,131},{4,132},{5,133},{6,134},{7,135},{8... | collective-permute-start | bytes 589832 | tf_op jit(solution)/shard_map/ppermute | solution.py:326
  123.1 1.1 collective-permute-done.13
  (72 shorter events, 15.4 us)
Async XLA Ops:
  0.6 26.8 %collective-permute-start.4 = (bf16[4,8,16,256]{3,2,1,0:T(8,128)(2,1)}, bf16[4,8,16,256]{3,2,1,0:T(8,128)(2,1)S(1)}, u32[]{:S(2)}, u32[]{:S(2)}) collective-permute-start(bf16[4,8,16,256]{3,2,1,0:T(8,128)(2,1)} %bitcast.22), channel_id=1, source_target_pairs={{0,136},{1,137},{2,138},{3,139},{4,140},{5,141},{6,142},{7,143},{8... | collective-permute-start | bytes 786440 | tf_op jit(solution)/shard_map/ppermute | solution.py:326
  5.6 21.9 %collective-permute-start.5 = (bf16[4,8,16,256]{3,2,1,0:T(8,128)(2,1)}, bf16[4,8,16,256]{3,2,1,0:T(8,128)(2,1)S(1)}, u32[]{:S(2)}, u32[]{:S(2)}) collective-permute-start(bf16[4,8,16,256]{3,2,1,0:T(8,128)(2,1)} %bitcast.23), channel_id=1, source_target_pairs={{0,128},{1,129},{2,130},{3,131},{4,132},{5,133},{6,134},{7,135},{8... | collective-permute-start | bytes 786440 | tf_op jit(solution)/shard_map/ppermute | solution.py:326
  5.7 21.8 %collective-permute-start.6 = (bf16[4,8,16,256]{3,2,1,0:T(8,128)(2,1)}, bf16[4,8,16,256]{3,2,1,0:T(8,128)(2,1)S(1)}, u32[]{:S(2)}, u32[]{:S(2)}) collective-permute-start(bf16[4,8,16,256]{3,2,1,0:T(8,128)(2,1)} %bitcast.24), channel_id=1, source_target_pairs={{8,128},{9,129},{10,130},{11,131},{12,132},{13,133},{14,134},{15,1... | collective-permute-start | bytes 786440 | tf_op jit(solution)/shard_map/ppermute | solution.py:326
  8.0 13.7 %collective-permute-start = (bf16[4,4,16,256]{3,2,1,0:T(8,128)(2,1)S(1)}, bf16[4,4,16,256]{3,2,1,0:T(8,128)(2,1)S(1)}, u32[]{:S(2)}, u32[]{:S(2)}) collective-permute-start(bf16[4,4,16,256]{3,2,1,0:T(8,128)(2,1)S(1)} %get-tuple-element.54), channel_id=1, source_target_pairs={{0,129},{1,130},{2,131},{3,132},{4,133},{5,134},{6,135},{8,137},{9... | collective-permute-start | bytes 393224 | tf_op jit(solution)/shard_map/ppermute | solution.py:326
  13.2 8.5 %collective-permute-start.1 = (bf16[4,4,16,256]{3,2,1,0:T(8,128)(2,1)S(1)}, bf16[4,4,16,256]{3,2,1,0:T(8,128)(2,1)S(1)}, u32[]{:S(2)}, u32[]{:S(2)}) collective-permute-start(bf16[4,4,16,256]{3,2,1,0:T(8,128)(2,1)S(1)} %get-tuple-element.55), channel_id=1, source_target_pairs={{1,128},{2,129},{3,130},{4,131},{5,132},{6,133},{7,134},{9,136},{1... | collective-permute-start | bytes 393224 | tf_op jit(solution)/shard_map/ppermute | solution.py:326
  17.4 1.0 copy-start
  18.3 0.9 copy-start.1
  19.3 0.9 copy-start.2
  20.2 0.9 copy-start.7
  21.8 14.0 %collective-permute-start.2 = (bf16[2,4,4,16,256]{4,3,2,1,0:T(8,128)(2,1)S(1)}, bf16[2,4,4,16,256]{4,3,2,1,0:T(8,128)(2,1)S(1)}, u32[]{:S(2)}, u32[]{:S(2)}) collective-permute-start(bf16[2,4,4,16,256]{4,3,2,1,0:T(8,128)(2,1)S(1)} %pad_maximum_fusion.mid_y), channel_id=1, source_target_pairs={{0,8},{1,9},{2,10},{3,11},{4,12},{5,13},{6,14},{7,15},{8,16},{9,17... | collective-permute-start | bytes 786440 | tf_op jit(solution)/shard_map/ppermute | solution.py:326
  26.1 9.7 %collective-permute-start.3 = (bf16[2,4,4,16,256]{4,3,2,1,0:T(8,128)(2,1)S(1)}, bf16[2,4,4,16,256]{4,3,2,1,0:T(8,128)(2,1)S(1)}, u32[]{:S(2)}, u32[]{:S(2)}) collective-permute-start(bf16[2,4,4,16,256]{4,3,2,1,0:T(8,128)(2,1)S(1)} %pad_maximum_fusion.mid_y), channel_id=1, source_target_pairs={{8,0},{9,1},{10,2},{11,3},{12,4},{13,5},{14,6},{15,7},{16,8},{17,9... | collective-permute-start | bytes 786440 | tf_op jit(solution)/shard_map/ppermute | solution.py:326
  27.5 0.9 copy-start.3
  29.3 6.5 %copy-start.4 = (bf16[256,256]{1,0:T(8,128)(2,1)S(1)}, bf16[256,256]{1,0:T(8,128)(2,1)}, u32[]{:S(2)}) copy-start(bf16[256,256]{1,0:T(8,128)(2,1)} %wp.5) | copy-start | bytes 393220
  29.3 6.5 %copy-start.6 = (bf16[256,256]{1,0:T(8,128)(2,1)S(1)}, bf16[256,256]{1,0:T(8,128)(2,1)}, u32[]{:S(2)}) copy-start(bf16[256,256]{1,0:T(8,128)(2,1)} %wv.3) | copy-start | bytes 393220
  29.3 6.6 %copy-start.8 = (bf16[256,256]{1,0:T(8,128)(2,1)S(1)}, bf16[256,256]{1,0:T(8,128)(2,1)}, u32[]{:S(2)}) copy-start(bf16[256,256]{1,0:T(8,128)(2,1)} %wo.3) | copy-start | bytes 393220
  55.9 29.2 %collective-permute-start.7 = (bf16[4,256,256]{2,1,0:T(8,128)(2,1)S(1)}, bf16[4,256,256]{2,1,0:T(8,128)(2,1)S(1)}, u32[]{:S(2)}, u32[]{:S(2)}) collective-permute-start(bf16[4,256,256]{2,1,0:T(8,128)(2,1)S(1)} %get-tuple-element.39), channel_id=1, source_target_pairs={{8,128},{9,129},{10,130},{11,131},{12,132},{13,133},{14,134},{15,1... | collective-permute-start | bytes 1572872 | tf_op jit(solution)/shard_map/ppermute | solution.py:326
  57.2 27.9 %collective-permute-start.8 = (bf16[4,256,256]{2,1,0:T(8,128)(2,1)S(1)}, bf16[4,256,256]{2,1,0:T(8,128)(2,1)}, u32[]{:S(2)}, u32[]{:S(2)}) collective-permute-start(bf16[4,256,256]{2,1,0:T(8,128)(2,1)S(1)} %get-tuple-element.40), channel_id=1, source_target_pairs={{0,128},{1,129},{2,130},{3,131},{4,132},{5,133},{6,134},{7,135},{8... | collective-permute-start | bytes 1572872 | tf_op jit(solution)/shard_map/ppermute | solution.py:326
  58.3 26.7 %collective-permute-start.9 = (bf16[4,256,256]{2,1,0:T(8,128)(2,1)S(1)}, bf16[4,256,256]{2,1,0:T(8,128)(2,1)}, u32[]{:S(2)}, u32[]{:S(2)}) collective-permute-start(bf16[4,256,256]{2,1,0:T(8,128)(2,1)S(1)} %get-tuple-element.41), channel_id=1, source_target_pairs={{0,136},{1,137},{2,138},{3,139},{4,140},{5,141},{6,142},{7,143},{8... | collective-permute-start | bytes 1572872 | tf_op jit(solution)/shard_map/ppermute | solution.py:326
  64.2 1.6 %collective-permute-start.12 = (bf16[128,768]{1,0:T(8,128)(2,1)S(1)}, bf16[128,768]{1,0:T(8,128)(2,1)S(1)}, u32[]{:S(2)}, u32[]{:S(2)}) collective-permute-start(bf16[128,768]{1,0:T(8,128)(2,1)S(1)} %constant_dynamic-slice_fusion), channel_id=1, source_target_pairs={{0,128},{1,129},{2,130},{3,131},{4,132},{5,133},{6,134},{7,135},{8... | collective-permute-start | bytes 589832 | tf_op jit(solution)/shard_map/ppermute | solution.py:326
  67.9 29.2 %all-to-all-start = ((bf16[128,2,384]{2,1,0:T(2,128)(2,1)}), bf16[128,2,384]{2,1,0:T(2,128)(2,1)S(1)}, u32[]{:S(2)}, u32[]{:S(2)}) async-start(bf16[128,2,384]{2,1,0:T(2,128)(2,1)} %reshape.63), calls=%async_computation | async-start | bytes 393216 | tf_op jit(solution)/shard_map/all_to_all | solution.py:370
  100.4 19.8 %all-to-all-start.1 = ((bf16[128,2,384]{2,1,0:T(2,128)(2,1)}), bf16[128,2,384]{2,1,0:T(2,128)(2,1)S(1)}, u32[]{:S(2)}, u32[]{:S(2)}) async-start(bf16[128,2,384]{2,1,0:T(2,128)(2,1)} %reshape.65), calls=%async_computation.1 | async-start | bytes 393216 | tf_op jit(solution)/shard_map/all_to_all | solution.py:376
  107.2 6.4 %collective-permute-start.10 = (bf16[256,256]{1,0:T(8,128)(2,1)S(1)}, bf16[256,256]{1,0:T(8,128)(2,1)S(1)}, u32[]{:S(2)}, u32[]{:S(2)}) collective-permute-start(bf16[256,256]{1,0:T(8,128)(2,1)S(1)} %get-tuple-element.51), channel_id=1, source_target_pairs={{0,1},{1,2},{2,3},{3,4},{4,5},{5,6},{6,7},{8,9},{9,10},{10,11},{11... | collective-permute-start | bytes 393224 | tf_op jit(solution)/shard_map/ppermute | solution.py:326
  111.2 8.0 %collective-permute-start.11 = (bf16[256,256]{1,0:T(8,128)(2,1)S(1)}, bf16[256,256]{1,0:T(8,128)(2,1)S(1)}, u32[]{:S(2)}, u32[]{:S(2)}) collective-permute-start(bf16[256,256]{1,0:T(8,128)(2,1)S(1)} %get-tuple-element.50), channel_id=1, source_target_pairs={{1,0},{2,1},{3,2},{4,3},{5,4},{6,5},{7,6},{9,8},{10,9},{11,10},{12... | collective-permute-start | bytes 393224 | tf_op jit(solution)/shard_map/ppermute | solution.py:326
  120.3 3.8 %collective-permute-start.13 = (bf16[128,768]{1,0:T(8,128)(2,1)S(1)}, bf16[128,768]{1,0:T(8,128)(2,1)S(1)}, u32[]{:S(2)}, u32[]{:S(2)}) collective-permute-start(bf16[128,768]{1,0:T(8,128)(2,1)S(1)} %bitcast.28), channel_id=1, source_target_pairs={{0,128},{1,129},{2,130},{3,131},{4,132},{5,133},{6,134},{7,135},{8... | collective-permute-start | bytes 589832 | tf_op jit(solution)/shard_map/ppermute | solution.py:326
  (1 other events, 0.9 us)

commit v4 on v3

v4 whole, which is shorter than its diff:
```python
import functools

import jax
import jax.numpy as jnp
import numpy as np
from jax import lax
from jax.experimental import pallas as pl
from jax.experimental.pallas import tpu as pltpu
from jax.sharding import PartitionSpec as P

D = 256
HEADS = 4
HEAD_DIM = 64
BLK = 4
CUBE = 64
ROW = 256
NEG = -1e30
AXES = ("scan", "gz", "gy")
F32 = jnp.float32
BF16 = jnp.bfloat16
NN = (((1,), (0,)), ((), ()))
NT = (((1,), (1,)), ((), ()))
TN = (((0,), (0,)), ((), ()))


def dot(a, b, dims=NN):
    return lax.dot_general(a, b, dims, preferred_element_type=F32)


def natural_of(t):
    return ((t >> 4) & 3) * 64 + ((t >> 2) & 3) * 16 + (t >> 6) * 4 + (t & 3)


def iota2(shape, axis):
    return lax.broadcasted_iota(jnp.int32, shape, axis)


def to_blocks_matrix():
    shape = (ROW, ROW)
    return (natural_of(iota2(shape, 0)) == iota2(shape, 1)).astype(F32).astype(BF16)


def from_blocks_matrix():
    shape = (ROW, ROW)
    return (natural_of(iota2(shape, 1)) == iota2(shape, 0)).astype(F32).astype(BF16)


def head_mask():
    shape = (ROW, D)
    return (iota2(shape, 0) // HEAD_DIM == iota2(shape, 1) // HEAD_DIM).astype(F32)


def spread(block, mask, scale=1.0):
    wide = jnp.concatenate([block.astype(F32)] * HEADS, axis=0)
    return wide * (mask * scale)


def collect(wide, mask):
    kept = wide * mask
    return (kept[0:64] + kept[64:128]) + (kept[128:192] + kept[192:256])


def chunks(rows, width):
    if width == ROW:
        return [(j, 1) for j in range(rows)]
    return [(j, min(2, rows - j)) for j in range(0, rows, 2)]


def take(ref, lead, j, count, start, width):
    return ref[(*lead, pl.ds(j, count), pl.ds(start, width))].reshape(count * width, D)


def span(x):
    return {0: (0, 128), 1: (0, 256), 2: (0, 256), 3: (128, 128)}[x]


def own_rows(ref, y, x):
    return ref[y, CUBE * x : CUBE * x + CUBE, :]


def bias_of(bias_a, bias_b, y, x, cols):
    return bias_b[2 * y + x - 1, :, cols] if x in (1, 2) else bias_a[2 * y + x // 3, :, cols]


def store(ref, lead, rows, j, count, x, value):
    start, width = span(x)
    for n in range(count):
        at = (j + n) * ROW + start
        ref[(*lead, rows, slice(at, at + width))] = value[:, n * width : n * width + width]


def lane_max(s):
    out = s[:, 0:128]
    for k in range(128, s.shape[1], 128):
        out = jnp.maximum(out, s[:, k : k + 128])
    return out


def lane_sum(s):
    out = s[:, 0:128]
    for k in range(128, s.shape[1], 128):
        out = out + s[:, k : k + 128]
    return out


def lanes(column, width):
    return column if width == 128 else jnp.concatenate([column] * (width // 128), axis=1)


def filled(column):
    return jnp.broadcast_to(column, (ROW, 128))


def turned(column):
    keep = iota2((CUBE, 128), 0) == (iota2((CUBE, 128), 1) & 63)
    rows = [
        jnp.sum(jnp.where(keep, column[64 * h : 64 * h + 64], 0.0), axis=0, keepdims=True)
        for h in range(HEADS)
    ]
    return jnp.concatenate(rows, axis=0)


def own_kernel(scans, cot, wp_in, wv_in, wo_in, xs, cs, p0, g0, wp, wv, wo):
    wp[...] = wp_in[...]
    wv[...] = wv_in[...]
    wo[...] = wo_in[...]
    shuffle = to_blocks_matrix()
    for y in range(2):
        x = dot(shuffle, scans[:, 4 * y : 4 * y + 4].reshape(ROW, D)).astype(BF16)
        c = dot(shuffle, cot[:, 4 * y : 4 * y + 4].reshape(ROW, D)).astype(BF16)
        xs[y] = x
        cs[y] = c
        p0[y] = dot(x, wp[...]).astype(BF16)
        g0[y] = dot(c, wo[...], NT).astype(BF16)


def project(shuffle, slab, wp, wv, xs, ps, vs, lead=()):
    for r in range(4):
        x = dot(shuffle, slab[:, 4 * r : 4 * r + 4].reshape(ROW, D)).astype(BF16)
        xs[(*lead, r)] = x
        ps[(*lead, r)] = dot(x, wp[...]).astype(BF16)
        vs[(*lead, r)] = dot(x, wv[...]).astype(BF16)


def window(ref, y, lead=()):
    return ref[(*lead, pl.ds(y, 3))].reshape(3 * ROW, D)


def larger(a, b):
    return b if a is None else jnp.maximum(a, b)


def mid_kernel(
    slab, wp, wv, p0, g0, bias_a, bias_b, xm, pm, vm, em, pushed, a1, top_out, sum_out, s_scr,
):
    shuffle = to_blocks_matrix()
    mask = head_mask()
    project(shuffle, slab, wp, wv, xm, pm, vm)

    def step(y, carry):
        for x in range(4):
            start, width = span(x)
            rows = slice(ROW * x, ROW * x + ROW)
            q = spread(own_rows(p0, y, x), mask, 0.125).astype(BF16)
            g = spread(own_rows(g0, y, x), mask).astype(BF16)
            top = None
            for j, count in chunks(3, width):
                cols = slice(j * width, (j + count) * width)
                s = dot(q, take(pm, (), y + j, count, start, width), NT)
                s = s + bias_of(bias_a, bias_b, y, x, cols)
                s_scr[x, :, cols] = s
                top = larger(top, lane_max(s))
                pushed[y, rows, cols] = dot(g, take(vm, (), y + j, count, start, width), NT)
            top = filled(jnp.max(top, axis=1, keepdims=True))
            total = jnp.zeros((ROW, 128), F32)
            for j, count in chunks(3, width):
                cols = slice(j * width, (j + count) * width)
                e = jnp.exp(s_scr[x, :, cols] - lanes(top, count * width))
                store(em, (y,), rows, j, count, x, e.astype(BF16))
                if width == 128:
                    store(em, (y,), rows, j, count, 3 - x, jnp.zeros((ROW, count * width), BF16))
                total = total + lane_sum(e)
            wide = dot(em[y, rows, :], window(vm, y))
            a1[y, CUBE * x : CUBE * x + CUBE, :] = collect(wide, mask)
            top_out[y, rows, :] = top
            sum_out[y, rows, :] = filled(jnp.sum(total, axis=1, keepdims=True))
        return carry

    lax.fori_loop(0, 2, step, 0)


def main_kernel(
    low_z, high_z, wp, wv, p0, g0, xs, cs, bias_a, bias_b, xm, pm, vm, em, pushed_in, a1,
    top_in, sum_in,
    back_mid, back_low, back_high, att, qg, part,
    xz, pz, vz, s_scr, ee, slopes, pf_mid, pf_edge, gf_mid, gf_edge, kg, vg,
):
    shuffle = to_blocks_matrix()
    mask = head_mask()
    for z, slab in enumerate((low_z, high_z)):
        project(shuffle, slab, wp, wv, xz, pz, vz, (z,))
    kg[...] = jnp.zeros_like(kg)
    vg[...] = jnp.zeros_like(vg)
    for x in (0, 3):
        rows = slice(ROW * x, ROW * x + ROW)
        for j in range(9):
            store(slopes, (), rows, j, 1, 3 - x, jnp.zeros((ROW, 128), BF16))
        for j in range(6):
            store(ee, (), rows, j, 1, 3 - x, jnp.zeros((ROW, 128), BF16))

    def step(y, carry):
        for x in range(4):
            start, width = span(x)
            rows = slice(ROW * x, ROW * x + ROW)
            here = slice(CUBE * x, CUBE * x + CUBE)
            outer = [(z, j, count) for z in range(2) for j, count in chunks(3, width)]
            q32 = spread(own_rows(p0, y, x), mask, 0.125)
            g32 = spread(own_rows(g0, y, x), mask)
            q = q32.astype(BF16)
            g = g32.astype(BF16)
            top1 = top_in[y, rows, :]
            top = None
            for z, j, count in outer:
                at = (3 * z + j) * width
                cols = slice(at, at + count * width)
                wide_cols = slice(3 * width + at, 3 * width + at + count * width)
                s = dot(q, take(pz, (z,), y + j, count, start, width), NT)
                s = s + bias_of(bias_a, bias_b, y, x, wide_cols)
                s_scr[x, :, cols] = s
                top = larger(top, lane_max(s))
            top = jnp.maximum(filled(jnp.max(top, axis=1, keepdims=True)), top1)
            total = jnp.zeros((ROW, 128), F32)
            for z, j, count in outer:
                at = (3 * z + j) * width
                e = jnp.exp(s_scr[x, :, at : at + count * width] - lanes(top, count * width))
                store(ee, (), rows, 3 * z + j, count, x, e.astype(BF16))
                total = total + lane_sum(e)
            keep = jnp.exp(top1 - top)
            total = filled(jnp.sum(total, axis=1, keepdims=True)) + sum_in[y, rows, :] * keep
            inverse = 1.0 / total
            f_edge = lanes(inverse, D)
            f_mid = lanes(keep * inverse, D)
            wide = dot(ee[rows, 0:768], window(vz, y, (0,)))
            wide = wide + dot(ee[rows, 768:1536], window(vz, y, (1,)))
            attended = a1[y, here, :] * collect(f_mid, mask) + collect(wide * f_edge, mask)
            attended = attended.astype(BF16)
            att[y, here, :] = attended
            product = own_rows(g0, y, x).astype(F32) * attended.astype(F32)
            delta = filled(jnp.sum(lane_sum(spread(product, mask)), axis=1, keepdims=True))
            pf_mid[rows, :] = (q32 * f_mid).astype(BF16)
            pf_edge[rows, :] = (q32 * f_edge).astype(BF16)
            gf_mid[rows, :] = (g32 * f_mid).astype(BF16)
            gf_edge[rows, :] = (g32 * f_edge).astype(BF16)
            for j in range(3):
                at = j * ROW + start
                value = pushed_in[y, rows, j * width : j * width + width] - lanes(delta, width)
                value = em[y, rows, at : at + width].astype(F32) * value
                slopes[rows, at : at + width] = value.astype(BF16)
            for z, j, count in outer:
                pushed = dot(g, take(vz, (z,), y + j, count, start, width), NT)
                pushed = pushed - lanes(delta, count * width)
                for n in range(count):
                    at = (3 * z + j + n) * ROW + start
                    value = ee[rows, at : at + width].astype(F32)
                    value = value * pushed[:, n * width : n * width + width]
                    slopes[rows, 768 + at : 768 + at + width] = value.astype(BF16)
            wide = dot(slopes[rows, 768:1536], window(pz, y, (0,)))
            wide = wide + dot(slopes[rows, 1536:2304], window(pz, y, (1,)))
            wide = wide * f_edge + dot(slopes[rows, 0:768], window(pm, y)) * f_mid
            qg[y, here, :] = (collect(wide, mask) * 0.125).astype(BF16)
        for j in range(3):
            cols = slice(j * ROW, j * ROW + ROW)
            kg[0, y + j] += dot(slopes[:, cols], pf_mid[...], TN)
            vg[0, y + j] += dot(em[y, :, cols], gf_mid[...], TN)
            for z in range(2):
                at = (3 * z + j) * ROW
                kg[1 + z, y + j] += dot(slopes[:, 768 + at : 1024 + at], pf_edge[...], TN)
                vg[1 + z, y + j] += dot(ee[:, at : at + ROW], gf_edge[...], TN)
        return carry

    lax.fori_loop(0, 2, step, 0)
    gp = dot(xs[0], qg[0], TN) + dot(xs[1], qg[1], TN)
    gv = jnp.zeros((D, D), F32)
    for z, out in enumerate((back_mid, back_low, back_high)):
        for r in range(4):
            x = xm[r] if z == 0 else xz[z - 1, r]
            k = kg[z, r].astype(BF16)
            v = vg[z, r].astype(BF16)
            out[r] = (dot(k, wp[...], NT) + dot(v, wv[...], NT)).astype(BF16)
            gp = gp + dot(x, k, TN)
            gv = gv + dot(x, v, TN)
    part[:, 0:256] = gp.astype(BF16)
    part[:, 256:512] = gv.astype(BF16)
    gout = dot(att[0], cs[0], TN) + dot(att[1], cs[1], TN)
    part[:, 512:768] = gout.astype(BF16)


def finish_kernel(att, qg, wp, wo, summed, from_low, from_high, mixed, grad):
    back = from_blocks_matrix()
    for y, side in enumerate((from_low, from_high)):
        out = dot(att[y], wo[...]).astype(BF16)
        mixed[:, 4 * y : 4 * y + 4] = dot(back, out).astype(BF16).reshape(4, 4, 16, D)
        out = dot(qg[y], wp[...], NT)
        out = (out + summed[y] + side[...].astype(F32)).astype(BF16)
        grad[:, 4 * y : 4 * y + 4] = dot(back, out).astype(BF16).reshape(4, 4, 16, D)


def call(body, outs, scratch=(), flops=0, name=None, limit=16):
    return pl.pallas_call(
        body,
        out_shape=tuple(jax.ShapeDtypeStruct(shape, dtype) for shape, dtype in outs),
        scratch_shapes=list(scratch),
        compiler_params=pltpu.CompilerParams(vmem_limit_bytes=limit * 1024 * 1024),
        cost_estimate=pl.CostEstimate(flops=flops, bytes_accessed=4 * 1024 * 1024, transcendentals=0),
        name=name,
    )


def shift(block, other, dz, dy):
    scans, depth, height = (lax.axis_size(axis) for axis in AXES)
    route = []
    for s in range(scans):
        for z in range(depth):
            for y in range(height):
                if 0 <= z + dz < depth and 0 <= y + dy < height:
                    target = s ^ other
                    route.append(
                        (
                            (s * depth + z) * height + y,
                            (target * depth + z + dz) * height + y + dy,
                        )
                    )
    return lax.ppermute(block, AXES, route)


def window_bias(flags):
    side = lax.axis_index("scan")
    plane = lax.axis_index("gz")
    row = lax.axis_index("gy") * 2
    near = jnp.pad(flags, ((0, 0), (1, 1), (1, 1), (0, 0)))
    near_other = lax.dynamic_slice(near, (1 - side, plane, row, 0), (1, 3, 4, 4))[0]

    def nine(near):
        return jnp.stack(
            [jnp.concatenate([near[z, y : y + 3] for z in (1, 0, 2)]) for y in range(2)]
        )

    xs = np.arange(4)
    adjacent = np.abs(xs[:, None] - xs[None, :]) <= 1
    center = np.zeros((2, 4, 9, 4), bool)
    for x in range(4):
        center[:, x, 1, x] = True
    adjacent = adjacent[None, :, None, :]
    valid = adjacent & ((nine(near_other)[:, None] > 0) | center)
    bias = jnp.where(valid, 0.0, NEG).astype(F32)
    a = jnp.stack([bias[:, 0, :, 0:2], bias[:, 3, :, 2:4]], axis=1)
    b = bias[:, 1:3]
    return (
        jnp.repeat(a.reshape(4, 1, 18), CUBE, axis=2),
        jnp.repeat(b.reshape(4, 1, 36), CUBE, axis=2),
    )


def chip_half(part):
    half = part.shape[0] // 2
    side = lax.axis_index("scan")
    mine = lax.dynamic_slice_in_dim(part, side * half, half, 0)
    other = lax.dynamic_slice_in_dim(part, (1 - side) * half, half, 0)
    return (mine.astype(F32) + shift(other, 1, 0, 0).astype(F32)).astype(BF16)


def summed_share(mine):
    places = lax.axis_size("gz") * lax.axis_size("gy")
    got = lax.all_to_all(mine.reshape(places, 2, -1), ("gz", "gy"), 0, 0)
    return jnp.sum(got.astype(F32), axis=0).astype(BF16)


def all_shares(total):
    places = lax.axis_size("gz") * lax.axis_size("gy")
    return lax.all_to_all(
        jnp.broadcast_to(total[None], (places,) + total.shape), ("gz", "gy"), 0, 0
    )


def both_halves(full, half):
    side = lax.axis_index("scan")
    away = shift(full, 1, 0, 0)
    first = jnp.where(side == 0, full, away)
    second = jnp.where(side == 0, away, full)
    return jnp.concatenate([first, second], axis=0).reshape(2 * half, -1).astype(F32)


def after(value, token):
    return lax.optimization_barrier((value, token))[0]


def on_device(scans, proj_weight, value_weight, out_weight, flags, cotangent):
    own = scans[0]
    cot = cotangent[0]
    wide = (ROW, D)
    columns = ((2, 4 * ROW, 128), F32)
    unit = 2 * ROW * ROW * D

    slab = jnp.concatenate(
        [shift(own[:, 4:], 1, 0, 1), shift(own, 1, 0, 0), shift(own[:, :4], 1, 0, -1)], axis=1
    )
    low_z = shift(slab, 0, 1, 0)
    high_z = shift(slab, 0, -1, 0)
    bias = window_bias(flags)
    xs, cs, p0, g0, wp, wv, wo = call(
        own_kernel, [((2,) + wide, BF16)] * 4 + [(wide, BF16)] * 3, flops=10 * unit, name="own"
    )(own, cot, proj_weight, value_weight, out_weight)
    xm, pm, vm, em, pushed, a1, top, total = call(
        mid_kernel,
        [((4,) + wide, BF16)] * 3
        + [((2, 4 * ROW, 3 * ROW), BF16), ((2, 4 * ROW, 3 * ROW), F32)]
        + [((2,) + wide, F32), columns, columns],
        [pltpu.VMEM((4, ROW, 3 * ROW), F32)],
        flops=200 * unit,
        name="mid",
    )(slab, wp, wv, p0, g0, *bias)
    back_mid, back_low, back_high, att, qg, part = call(
        main_kernel,
        [((4,) + wide, BF16)] * 3 + [((2,) + wide, BF16)] * 2 + [((ROW, 3 * D), BF16)],
        [pltpu.VMEM((2, 4) + wide, BF16)] * 3
        + [
            pltpu.VMEM((4, ROW, 6 * ROW), F32),
            pltpu.VMEM((4 * ROW, 6 * ROW), BF16),
            pltpu.VMEM((4 * ROW, 9 * ROW), BF16),
        ]
        + [pltpu.VMEM((4 * ROW, D), BF16)] * 4
        + [pltpu.VMEM((3, 4) + wide, F32)] * 2,
        flops=900 * unit,
        name="main",
        limit=32,
    )(low_z, high_z, wp, wv, p0, g0, xs, cs, *bias, xm, pm, vm, em, pushed, a1, top, total)

    mine = chip_half(part)
    got = (
        shift(back_low, 1, -1, 0).astype(F32)
        + shift(back_mid, 1, 0, 0).astype(F32)
        + shift(back_high, 1, 1, 0).astype(F32)
    )
    to_low = got[0].astype(BF16)
    to_high = got[3].astype(BF16)
    share = after(summed_share(mine), (to_low, to_high))
    from_high = shift(to_low, 0, 0, -1)
    from_low = shift(to_high, 0, 0, 1)
    shares = all_shares(share)
    mixed, grad = call(finish_kernel, [(own.shape, BF16)] * 2, flops=10 * unit, name="finish")(
        att, qg, wp, wo, got[1:3], from_low, from_high
    )
    sums = both_halves(after(shares, grad), part.shape[0] // 2)
    return (
        mixed[None],
        grad[None],
        sums[:, 0:256],
        sums[:, 256:512],
        sums[:, 512:768],
    )


def solution(mesh):
    field = P("scan", "gz", "gy", None, None)
    return jax.shard_map(
        on_device,
        mesh=mesh,
        in_specs=(field, P(), P(), P(), P(), field),
        out_specs=(field, field, P(), P(), P()),
        check_vma=False,
    )
```

time: 126 us -> 127 us (level)
  waiting for transfers between devices: 19.4 us -> 28.6 us
  starting transfers between devices: 59.4 us -> 52.6 us
  local copies, waits for them, and re-layouts: 11.9 us -> 10.4 us
  other arithmetic: 5.37 us -> 3.96 us
  Pallas kernels: 28.1 us -> 29.4 us
    ppermute x14 -> x12, waiting for transfers between devices: 8.84 us -> 18 us  [shift(): return lax.ppermute(block, AXES, route)]
    ppermute x14 -> x12, starting transfers between devices: 35.4 us -> 28.7 us  [shift(): return lax.ppermute(block, AXES, route)]
    unnamed x23 -> x13, local copies, waits for them, and re-layouts: 7.29 us -> 4.69 us
    broadcast_in_dim x1 -> x0, other arithmetic: 1.8 us -> none  [all_shares(): jnp.broadcast_to(total[None], (places,) + total.shape)]
    convert_element_type x1 -> x2, other arithmetic: 0.05 us -> 1.4 us  [the longest x1 0.97 us: chip_half(): return (mine.astype(F32) + shift(other, 1, 0, 0).astype(F32)).astype(BF16)]
    pallas_call x4, Pallas kernels: 28.1 us -> 29.4 us  [the longest x1 22.9 us: on_device(): call(main_kernel, [((4,) + wide, BF16)] * 3 + [((2,) + wide, BF16)] * 2 +...]
  transfers between devices with their start and end apart: 16 -> 14, of which waited for: 6 -> 7; matrix products, arithmetic and copies ran while one was open for 6% -> 6% of each run, Pallas kernels for 6% -> 5%
where the time goes in v4:
time: 127 us; the launch traced here: 126 us
  starting transfers between devices  52.6 us (41%)
  Pallas kernels  29.4 us (23%)
  waiting for transfers between devices  28.6 us (23%)
  local copies, waits for them, and re-layouts  10.4 us (8%)
  other arithmetic  3.96 us (3%)
    ppermute x12, starting transfers between devices, shift(): return lax.ppermute(block, AXES, route)  28.7 us
    pallas_call x1, Pallas kernels, on_device(): call(main_kernel, [((4,) + wide, BF16)] * 3 + [((2,) + wide, BF16)] * 2 +...  22.9 us
    ppermute x12, waiting for transfers between devices, shift(): return lax.ppermute(block, AXES, route)  18 us
    all_to_all x1, starting transfers between devices, summed_share(): got = lax.all_to_all(mine.reshape(places, 2, -1), ('gz', 'gy'), 0, 0)  17 us
    all_to_all x1, waiting for transfers between devices, summed_share(): got = lax.all_to_all(mine.reshape(places, 2, -1), ('gz', 'gy'), 0, 0)  10.5 us
    all_to_all x1, starting transfers between devices, all_shares(): lax.all_to_all(jnp.broadcast_to(total[None], (places,) + total.shape), ('...  6.82 us
    unnamed x13, local copies, waits for them, and re-layouts  4.69 us
    pallas_call x1, Pallas kernels, on_device(): call(mid_kernel, [((4,) + wide, BF16)] * 3 + [((2, 4 * ROW, 3 * ROW), BF1...  4.57 us
  transfers between devices with their start and end apart: 14, of which 7 were waited for; matrix products, arithmetic and copies ran while one was open for 6% of the time, Pallas kernels for 5%

profile of v4, /device:TPU:1, one launch (start us, length us, event | category | flops | bytes accessed | tf_op | source)
XLA Modules:
  0.0 125.9 jit_solution(1613231609576057065)
XLA Ops:
  0.6 3.3 %collective-permute-start.1 = (bf16[4,8,16,256]{3,2,1,0:T(8,128)(2,1)}, bf16[4,8,16,256]{3,2,1,0:T(8,128)(2,1)S(1)}, u32[]{:S(2)}, u32[]{:S(2)}) collective-permute-start(bf16[4,8,16,256]{3,2,1,0:T(8,128)(2,1)} %bitcast.31), channel_id=1, source_target_pairs={{0,128},{1,129},{2,130},{3,131},{4,132},{5,133},{6,134},{7,135},{8... | collective-permute-start | bytes 786440 | tf_op jit(solution)/shard_map/ppermute | solution.py:333
  4.9 3.0 %collective-permute-start = (bf16[4,4,16,256]{3,2,1,0:T(8,128)(2,1)S(1)}, bf16[4,4,16,256]{3,2,1,0:T(8,128)(2,1)S(1)}, u32[]{:S(2)}, u32[]{:S(2)}) collective-permute-start(bf16[4,4,16,256]{3,2,1,0:T(8,128)(2,1)S(1)} %get-tuple-element.65), channel_id=1, source_target_pairs={{0,129},{1,130},{2,131},{3,132},{4,133},{5,134},{6,135},{8,137},{9... | collective-permute-start | bytes 393224 | tf_op jit(solution)/shard_map/ppermute | solution.py:333
  8.0 1.3 %collective-permute-start.2 = (bf16[4,4,16,256]{3,2,1,0:T(8,128)(2,1)S(1)}, bf16[4,4,16,256]{3,2,1,0:T(8,128)(2,1)S(1)}, u32[]{:S(2)}, u32[]{:S(2)}) collective-permute-start(bf16[4,4,16,256]{3,2,1,0:T(8,128)(2,1)S(1)} %get-tuple-element.64), channel_id=1, source_target_pairs={{1,128},{2,129},{3,130},{4,131},{5,132},{6,133},{7,134},{9,136},{1... | collective-permute-start | bytes 393224 | tf_op jit(solution)/shard_map/ppermute | solution.py:333
  17.7 3.6 %collective-permute-start.3 = (bf16[4,16,16,256]{3,2,1,0:T(8,128)(2,1)S(1)}, bf16[4,16,16,256]{3,2,1,0:T(8,128)(2,1)S(1)}, u32[]{:S(2)}, u32[]{:S(2)}) collective-permute-start(bf16[4,16,16,256]{3,2,1,0:T(8,128)(2,1)S(1)} %constant_dynamic-update-slice_fusion.slab), channel_id=1, source_target_pairs={{0,8},{1,9},{2,10},{3,11},{4,12},{5,13},{6,14},{7,15},{8,16},{9,17... | collective-permute-start | bytes 1572872 | tf_op jit(solution)/shard_map/ppermute | solution.py:333
  21.3 1.3 %collective-permute-start.4 = (bf16[4,16,16,256]{3,2,1,0:T(8,128)(2,1)S(1)}, bf16[4,16,16,256]{3,2,1,0:T(8,128)(2,1)S(1)}, u32[]{:S(2)}, u32[]{:S(2)}) collective-permute-start(bf16[4,16,16,256]{3,2,1,0:T(8,128)(2,1)S(1)} %constant_dynamic-update-slice_fusion.slab), channel_id=1, source_target_pairs={{8,0},{9,1},{10,2},{11,3},{12,4},{13,5},{14,6},{15,7},{16,8},{17,9... | collective-permute-start | bytes 1572872 | tf_op jit(solution)/shard_map/ppermute | solution.py:333
  22.6 4.6 %mid.1 = (bf16[4,256,256]{2,1,0:T(8,128)(2,1)S(1)}, bf16[4,256,256]{2,1,0:T(8,128)(2,1)S(1)}, bf16[4,256,256]{2,1,0:T(8,128)(2,1)S(1)}, bf16[2,1024,768]{2,1,0:T...) custom-call(bf16[4,16,16,256]{3,2,1,0:T(8,128)(2,1)S(1)} %constant_d, ...), custom_call_target="tpu_custom_call" | custom-call | flops 6710886400 | bytes 4194304 | tf_op jit(solution)/shard_map/mid/pallas_call | solution.py:413
  27.1 4.9 %collective-permute-done.3.low_z = bf16[4,16,16,256]{3,2,1,0:T(8,128)(2,1)S(1)} collective-permute-done((bf16[4,16,16,256]{3,2,1,0:T(8,128)(2,1)S(1)}, bf16[4,16,16,256]{3,2,1,0:T(8,128)(2,1)S(1)}, u32[]{:S(2)}, u32[]{:S(2)}) %collective-permute-start.3) | collective-permute-done | bytes 524320 | tf_op jit(solution)/shard_map/ppermute | solution.py:333
  32.0 4.2 %collective-permute-done.4.high_z = bf16[4,16,16,256]{3,2,1,0:T(8,128)(2,1)S(1)} collective-permute-done((bf16[4,16,16,256]{3,2,1,0:T(8,128)(2,1)S(1)}, bf16[4,16,16,256]{3,2,1,0:T(8,128)(2,1)S(1)}, u32[]{:S(2)}, u32[]{:S(2)}) %collective-permute-start.4) | collective-permute-done | bytes 524320 | tf_op jit(solution)/shard_map/ppermute | solution.py:333
  36.2 22.9 %main.1 = (bf16[4,256,256]{2,1,0:T(8,128)(2,1)S(1)}, bf16[4,256,256]{2,1,0:T(8,128)(2,1)S(1)}, bf16[4,256,256]{2,1,0:T(8,128)(2,1)S(1)}, bf16[2,256,256]{2,1,0:T...) custom-call(bf16[4,16,16,256]{3,2,1,0:T(8,128)(2,1)S(1)} %collective-permute-done.3.low_z, ...), custom_call_target="tpu_custom_call" | custom-call | flops 30198988800 | bytes 4194304 | tf_op jit(solution)/shard_map/main/pallas_call | solution.py:422
  59.2 1.3 %collective-permute-start.5 = (bf16[4,256,256]{2,1,0:T(8,128)(2,1)S(1)}, bf16[4,256,256]{2,1,0:T(8,128)(2,1)S(1)}, u32[]{:S(2)}, u32[]{:S(2)}) collective-permute-start(bf16[4,256,256]{2,1,0:T(8,128)(2,1)S(1)} %get-tuple-element.47), channel_id=1, source_target_pairs={{8,128},{9,129},{10,130},{11,131},{12,132},{13,133},{14,134},{15,1... | collective-permute-start | bytes 1572872 | tf_op jit(solution)/shard_map/ppermute | solution.py:333
  60.5 1.6 %collective-permute-start.6 = (bf16[4,256,256]{2,1,0:T(8,128)(2,1)S(1)}, bf16[4,256,256]{2,1,0:T(8,128)(2,1)}, u32[]{:S(2)}, u32[]{:S(2)}) collective-permute-start(bf16[4,256,256]{2,1,0:T(8,128)(2,1)S(1)} %get-tuple-element.48), channel_id=1, source_target_pairs={{0,128},{1,129},{2,130},{3,131},{4,132},{5,133},{6,134},{7,135},{8... | collective-permute-start | bytes 1572872 | tf_op jit(solution)/shard_map/ppermute | solution.py:333
  62.0 5.1 %collective-permute-start.7 = (bf16[4,256,256]{2,1,0:T(8,128)(2,1)S(1)}, bf16[4,256,256]{2,1,0:T(8,128)(2,1)}, u32[]{:S(2)}, u32[]{:S(2)}) collective-permute-start(bf16[4,256,256]{2,1,0:T(8,128)(2,1)S(1)} %get-tuple-element.49), channel_id=1, source_target_pairs={{0,136},{1,137},{2,138},{3,139},{4,140},{5,141},{6,142},{7,143},{8... | collective-permute-start | bytes 1572872 | tf_op jit(solution)/shard_map/ppermute | solution.py:333
  67.5 1.3 %collective-permute-done.10 = bf16[128,768]{1,0:T(8,128)(2,1)} collective-permute-done((bf16[128,768]{1,0:T(8,128)(2,1)S(1)}, bf16[128,768]{1,0:T(8,128)(2,1)}, u32[]{:S(2)}, u32[]{:S(2)}) %collective-permute-start.10) | collective-permute-done | bytes 196640 | tf_op jit(solution)/shard_map/ppermute | solution.py:333
  70.5 17.0 %all-to-all-start = ((bf16[128,2,384]{2,1,0:T(2,128)(2,1)}), bf16[128,2,384]{2,1,0:T(2,128)(2,1)S(1)}, u32[]{:S(2)}, u32[]{:S(2)}) async-start(bf16[128,2,384]{2,1,0:T(2,128)(2,1)} %reshape.57), calls=%async_computation | async-start | bytes 393216 | tf_op jit(solution)/shard_map/all_to_all | solution.py:374
  87.6 1.4 %fusion = (bf16[4,256,256]{2,1,0:T(8,128)(2,1)S(1)}, f32[4,256,256]{2,1,0:T(8,128)S(1)}) fusion(bf16[4,256,256]{2,1,0:T(8,128)(2,1)} %collective-permute-done.7, bf16[4,256,256]{2,1,0:T(8,128)(2,1)} %collective-permute-done.6, bf16[4,256,256]{2,1,0:T(8,128)(2,1)S(1)} %collective-permute-done.5), kind=kLoop, calls=%fused_computation.23 | loop fusion | flops 1572864 | bytes 3145728 | tf_op jit(solution)/shard_map/convert.3
  89.0 10.5 %all-to-all-done = bf16[128,2,384]{2,1,0:T(2,128)(2,1)S(1)} async-done(((bf16[128,2,384]{2,1,0:T(2,128)(2,1)}), bf16[128,2,384]{2,1,0:T(2,128)(2,1)S(1)}, u32[]{:S(2)}, u32[]{:S(2)}) %all-to-all-start) | async-done | bytes 196640 | tf_op jit(solution)/shard_map/all_to_all | solution.py:374
  100.6 6.8 %all-to-all-start.1 = ((bf16[128,2,384]{2,1,0:T(2,128)(2,1)}), bf16[128,2,384]{2,1,0:T(2,128)(2,1)S(1)}, u32[]{:S(2)}, u32[]{:S(2)}) async-start(bf16[128,2,384]{2,1,0:T(2,128)(2,1)} %broadcast_in_dim.39), calls=%async_computation.1 | async-start | bytes 393216 | tf_op jit(solution)/shard_map/all_to_all | solution.py:380
  107.4 4.0 %collective-permute-start.8 = (bf16[256,256]{1,0:T(8,128)(2,1)S(1)}, bf16[256,256]{1,0:T(8,128)(2,1)S(1)}, u32[]{:S(2)}, u32[]{:S(2)}) collective-permute-start(bf16[256,256]{1,0:T(8,128)(2,1)S(1)} %get-tuple-element.61), channel_id=1, source_target_pairs={{0,1},{1,2},{2,3},{3,4},{4,5},{5,6},{6,7},{8,9},{9,10},{10,11},{11... | collective-permute-start | bytes 393224 | tf_op jit(solution)/shard_map/ppermute | solution.py:333
  111.4 1.3 %collective-permute-start.9 = (bf16[256,256]{1,0:T(8,128)(2,1)S(1)}, bf16[256,256]{1,0:T(8,128)(2,1)S(1)}, u32[]{:S(2)}, u32[]{:S(2)}) collective-permute-start(bf16[256,256]{1,0:T(8,128)(2,1)S(1)} %get-tuple-element.60), channel_id=1, source_target_pairs={{1,0},{2,1},{3,2},{4,3},{5,4},{6,5},{7,6},{9,8},{10,9},{11,10},{12... | collective-permute-start | bytes 393224 | tf_op jit(solution)/shard_map/ppermute | solution.py:333
  112.7 1.1 collective-permute-done.8.from_low
  113.8 5.5 %collective-permute-done.9.from_high = bf16[256,256]{1,0:T(8,128)(2,1)S(1)} collective-permute-done((bf16[256,256]{1,0:T(8,128)(2,1)S(1)}, bf16[256,256]{1,0:T(8,128)(2,1)S(1)}, u32[]{:S(2)}, u32[]{:S(2)}) %collective-permute-start.9) | collective-permute-done | bytes 131104 | tf_op jit(solution)/shard_map/ppermute | solution.py:333
  119.3 1.3 %finish.1 = (bf16[4,8,16,256]{3,2,1,0:T(8,128)(2,1)}, bf16[4,8,16,256]{3,2,1,0:T(8,128)(2,1)}) custom-call(bf16[2,256,256]{2,1,0:T(8,128)(2,1)S(1)} %get-tuple-element.44.att, bf16[2,256,256]{2,1,0:T(8,128)(2,1)S(1)} %get-tuple-element.45.qg, bf16[256,256]{1,0:T(8,128)(2,1)S(1)} %get-tuple-element.30.wp, bf16[256,256]{1,0:T(8,128)(2,1)S(1)} %get-tuple-element.46.wo, ...), custom_call_target="tpu_custom_call" | custom-call | flops 335544320 | bytes 4194304 | tf_op jit(solution)/shard_map/finish/pallas_call | solution.py:450
  120.7 2.7 %collective-permute-start.11 = (bf16[128,2,384]{2,1,0:T(2,128)(2,1)S(1)}, bf16[128,2,384]{2,1,0:T(2,128)(2,1)S(1)}, u32[]{:S(2)}, u32[]{:S(2)}) collective-permute-start(bf16[128,2,384]{2,1,0:T(2,128)(2,1)S(1)} %all-to-all-done.1), channel_id=1, source_target_pairs={{0,128},{1,129},{2,130},{3,131},{4,132},{5,133},{6,134},{7,135},{8... | collective-permute-start | bytes 589832 | tf_op jit(solution)/shard_map/ppermute | solution.py:333
  123.3 1.1 collective-permute-done.11
  (57 shorter events, 13.9 us)
Async XLA Ops:
  0.6 17.0 %collective-permute-start.1 = (bf16[4,8,16,256]{3,2,1,0:T(8,128)(2,1)}, bf16[4,8,16,256]{3,2,1,0:T(8,128)(2,1)S(1)}, u32[]{:S(2)}, u32[]{:S(2)}) collective-permute-start(bf16[4,8,16,256]{3,2,1,0:T(8,128)(2,1)} %bitcast.31), channel_id=1, source_target_pairs={{0,128},{1,129},{2,130},{3,131},{4,132},{5,133},{6,134},{7,135},{8... | collective-permute-start | bytes 786440 | tf_op jit(solution)/shard_map/ppermute | solution.py:333
  4.9 12.6 %collective-permute-start = (bf16[4,4,16,256]{3,2,1,0:T(8,128)(2,1)S(1)}, bf16[4,4,16,256]{3,2,1,0:T(8,128)(2,1)S(1)}, u32[]{:S(2)}, u32[]{:S(2)}) collective-permute-start(bf16[4,4,16,256]{3,2,1,0:T(8,128)(2,1)S(1)} %get-tuple-element.65), channel_id=1, source_target_pairs={{0,129},{1,130},{2,131},{3,132},{4,133},{5,134},{6,135},{8,137},{9... | collective-permute-start | bytes 393224 | tf_op jit(solution)/shard_map/ppermute | solution.py:333
  8.0 9.7 %collective-permute-start.2 = (bf16[4,4,16,256]{3,2,1,0:T(8,128)(2,1)S(1)}, bf16[4,4,16,256]{3,2,1,0:T(8,128)(2,1)S(1)}, u32[]{:S(2)}, u32[]{:S(2)}) collective-permute-start(bf16[4,4,16,256]{3,2,1,0:T(8,128)(2,1)S(1)} %get-tuple-element.64), channel_id=1, source_target_pairs={{1,128},{2,129},{3,130},{4,131},{5,132},{6,133},{7,134},{9,136},{1... | collective-permute-start | bytes 393224 | tf_op jit(solution)/shard_map/ppermute | solution.py:333
  12.4 1.0 copy-start
  13.3 0.9 copy-start.1
  14.3 0.9 copy-start.2
  15.2 0.9 copy-start.3
  16.1 0.9 copy-start.4
  17.7 14.3 %collective-permute-start.3 = (bf16[4,16,16,256]{3,2,1,0:T(8,128)(2,1)S(1)}, bf16[4,16,16,256]{3,2,1,0:T(8,128)(2,1)S(1)}, u32[]{:S(2)}, u32[]{:S(2)}) collective-permute-start(bf16[4,16,16,256]{3,2,1,0:T(8,128)(2,1)S(1)} %constant_dynamic-update-slice_fusion.slab), channel_id=1, source_target_pairs={{0,8},{1,9},{2,10},{3,11},{4,12},{5,13},{6,14},{7,15},{8,16},{9,17... | collective-permute-start | bytes 1572872 | tf_op jit(solution)/shard_map/ppermute | solution.py:333
  21.3 14.9 %collective-permute-start.4 = (bf16[4,16,16,256]{3,2,1,0:T(8,128)(2,1)S(1)}, bf16[4,16,16,256]{3,2,1,0:T(8,128)(2,1)S(1)}, u32[]{:S(2)}, u32[]{:S(2)}) collective-permute-start(bf16[4,16,16,256]{3,2,1,0:T(8,128)(2,1)S(1)} %constant_dynamic-update-slice_fusion.slab), channel_id=1, source_target_pairs={{8,0},{9,1},{10,2},{11,3},{12,4},{13,5},{14,6},{15,7},{16,8},{17,9... | collective-permute-start | bytes 1572872 | tf_op jit(solution)/shard_map/ppermute | solution.py:333
  59.2 28.4 %collective-permute-start.5 = (bf16[4,256,256]{2,1,0:T(8,128)(2,1)S(1)}, bf16[4,256,256]{2,1,0:T(8,128)(2,1)S(1)}, u32[]{:S(2)}, u32[]{:S(2)}) collective-permute-start(bf16[4,256,256]{2,1,0:T(8,128)(2,1)S(1)} %get-tuple-element.47), channel_id=1, source_target_pairs={{8,128},{9,129},{10,130},{11,131},{12,132},{13,133},{14,134},{15,1... | collective-permute-start | bytes 1572872 | tf_op jit(solution)/shard_map/ppermute | solution.py:333
  60.5 27.1 %collective-permute-start.6 = (bf16[4,256,256]{2,1,0:T(8,128)(2,1)S(1)}, bf16[4,256,256]{2,1,0:T(8,128)(2,1)}, u32[]{:S(2)}, u32[]{:S(2)}) collective-permute-start(bf16[4,256,256]{2,1,0:T(8,128)(2,1)S(1)} %get-tuple-element.48), channel_id=1, source_target_pairs={{0,128},{1,129},{2,130},{3,131},{4,132},{5,133},{6,134},{7,135},{8... | collective-permute-start | bytes 1572872 | tf_op jit(solution)/shard_map/ppermute | solution.py:333
  62.0 25.5 %collective-permute-start.7 = (bf16[4,256,256]{2,1,0:T(8,128)(2,1)S(1)}, bf16[4,256,256]{2,1,0:T(8,128)(2,1)}, u32[]{:S(2)}, u32[]{:S(2)}) collective-permute-start(bf16[4,256,256]{2,1,0:T(8,128)(2,1)S(1)} %get-tuple-element.49), channel_id=1, source_target_pairs={{0,136},{1,137},{2,138},{3,139},{4,140},{5,141},{6,142},{7,143},{8... | collective-permute-start | bytes 1572872 | tf_op jit(solution)/shard_map/ppermute | solution.py:333
  67.1 1.7 %collective-permute-start.10 = (bf16[128,768]{1,0:T(8,128)(2,1)S(1)}, bf16[128,768]{1,0:T(8,128)(2,1)}, u32[]{:S(2)}, u32[]{:S(2)}) collective-permute-start(bf16[128,768]{1,0:T(8,128)(2,1)S(1)} %constant_dynamic-slice_fusion), channel_id=1, source_target_pairs={{0,128},{1,129},{2,130},{3,131},{4,132},{5,133},{6,134},{7,135},{8... | collective-permute-start | bytes 589832 | tf_op jit(solution)/shard_map/ppermute | solution.py:333
  70.5 29.1 %all-to-all-start = ((bf16[128,2,384]{2,1,0:T(2,128)(2,1)}), bf16[128,2,384]{2,1,0:T(2,128)(2,1)S(1)}, u32[]{:S(2)}, u32[]{:S(2)}) async-start(bf16[128,2,384]{2,1,0:T(2,128)(2,1)} %reshape.57), calls=%async_computation | async-start | bytes 393216 | tf_op jit(solution)/shard_map/all_to_all | solution.py:374
  100.6 20.1 %all-to-all-start.1 = ((bf16[128,2,384]{2,1,0:T(2,128)(2,1)}), bf16[128,2,384]{2,1,0:T(2,128)(2,1)S(1)}, u32[]{:S(2)}, u32[]{:S(2)}) async-start(bf16[128,2,384]{2,1,0:T(2,128)(2,1)} %broadcast_in_dim.39), calls=%async_computation.1 | async-start | bytes 393216 | tf_op jit(solution)/shard_map/all_to_all | solution.py:380
  107.4 6.4 %collective-permute-start.8 = (bf16[256,256]{1,0:T(8,128)(2,1)S(1)}, bf16[256,256]{1,0:T(8,128)(2,1)S(1)}, u32[]{:S(2)}, u32[]{:S(2)}) collective-permute-start(bf16[256,256]{1,0:T(8,128)(2,1)S(1)} %get-tuple-element.61), channel_id=1, source_target_pairs={{0,1},{1,2},{2,3},{3,4},{4,5},{5,6},{6,7},{8,9},{9,10},{10,11},{11... | collective-permute-start | bytes 393224 | tf_op jit(solution)/shard_map/ppermute | solution.py:333
  111.4 8.0 %collective-permute-start.9 = (bf16[256,256]{1,0:T(8,128)(2,1)S(1)}, bf16[256,256]{1,0:T(8,128)(2,1)S(1)}, u32[]{:S(2)}, u32[]{:S(2)}) collective-permute-start(bf16[256,256]{1,0:T(8,128)(2,1)S(1)} %get-tuple-element.60), channel_id=1, source_target_pairs={{1,0},{2,1},{3,2},{4,3},{5,4},{6,5},{7,6},{9,8},{10,9},{11,10},{12... | collective-permute-start | bytes 393224 | tf_op jit(solution)/shard_map/ppermute | solution.py:333
  120.7 3.7 %collective-permute-start.11 = (bf16[128,2,384]{2,1,0:T(2,128)(2,1)S(1)}, bf16[128,2,384]{2,1,0:T(2,128)(2,1)S(1)}, u32[]{:S(2)}, u32[]{:S(2)}) collective-permute-start(bf16[128,2,384]{2,1,0:T(2,128)(2,1)S(1)} %all-to-all-done.1), channel_id=1, source_target_pairs={{0,128},{1,129},{2,130},{3,131},{4,132},{5,133},{6,134},{7,135},{8... | collective-permute-start | bytes 589832 | tf_op jit(solution)/shard_map/ppermute | solution.py:333

commit v5 on v4

--- a/solution.py
+++ b/solution.py
@@ -60,47 +60,37 @@
     return (kept[0:64] + kept[64:128]) + (kept[128:192] + kept[192:256])
 
 
-def chunks(rows, width):
-    if width == ROW:
-        return [(j, 1) for j in range(rows)]
-    return [(j, min(2, rows - j)) for j in range(0, rows, 2)]
-
-
-def take(ref, lead, j, count, start, width):
-    return ref[(*lead, pl.ds(j, count), pl.ds(start, width))].reshape(count * width, D)
-
-
-def span(x):
-    return {0: (0, 128), 1: (0, 256), 2: (0, 256), 3: (128, 128)}[x]
+HALVES = ((0,), (0, 1), (0, 1), (1,))
+UNITS = [(x, half) for x in range(4) for half in HALVES[x]]
+
+
+def pairs(x, rows):
+    pieces = [(half, n) for half in HALVES[x] for n in range(rows)]
+    return [pieces[k : k + 2] for k in range(0, len(pieces), 2)]
+
+
+def place(n):
+    return slice(n * 128, n * 128 + 128)
+
+
+def gathered(ref, y, pieces):
+    parts = []
+    for half, n in pieces:
+        lead = () if len(ref.shape) == 3 else (n // 3,)
+        parts.append(ref[(*lead, y + n % 3, place(half), slice(None))])
+    return parts[0] if len(parts) == 1 else jnp.concatenate(parts, axis=0)
+
+
+def half_window(ref, y, half, lead=()):
+    return ref[(*lead, pl.ds(y, 3), place(half), slice(None))].reshape(384, D)
 
 
 def own_rows(ref, y, x):
     return ref[y, CUBE * x : CUBE * x + CUBE, :]
 
 
-def bias_of(bias_a, bias_b, y, x, cols):
-    return bias_b[2 * y + x - 1, :, cols] if x in (1, 2) else bias_a[2 * y + x // 3, :, cols]
-
-
-def store(ref, lead, rows, j, count, x, value):
-    start, width = span(x)
-    for n in range(count):
-        at = (j + n) * ROW + start
-        ref[(*lead, rows, slice(at, at + width))] = value[:, n * width : n * width + width]
-
-
-def lane_max(s):
-    out = s[:, 0:128]
-    for k in range(128, s.shape[1], 128):
-        out = jnp.maximum(out, s[:, k : k + 128])
-    return out
-
-
-def lane_sum(s):
-    out = s[:, 0:128]
-    for k in range(128, s.shape[1], 128):
-        out = out + s[:, k : k + 128]
-    return out
+def members(half):
+    return slice(0, 768) if half == 0 else slice(256, 1024)
 
 
 def lanes(column, width):
@@ -142,16 +132,12 @@
         vs[(*lead, r)] = dot(x, wv[...]).astype(BF16)
 
 
-def window(ref, y, lead=()):
-    return ref[(*lead, pl.ds(y, 3))].reshape(3 * ROW, D)
-
-
 def larger(a, b):
     return b if a is None else jnp.maximum(a, b)
 
 
 def mid_kernel(
-    slab, wp, wv, p0, g0, bias_a, bias_b, xm, pm, vm, em, pushed, a1, top_out, sum_out, s_scr,
+    slab, wp, wv, p0, g0, bias, xm, pm, vm, em, pushed, a1, top_out, sum_out, s_scr,
 ):
     shuffle = to_blocks_matrix()
     mask = head_mask()
@@ -159,28 +145,26 @@
 
     def step(y, carry):
         for x in range(4):
-            start, width = span(x)
             rows = slice(ROW * x, ROW * x + ROW)
             q = spread(own_rows(p0, y, x), mask, 0.125).astype(BF16)
             g = spread(own_rows(g0, y, x), mask).astype(BF16)
             top = None
-            for j, count in chunks(3, width):
-                cols = slice(j * width, (j + count) * width)
-                s = dot(q, take(pm, (), y + j, count, start, width), NT)
-                s = s + bias_of(bias_a, bias_b, y, x, cols)
-                s_scr[x, :, cols] = s
-                top = larger(top, lane_max(s))
-                pushed[y, rows, cols] = dot(g, take(vm, (), y + j, count, start, width), NT)
+            for pieces in pairs(x, 3):
+                s = dot(q, gathered(pm, y, pieces), NT)
+                p = dot(g, gathered(vm, y, pieces), NT)
+                for k, (half, n) in enumerate(pieces):
+                    part = s[:, place(k)] + bias[y, UNITS.index((x, half)), :, place(n)]
+                    s_scr[x, half, :, place(n)] = part
+                    pushed[y, half, rows, place(n)] = p[:, place(k)]
+                    top = larger(top, part)
             top = filled(jnp.max(top, axis=1, keepdims=True))
             total = jnp.zeros((ROW, 128), F32)
-            for j, count in chunks(3, width):
-                cols = slice(j * width, (j + count) * width)
-                e = jnp.exp(s_scr[x, :, cols] - lanes(top, count * width))
-                store(em, (y,), rows, j, count, x, e.astype(BF16))
-                if width == 128:
-                    store(em, (y,), rows, j, count, 3 - x, jnp.zeros((ROW, count * width), BF16))
-                total = total + lane_sum(e)
-            wide = dot(em[y, rows, :], window(vm, y))
+            for half in HALVES[x]:
+                for n in range(3):
+                    e = jnp.exp(s_scr[x, half, :, place(n)] - top)
+                    em[y, half, rows, place(n)] = e.astype(BF16)
+                    total = total + e
+            wide = sum(dot(em[y, half, rows, :], half_window(vm, y, half)) for half in HALVES[x])
             a1[y, CUBE * x : CUBE * x + CUBE, :] = collect(wide, mask)
             top_out[y, rows, :] = top
             sum_out[y, rows, :] = filled(jnp.sum(total, axis=1, keepdims=True))
@@ -190,8 +174,7 @@
 
 
 def main_kernel(
-    low_z, high_z, wp, wv, p0, g0, xs, cs, bias_a, bias_b, xm, pm, vm, em, pushed_in, a1,
-    top_in, sum_in,
+    low_z, high_z, wp, wv, p0, g0, xs, cs, bias, xm, pm, vm, em, pushed_in, a1, top_in, sum_in,
     back_mid, back_low, back_high, att, qg, part,
     xz, pz, vz, s_scr, ee, slopes, pf_mid, pf_edge, gf_mid, gf_edge, kg, vg,
 ):
@@ -201,81 +184,83 @@
         project(shuffle, slab, wp, wv, xz, pz, vz, (z,))
     kg[...] = jnp.zeros_like(kg)
     vg[...] = jnp.zeros_like(vg)
-    for x in (0, 3):
-        rows = slice(ROW * x, ROW * x + ROW)
-        for j in range(9):
-            store(slopes, (), rows, j, 1, 3 - x, jnp.zeros((ROW, 128), BF16))
-        for j in range(6):
-            store(ee, (), rows, j, 1, 3 - x, jnp.zeros((ROW, 128), BF16))
 
     def step(y, carry):
         for x in range(4):
-            start, width = span(x)
             rows = slice(ROW * x, ROW * x + ROW)
             here = slice(CUBE * x, CUBE * x + CUBE)
-            outer = [(z, j, count) for z in range(2) for j, count in chunks(3, width)]
             q32 = spread(own_rows(p0, y, x), mask, 0.125)
             g32 = spread(own_rows(g0, y, x), mask)
             q = q32.astype(BF16)
             g = g32.astype(BF16)
             top1 = top_in[y, rows, :]
             top = None
-            for z, j, count in outer:
-                at = (3 * z + j) * width
-                cols = slice(at, at + count * width)
-                wide_cols = slice(3 * width + at, 3 * width + at + count * width)
-                s = dot(q, take(pz, (z,), y + j, count, start, width), NT)
-                s = s + bias_of(bias_a, bias_b, y, x, wide_cols)
-                s_scr[x, :, cols] = s
-                top = larger(top, lane_max(s))
+            for pieces in pairs(x, 6):
+                s = dot(q, gathered(pz, y, pieces), NT)
+                for k, (half, n) in enumerate(pieces):
+                    value = s[:, place(k)] + bias[y, UNITS.index((x, half)), :, place(3 + n)]
+                    s_scr[x, half, :, place(n)] = value
+                    top = larger(top, value)
             top = jnp.maximum(filled(jnp.max(top, axis=1, keepdims=True)), top1)
             total = jnp.zeros((ROW, 128), F32)
-            for z, j, count in outer:
-                at = (3 * z + j) * width
-                e = jnp.exp(s_scr[x, :, at : at + count * width] - lanes(top, count * width))
-                store(ee, (), rows, 3 * z + j, count, x, e.astype(BF16))
-                total = total + lane_sum(e)
+            for half in HALVES[x]:
+                for n in range(6):
+                    e = jnp.exp(s_scr[x, half, :, place(n)] - top)
+                    ee[half, rows, place(n)] = e.astype(BF16)
+                    total = total + e
             keep = jnp.exp(top1 - top)
             total = filled(jnp.sum(total, axis=1, keepdims=True)) + sum_in[y, rows, :] * keep
             inverse = 1.0 / total
             f_edge = lanes(inverse, D)
             f_mid = lanes(keep * inverse, D)
-            wide = dot(ee[rows, 0:768], window(vz, y, (0,)))
-            wide = wide + dot(ee[rows, 768:1536], window(vz, y, (1,)))
+            wide = sum(
+                dot(ee[half, rows, 384 * z : 384 * z + 384], half_window(vz, y, half, (z,)))
+                for half in HALVES[x]
+                for z in range(2)
+            )
             attended = a1[y, here, :] * collect(f_mid, mask) + collect(wide * f_edge, mask)
             attended = attended.astype(BF16)
             att[y, here, :] = attended
             product = own_rows(g0, y, x).astype(F32) * attended.astype(F32)
-            delta = filled(jnp.sum(lane_sum(spread(product, mask)), axis=1, keepdims=True))
+            delta = filled(jnp.sum(spread(product, mask), axis=1, keepdims=True))
             pf_mid[rows, :] = (q32 * f_mid).astype(BF16)
             pf_edge[rows, :] = (q32 * f_edge).astype(BF16)
             gf_mid[rows, :] = (g32 * f_mid).astype(BF16)
             gf_edge[rows, :] = (g32 * f_edge).astype(BF16)
-            for j in range(3):
-                at = j * ROW + start
-                value = pushed_in[y, rows, j * width : j * width + width] - lanes(delta, width)
-                value = em[y, rows, at : at + width].astype(F32) * value
-                slopes[rows, at : at + width] = value.astype(BF16)
-            for z, j, count in outer:
-                pushed = dot(g, take(vz, (z,), y + j, count, start, width), NT)
-                pushed = pushed - lanes(delta, count * width)
-                for n in range(count):
-                    at = (3 * z + j + n) * ROW + start
-                    value = ee[rows, at : at + width].astype(F32)
-                    value = value * pushed[:, n * width : n * width + width]
-                    slopes[rows, 768 + at : 768 + at + width] = value.astype(BF16)
-            wide = dot(slopes[rows, 768:1536], window(pz, y, (0,)))
-            wide = wide + dot(slopes[rows, 1536:2304], window(pz, y, (1,)))
-            wide = wide * f_edge + dot(slopes[rows, 0:768], window(pm, y)) * f_mid
-            qg[y, here, :] = (collect(wide, mask) * 0.125).astype(BF16)
-        for j in range(3):
-            cols = slice(j * ROW, j * ROW + ROW)
-            kg[0, y + j] += dot(slopes[:, cols], pf_mid[...], TN)
-            vg[0, y + j] += dot(em[y, :, cols], gf_mid[...], TN)
-            for z in range(2):
-                at = (3 * z + j) * ROW
-                kg[1 + z, y + j] += dot(slopes[:, 768 + at : 1024 + at], pf_edge[...], TN)
-                vg[1 + z, y + j] += dot(ee[:, at : at + ROW], gf_edge[...], TN)
+            for half in HALVES[x]:
+                for n in range(3):
+                    value = pushed_in[y, half, rows, place(n)] - delta
+                    value = em[y, half, rows, place(n)].astype(F32) * value
+                    slopes[half, rows, place(n)] = value.astype(BF16)
+            for pieces in pairs(x, 6):
+                pushed = dot(g, gathered(vz, y, pieces), NT)
+                for k, (half, n) in enumerate(pieces):
+                    value = ee[half, rows, place(n)].astype(F32) * (pushed[:, place(k)] - delta)
+                    slopes[half, rows, place(3 + n)] = value.astype(BF16)
+            near = sum(
+                dot(slopes[half, rows, 0:384], half_window(pm, y, half)) for half in HALVES[x]
+            )
+            far = sum(
+                dot(
+                    slopes[half, rows, 384 + 384 * z : 768 + 384 * z],
+                    half_window(pz, y, half, (z,)),
+                )
+                for half in HALVES[x]
+                for z in range(2)
+            )
+            qg[y, here, :] = (collect(near * f_mid + far * f_edge, mask) * 0.125).astype(BF16)
+        for half in range(2):
+            sources = members(half)
+            for grad, weights, near, p_mid, p_edge in (
+                (kg, slopes[half, sources, 384:1152], slopes[half, sources, 0:384], pf_mid, pf_edge),
+                (vg, ee[half, sources, :], em[y, half, sources, :], gf_mid, gf_edge),
+            ):
+                mid = dot(near, p_mid[sources, :], TN)
+                far = dot(weights, p_edge[sources, :], TN)
+                for j in range(3):
+                    grad[0, y + j, place(half), :] += mid[place(j)]
+                    grad[1, y + j, place(half), :] += far[place(j)]
+                    grad[2, y + j, place(half), :] += far[place(3 + j)]
         return carry
 
     lax.fori_loop(0, 2, step, 0)
@@ -353,12 +338,8 @@
     adjacent = adjacent[None, :, None, :]
     valid = adjacent & ((nine(near_other)[:, None] > 0) | center)
     bias = jnp.where(valid, 0.0, NEG).astype(F32)
-    a = jnp.stack([bias[:, 0, :, 0:2], bias[:, 3, :, 2:4]], axis=1)
-    b = bias[:, 1:3]
-    return (
-        jnp.repeat(a.reshape(4, 1, 18), CUBE, axis=2),
-        jnp.repeat(b.reshape(4, 1, 36), CUBE, axis=2),
-    )
+    units = jnp.stack([bias[:, x, :, 2 * half : 2 * half + 2] for x, half in UNITS], axis=1)
+    return jnp.repeat(units.reshape(2, len(UNITS), 1, 18), CUBE, axis=3)
 
 
 def chip_half(part):
@@ -409,31 +390,31 @@
     bias = window_bias(flags)
     xs, cs, p0, g0, wp, wv, wo = call(
         own_kernel, [((2,) + wide, BF16)] * 4 + [(wide, BF16)] * 3, flops=10 * unit, name="own"
-    )(own, cot, proj_weight, value_weight, out_weight)
+    )(*after((own, cot, proj_weight, value_weight, out_weight), slab))
     xm, pm, vm, em, pushed, a1, top, total = call(
         mid_kernel,
         [((4,) + wide, BF16)] * 3
-        + [((2, 4 * ROW, 3 * ROW), BF16), ((2, 4 * ROW, 3 * ROW), F32)]
+        + [((2, 2, 4 * ROW, 384), BF16), ((2, 2, 4 * ROW, 384), F32)]
         + [((2,) + wide, F32), columns, columns],
-        [pltpu.VMEM((4, ROW, 3 * ROW), F32)],
+        [pltpu.VMEM((4, 2, ROW, 384), F32)],
         flops=200 * unit,
         name="mid",
-    )(slab, wp, wv, p0, g0, *bias)
+    )(slab, wp, wv, p0, g0, bias)
     back_mid, back_low, back_high, att, qg, part = call(
         main_kernel,
         [((4,) + wide, BF16)] * 3 + [((2,) + wide, BF16)] * 2 + [((ROW, 3 * D), BF16)],
         [pltpu.VMEM((2, 4) + wide, BF16)] * 3
         + [
-            pltpu.VMEM((4, ROW, 6 * ROW), F32),
-            pltpu.VMEM((4 * ROW, 6 * ROW), BF16),
-            pltpu.VMEM((4 * ROW, 9 * ROW), BF16),
+            pltpu.VMEM((4, 2, ROW, 768), F32),
+            pltpu.VMEM((2, 4 * ROW, 768), BF16),
+            pltpu.VMEM((2, 4 * ROW, 1152), BF16),
         ]
         + [pltpu.VMEM((4 * ROW, D), BF16)] * 4
         + [pltpu.VMEM((3, 4) + wide, F32)] * 2,
         flops=900 * unit,
         name="main",
         limit=32,
-    )(low_z, high_z, wp, wv, p0, g0, xs, cs, *bias, xm, pm, vm, em, pushed, a1, top, total)
+    )(low_z, high_z, wp, wv, p0, g0, xs, cs, bias, xm, pm, vm, em, pushed, a1, top, total)
 
     mine = chip_half(part)
     got = (

time: 127 us -> 122 us (0.961)
  starting transfers between devices: 52.6 us -> 50.4 us
  waiting for transfers between devices: 28.6 us -> 27.2 us
    all_to_all x1, starting transfers between devices: 17 us -> 15 us  [summed_share(): got = lax.all_to_all(mine.reshape(places, 2, -1), ('gz', 'gy'), 0, 0)]
    pallas_call x1, Pallas kernels: 22.9 us -> 21.1 us  [on_device(): call(main_kernel, [((4,) + wide, BF16)] * 3 + [((2,) + wide, BF16)] * 2 +...]
    ppermute x12, waiting for transfers between devices: 18 us -> 16.6 us  [shift(): return lax.ppermute(block, AXES, route)]
  transfers between devices with their start and end apart: 14 -> 14, of which waited for: 7 -> 7; matrix products, arithmetic and copies ran while one was open for 6% -> 6% of each run, Pallas kernels for 5% -> 6%
where the time goes in v5:
time: 122 us; the launch traced here: 121 us
  starting transfers between devices  50.4 us (41%)
  Pallas kernels  28.3 us (23%)
  waiting for transfers between devices  27.2 us (22%)
  local copies, waits for them, and re-layouts  10.3 us (8%)
  other arithmetic  4.14 us (3%)
    ppermute x12, starting transfers between devices, shift(): return lax.ppermute(block, AXES, route)  28.6 us
    pallas_call x1, Pallas kernels, on_device(): call(main_kernel, [((4,) + wide, BF16)] * 3 + [((2,) + wide, BF16)] * 2 +...  21.1 us
    ppermute x12, waiting for transfers between devices, shift(): return lax.ppermute(block, AXES, route)  16.6 us
    all_to_all x1, starting transfers between devices, summed_share(): got = lax.all_to_all(mine.reshape(places, 2, -1), ('gz', 'gy'), 0, 0)  15 us
    all_to_all x1, waiting for transfers between devices, summed_share(): got = lax.all_to_all(mine.reshape(places, 2, -1), ('gz', 'gy'), 0, 0)  10.5 us
    all_to_all x1, starting transfers between devices, all_shares(): lax.all_to_all(jnp.broadcast_to(total[None], (places,) + total.shape), ('...  6.82 us
    pallas_call x1, Pallas kernels, on_device(): call(mid_kernel, [((4,) + wide, BF16)] * 3 + [((2, 2, 4 * ROW, 384), BF16...  5.33 us
    unnamed x13, local copies, waits for them, and re-layouts  4.69 us
  transfers between devices with their start and end apart: 14, of which 7 were waited for; matrix products, arithmetic and copies ran while one was open for 6% of the time, Pallas kernels for 6%

profile of v5, /device:TPU:1, one launch (start us, length us, event | category | flops | bytes accessed | tf_op | source)
XLA Modules:
  0.0 121.3 jit_solution(16913795020128621641)
XLA Ops:
  0.6 3.3 %collective-permute-start.1 = (bf16[4,8,16,256]{3,2,1,0:T(8,128)(2,1)}, bf16[4,8,16,256]{3,2,1,0:T(8,128)(2,1)S(1)}, u32[]{:S(2)}, u32[]{:S(2)}) collective-permute-start(bf16[4,8,16,256]{3,2,1,0:T(8,128)(2,1)} %bitcast.34), channel_id=1, source_target_pairs={{0,128},{1,129},{2,130},{3,131},{4,132},{5,133},{6,134},{7,135},{8... | collective-permute-start | bytes 786440 | tf_op jit(solution)/shard_map/ppermute | solution.py:318
  5.0 3.0 %collective-permute-start = (bf16[4,4,16,256]{3,2,1,0:T(8,128)(2,1)S(1)}, bf16[4,4,16,256]{3,2,1,0:T(8,128)(2,1)S(1)}, u32[]{:S(2)}, u32[]{:S(2)}) collective-permute-start(bf16[4,4,16,256]{3,2,1,0:T(8,128)(2,1)S(1)} %get-tuple-element.75), channel_id=1, source_target_pairs={{0,129},{1,130},{2,131},{3,132},{4,133},{5,134},{6,135},{8,137},{9... | collective-permute-start | bytes 393224 | tf_op jit(solution)/shard_map/ppermute | solution.py:318
  8.0 1.3 %collective-permute-start.2 = (bf16[4,4,16,256]{3,2,1,0:T(8,128)(2,1)S(1)}, bf16[4,4,16,256]{3,2,1,0:T(8,128)(2,1)S(1)}, u32[]{:S(2)}, u32[]{:S(2)}) collective-permute-start(bf16[4,4,16,256]{3,2,1,0:T(8,128)(2,1)S(1)} %get-tuple-element.74), channel_id=1, source_target_pairs={{1,128},{2,129},{3,130},{4,131},{5,132},{6,133},{7,134},{9,136},{1... | collective-permute-start | bytes 393224 | tf_op jit(solution)/shard_map/ppermute | solution.py:318
  12.6 4.5 %collective-permute-done.2 = bf16[4,4,16,256]{3,2,1,0:T(8,128)(2,1)S(1)} collective-permute-done((bf16[4,4,16,256]{3,2,1,0:T(8,128)(2,1)S(1)}, bf16[4,4,16,256]{3,2,1,0:T(8,128)(2,1)S(1)}, u32[]{:S(2)}, u32[]{:S(2)}) %collective-permute-start.2) | collective-permute-done | bytes 131104 | tf_op jit(solution)/shard_map/ppermute | solution.py:318
  17.1 3.6 %collective-permute-start.3 = (bf16[4,16,16,256]{3,2,1,0:T(8,128)(2,1)S(1)}, bf16[4,16,16,256]{3,2,1,0:T(8,128)(2,1)S(1)}, u32[]{:S(2)}, u32[]{:S(2)}) collective-permute-start(bf16[4,16,16,256]{3,2,1,0:T(8,128)(2,1)S(1)} %constant_dynamic-update-slice_fusion.slab), channel_id=1, source_target_pairs={{0,8},{1,9},{2,10},{3,11},{4,12},{5,13},{6,14},{7,15},{8,16},{9,17... | collective-permute-start | bytes 1572872 | tf_op jit(solution)/shard_map/ppermute | solution.py:318
  20.6 1.3 %collective-permute-start.4 = (bf16[4,16,16,256]{3,2,1,0:T(8,128)(2,1)S(1)}, bf16[4,16,16,256]{3,2,1,0:T(8,128)(2,1)S(1)}, u32[]{:S(2)}, u32[]{:S(2)}) collective-permute-start(bf16[4,16,16,256]{3,2,1,0:T(8,128)(2,1)S(1)} %constant_dynamic-update-slice_fusion.slab), channel_id=1, source_target_pairs={{8,0},{9,1},{10,2},{11,3},{12,4},{13,5},{14,6},{15,7},{16,8},{17,9... | collective-permute-start | bytes 1572872 | tf_op jit(solution)/shard_map/ppermute | solution.py:318
  27.1 5.3 %mid.1 = (bf16[4,256,256]{2,1,0:T(8,128)(2,1)S(1)}, bf16[4,256,256]{2,1,0:T(8,128)(2,1)S(1)}, bf16[4,256,256]{2,1,0:T(8,128)(2,1)S(1)}, bf16[2,2,1024,384]{3,2,1...) custom-call(bf16[4,16,16,256]{3,2,1,0:T(8,128)(2,1)S(1)} %constant_d, ...), custom_call_target="tpu_custom_call" | custom-call | flops 6710886400 | bytes 4194304 | tf_op jit(solution)/shard_map/mid/pallas_call | solution.py:394
  32.5 3.2 %collective-permute-done.4.high_z = bf16[4,16,16,256]{3,2,1,0:T(8,128)(2,1)S(1)} collective-permute-done((bf16[4,16,16,256]{3,2,1,0:T(8,128)(2,1)S(1)}, bf16[4,16,16,256]{3,2,1,0:T(8,128)(2,1)S(1)}, u32[]{:S(2)}, u32[]{:S(2)}) %collective-permute-start.4) | collective-permute-done | bytes 524320 | tf_op jit(solution)/shard_map/ppermute | solution.py:318
  35.7 21.1 %main.1 = (bf16[4,256,256]{2,1,0:T(8,128)(2,1)S(1)}, bf16[4,256,256]{2,1,0:T(8,128)(2,1)S(1)}, bf16[4,256,256]{2,1,0:T(8,128)(2,1)S(1)}, bf16[2,256,256]{2,1,0:T...) custom-call(bf16[4,16,16,256]{3,2,1,0:T(8,128)(2,1)S(1)} %collective-permute-done.3.low_z, ...), custom_call_target="tpu_custom_call" | custom-call | flops 30198988800 | bytes 4194304 | tf_op jit(solution)/shard_map/main/pallas_call | solution.py:403
  56.7 1.3 %collective-permute-start.5 = (bf16[4,256,256]{2,1,0:T(8,128)(2,1)S(1)}, bf16[4,256,256]{2,1,0:T(8,128)(2,1)S(1)}, u32[]{:S(2)}, u32[]{:S(2)}) collective-permute-start(bf16[4,256,256]{2,1,0:T(8,128)(2,1)S(1)} %get-tuple-element.57), channel_id=1, source_target_pairs={{8,128},{9,129},{10,130},{11,131},{12,132},{13,133},{14,134},{15,1... | collective-permute-start | bytes 1572872 | tf_op jit(solution)/shard_map/ppermute | solution.py:318
  58.0 1.5 %collective-permute-start.6 = (bf16[4,256,256]{2,1,0:T(8,128)(2,1)S(1)}, bf16[4,256,256]{2,1,0:T(8,128)(2,1)}, u32[]{:S(2)}, u32[]{:S(2)}) collective-permute-start(bf16[4,256,256]{2,1,0:T(8,128)(2,1)S(1)} %get-tuple-element.58), channel_id=1, source_target_pairs={{0,128},{1,129},{2,130},{3,131},{4,132},{5,133},{6,134},{7,135},{8... | collective-permute-start | bytes 1572872 | tf_op jit(solution)/shard_map/ppermute | solution.py:318
  59.5 5.1 %collective-permute-start.7 = (bf16[4,256,256]{2,1,0:T(8,128)(2,1)S(1)}, bf16[4,256,256]{2,1,0:T(8,128)(2,1)}, u32[]{:S(2)}, u32[]{:S(2)}) collective-permute-start(bf16[4,256,256]{2,1,0:T(8,128)(2,1)S(1)} %get-tuple-element.59), channel_id=1, source_target_pairs={{0,136},{1,137},{2,138},{3,139},{4,140},{5,141},{6,142},{7,143},{8... | collective-permute-start | bytes 1572872 | tf_op jit(solution)/shard_map/ppermute | solution.py:318
  65.0 1.3 %collective-permute-done.10 = bf16[128,768]{1,0:T(8,128)(2,1)} collective-permute-done((bf16[128,768]{1,0:T(8,128)(2,1)S(1)}, bf16[128,768]{1,0:T(8,128)(2,1)}, u32[]{:S(2)}, u32[]{:S(2)}) %collective-permute-start.10) | collective-permute-done | bytes 196640 | tf_op jit(solution)/shard_map/ppermute | solution.py:318
  68.0 15.0 %all-to-all-start = ((bf16[128,2,384]{2,1,0:T(2,128)(2,1)}), bf16[128,2,384]{2,1,0:T(2,128)(2,1)S(1)}, u32[]{:S(2)}, u32[]{:S(2)}) async-start(bf16[128,2,384]{2,1,0:T(2,128)(2,1)} %reshape.47), calls=%async_computation | async-start | bytes 393216 | tf_op jit(solution)/shard_map/all_to_all | solution.py:355
  83.0 1.4 %fusion = (bf16[4,256,256]{2,1,0:T(8,128)(2,1)S(1)}, f32[4,256,256]{2,1,0:T(8,128)S(1)}) fusion(bf16[4,256,256]{2,1,0:T(8,128)(2,1)} %collective-permute-done.7, bf16[4,256,256]{2,1,0:T(8,128)(2,1)} %collective-permute-done.6, bf16[4,256,256]{2,1,0:T(8,128)(2,1)S(1)} %collective-permute-done.5), kind=kLoop, calls=%fused_computation.23 | loop fusion | flops 1572864 | bytes 3145728 | tf_op jit(solution)/shard_map/convert.3
  84.4 10.5 %all-to-all-done = bf16[128,2,384]{2,1,0:T(2,128)(2,1)S(1)} async-done(((bf16[128,2,384]{2,1,0:T(2,128)(2,1)}), bf16[128,2,384]{2,1,0:T(2,128)(2,1)S(1)}, u32[]{:S(2)}, u32[]{:S(2)}) %all-to-all-start) | async-done | bytes 196640 | tf_op jit(solution)/shard_map/all_to_all | solution.py:355
  96.0 6.8 %all-to-all-start.1 = ((bf16[128,2,384]{2,1,0:T(2,128)(2,1)}), bf16[128,2,384]{2,1,0:T(2,128)(2,1)S(1)}, u32[]{:S(2)}, u32[]{:S(2)}) async-start(bf16[128,2,384]{2,1,0:T(2,128)(2,1)} %broadcast_in_dim.32), calls=%async_computation.1 | async-start | bytes 393216 | tf_op jit(solution)/shard_map/all_to_all | solution.py:361
  102.8 4.0 %collective-permute-start.8 = (bf16[256,256]{1,0:T(8,128)(2,1)S(1)}, bf16[256,256]{1,0:T(8,128)(2,1)S(1)}, u32[]{:S(2)}, u32[]{:S(2)}) collective-permute-start(bf16[256,256]{1,0:T(8,128)(2,1)S(1)} %get-tuple-element.71), channel_id=1, source_target_pairs={{0,1},{1,2},{2,3},{3,4},{4,5},{5,6},{6,7},{8,9},{9,10},{10,11},{11... | collective-permute-start | bytes 393224 | tf_op jit(solution)/shard_map/ppermute | solution.py:318
  106.8 1.3 %collective-permute-start.9 = (bf16[256,256]{1,0:T(8,128)(2,1)S(1)}, bf16[256,256]{1,0:T(8,128)(2,1)S(1)}, u32[]{:S(2)}, u32[]{:S(2)}) collective-permute-start(bf16[256,256]{1,0:T(8,128)(2,1)S(1)} %get-tuple-element.70), channel_id=1, source_target_pairs={{1,0},{2,1},{3,2},{4,3},{5,4},{6,5},{7,6},{9,8},{10,9},{11,10},{12... | collective-permute-start | bytes 393224 | tf_op jit(solution)/shard_map/ppermute | solution.py:318
  108.2 1.1 collective-permute-done.8.from_low
  109.3 5.5 %collective-permute-done.9.from_high = bf16[256,256]{1,0:T(8,128)(2,1)S(1)} collective-permute-done((bf16[256,256]{1,0:T(8,128)(2,1)S(1)}, bf16[256,256]{1,0:T(8,128)(2,1)S(1)}, u32[]{:S(2)}, u32[]{:S(2)}) %collective-permute-start.9) | collective-permute-done | bytes 131104 | tf_op jit(solution)/shard_map/ppermute | solution.py:318
  114.8 1.3 %finish.1 = (bf16[4,8,16,256]{3,2,1,0:T(8,128)(2,1)}, bf16[4,8,16,256]{3,2,1,0:T(8,128)(2,1)}) custom-call(bf16[2,256,256]{2,1,0:T(8,128)(2,1)S(1)} %get-tuple-element.54.att, bf16[2,256,256]{2,1,0:T(8,128)(2,1)S(1)} %get-tuple-element.55.qg, bf16[256,256]{1,0:T(8,128)(2,1)S(1)} %get-tuple-element.40.wp, bf16[256,256]{1,0:T(8,128)(2,1)S(1)} %get-tuple-element.56.wo, ...), custom_call_target="tpu_custom_call" | custom-call | flops 335544320 | bytes 4194304 | tf_op jit(solution)/shard_map/finish/pallas_call | solution.py:431
  116.1 2.7 %collective-permute-start.11 = (bf16[128,2,384]{2,1,0:T(2,128)(2,1)S(1)}, bf16[128,2,384]{2,1,0:T(2,128)(2,1)S(1)}, u32[]{:S(2)}, u32[]{:S(2)}) collective-permute-start(bf16[128,2,384]{2,1,0:T(2,128)(2,1)S(1)} %all-to-all-done.1), channel_id=1, source_target_pairs={{0,128},{1,129},{2,130},{3,131},{4,132},{5,133},{6,134},{7,135},{8... | collective-permute-start | bytes 589832 | tf_op jit(solution)/shard_map/ppermute | solution.py:318
  118.8 1.1 collective-permute-done.11
  (54 shorter events, 14.0 us)
Async XLA Ops:
  0.6 11.9 %collective-permute-start.1 = (bf16[4,8,16,256]{3,2,1,0:T(8,128)(2,1)}, bf16[4,8,16,256]{3,2,1,0:T(8,128)(2,1)S(1)}, u32[]{:S(2)}, u32[]{:S(2)}) collective-permute-start(bf16[4,8,16,256]{3,2,1,0:T(8,128)(2,1)} %bitcast.34), channel_id=1, source_target_pairs={{0,128},{1,129},{2,130},{3,131},{4,132},{5,133},{6,134},{7,135},{8... | collective-permute-start | bytes 786440 | tf_op jit(solution)/shard_map/ppermute | solution.py:318
  5.0 7.5 %collective-permute-start = (bf16[4,4,16,256]{3,2,1,0:T(8,128)(2,1)S(1)}, bf16[4,4,16,256]{3,2,1,0:T(8,128)(2,1)S(1)}, u32[]{:S(2)}, u32[]{:S(2)}) collective-permute-start(bf16[4,4,16,256]{3,2,1,0:T(8,128)(2,1)S(1)} %get-tuple-element.75), channel_id=1, source_target_pairs={{0,129},{1,130},{2,131},{3,132},{4,133},{5,134},{6,135},{8,137},{9... | collective-permute-start | bytes 393224 | tf_op jit(solution)/shard_map/ppermute | solution.py:318
  8.0 9.1 %collective-permute-start.2 = (bf16[4,4,16,256]{3,2,1,0:T(8,128)(2,1)S(1)}, bf16[4,4,16,256]{3,2,1,0:T(8,128)(2,1)S(1)}, u32[]{:S(2)}, u32[]{:S(2)}) collective-permute-start(bf16[4,4,16,256]{3,2,1,0:T(8,128)(2,1)S(1)} %get-tuple-element.74), channel_id=1, source_target_pairs={{1,128},{2,129},{3,130},{4,131},{5,132},{6,133},{7,134},{9,136},{1... | collective-permute-start | bytes 393224 | tf_op jit(solution)/shard_map/ppermute | solution.py:318
  17.1 15.4 %collective-permute-start.3 = (bf16[4,16,16,256]{3,2,1,0:T(8,128)(2,1)S(1)}, bf16[4,16,16,256]{3,2,1,0:T(8,128)(2,1)S(1)}, u32[]{:S(2)}, u32[]{:S(2)}) collective-permute-start(bf16[4,16,16,256]{3,2,1,0:T(8,128)(2,1)S(1)} %constant_dynamic-update-slice_fusion.slab), channel_id=1, source_target_pairs={{0,8},{1,9},{2,10},{3,11},{4,12},{5,13},{6,14},{7,15},{8,16},{9,17... | collective-permute-start | bytes 1572872 | tf_op jit(solution)/shard_map/ppermute | solution.py:318
  20.6 15.0 %collective-permute-start.4 = (bf16[4,16,16,256]{3,2,1,0:T(8,128)(2,1)S(1)}, bf16[4,16,16,256]{3,2,1,0:T(8,128)(2,1)S(1)}, u32[]{:S(2)}, u32[]{:S(2)}) collective-permute-start(bf16[4,16,16,256]{3,2,1,0:T(8,128)(2,1)S(1)} %constant_dynamic-update-slice_fusion.slab), channel_id=1, source_target_pairs={{8,0},{9,1},{10,2},{11,3},{12,4},{13,5},{14,6},{15,7},{16,8},{17,9... | collective-permute-start | bytes 1572872 | tf_op jit(solution)/shard_map/ppermute | solution.py:318
  21.9 1.0 copy-start
  22.9 0.9 copy-start.1
  23.8 0.9 copy-start.2
  24.7 0.9 copy-start.3
  25.6 0.9 copy-start.4
  56.7 26.2 %collective-permute-start.5 = (bf16[4,256,256]{2,1,0:T(8,128)(2,1)S(1)}, bf16[4,256,256]{2,1,0:T(8,128)(2,1)S(1)}, u32[]{:S(2)}, u32[]{:S(2)}) collective-permute-start(bf16[4,256,256]{2,1,0:T(8,128)(2,1)S(1)} %get-tuple-element.57), channel_id=1, source_target_pairs={{8,128},{9,129},{10,130},{11,131},{12,132},{13,133},{14,134},{15,1... | collective-permute-start | bytes 1572872 | tf_op jit(solution)/shard_map/ppermute | solution.py:318
  58.0 24.9 %collective-permute-start.6 = (bf16[4,256,256]{2,1,0:T(8,128)(2,1)S(1)}, bf16[4,256,256]{2,1,0:T(8,128)(2,1)}, u32[]{:S(2)}, u32[]{:S(2)}) collective-permute-start(bf16[4,256,256]{2,1,0:T(8,128)(2,1)S(1)} %get-tuple-element.58), channel_id=1, source_target_pairs={{0,128},{1,129},{2,130},{3,131},{4,132},{5,133},{6,134},{7,135},{8... | collective-permute-start | bytes 1572872 | tf_op jit(solution)/shard_map/ppermute | solution.py:318
  59.5 23.5 %collective-permute-start.7 = (bf16[4,256,256]{2,1,0:T(8,128)(2,1)S(1)}, bf16[4,256,256]{2,1,0:T(8,128)(2,1)}, u32[]{:S(2)}, u32[]{:S(2)}) collective-permute-start(bf16[4,256,256]{2,1,0:T(8,128)(2,1)S(1)} %get-tuple-element.59), channel_id=1, source_target_pairs={{0,136},{1,137},{2,138},{3,139},{4,140},{5,141},{6,142},{7,143},{8... | collective-permute-start | bytes 1572872 | tf_op jit(solution)/shard_map/ppermute | solution.py:318
  64.6 1.7 %collective-permute-start.10 = (bf16[128,768]{1,0:T(8,128)(2,1)S(1)}, bf16[128,768]{1,0:T(8,128)(2,1)}, u32[]{:S(2)}, u32[]{:S(2)}) collective-permute-start(bf16[128,768]{1,0:T(8,128)(2,1)S(1)} %constant_dynamic-slice_fusion), channel_id=1, source_target_pairs={{0,128},{1,129},{2,130},{3,131},{4,132},{5,133},{6,134},{7,135},{8... | collective-permute-start | bytes 589832 | tf_op jit(solution)/shard_map/ppermute | solution.py:318
  68.0 27.0 %all-to-all-start = ((bf16[128,2,384]{2,1,0:T(2,128)(2,1)}), bf16[128,2,384]{2,1,0:T(2,128)(2,1)S(1)}, u32[]{:S(2)}, u32[]{:S(2)}) async-start(bf16[128,2,384]{2,1,0:T(2,128)(2,1)} %reshape.47), calls=%async_computation | async-start | bytes 393216 | tf_op jit(solution)/shard_map/all_to_all | solution.py:355
  96.0 20.1 %all-to-all-start.1 = ((bf16[128,2,384]{2,1,0:T(2,128)(2,1)}), bf16[128,2,384]{2,1,0:T(2,128)(2,1)S(1)}, u32[]{:S(2)}, u32[]{:S(2)}) async-start(bf16[128,2,384]{2,1,0:T(2,128)(2,1)} %broadcast_in_dim.32), calls=%async_computation.1 | async-start | bytes 393216 | tf_op jit(solution)/shard_map/all_to_all | solution.py:361
  102.8 6.4 %collective-permute-start.8 = (bf16[256,256]{1,0:T(8,128)(2,1)S(1)}, bf16[256,256]{1,0:T(8,128)(2,1)S(1)}, u32[]{:S(2)}, u32[]{:S(2)}) collective-permute-start(bf16[256,256]{1,0:T(8,128)(2,1)S(1)} %get-tuple-element.71), channel_id=1, source_target_pairs={{0,1},{1,2},{2,3},{3,4},{4,5},{5,6},{6,7},{8,9},{9,10},{10,11},{11... | collective-permute-start | bytes 393224 | tf_op jit(solution)/shard_map/ppermute | solution.py:318
  106.8 8.0 %collective-permute-start.9 = (bf16[256,256]{1,0:T(8,128)(2,1)S(1)}, bf16[256,256]{1,0:T(8,128)(2,1)S(1)}, u32[]{:S(2)}, u32[]{:S(2)}) collective-permute-start(bf16[256,256]{1,0:T(8,128)(2,1)S(1)} %get-tuple-element.70), channel_id=1, source_target_pairs={{1,0},{2,1},{3,2},{4,3},{5,4},{6,5},{7,6},{9,8},{10,9},{11,10},{12... | collective-permute-start | bytes 393224 | tf_op jit(solution)/shard_map/ppermute | solution.py:318
  116.1 3.7 %collective-permute-start.11 = (bf16[128,2,384]{2,1,0:T(2,128)(2,1)S(1)}, bf16[128,2,384]{2,1,0:T(2,128)(2,1)S(1)}, u32[]{:S(2)}, u32[]{:S(2)}) collective-permute-start(bf16[128,2,384]{2,1,0:T(2,128)(2,1)S(1)} %all-to-all-done.1), channel_id=1, source_target_pairs={{0,128},{1,129},{2,130},{3,131},{4,132},{5,133},{6,134},{7,135},{8... | collective-permute-start | bytes 589832 | tf_op jit(solution)/shard_map/ppermute | solution.py:318

commit v6 on v5

--- a/solution.py
+++ b/solution.py
@@ -182,18 +182,14 @@
     mask = head_mask()
     for z, slab in enumerate((low_z, high_z)):
         project(shuffle, slab, wp, wv, xz, pz, vz, (z,))
-    kg[...] = jnp.zeros_like(kg)
-    vg[...] = jnp.zeros_like(vg)
-
-    def step(y, carry):
-        for x in range(4):
-            rows = slice(ROW * x, ROW * x + ROW)
-            here = slice(CUBE * x, CUBE * x + CUBE)
+    for y in range(2):
+        spreads = []
+        tops = []
+        for x in range(4):
             q32 = spread(own_rows(p0, y, x), mask, 0.125)
             g32 = spread(own_rows(g0, y, x), mask)
+            spreads.append((q32, g32))
             q = q32.astype(BF16)
-            g = g32.astype(BF16)
-            top1 = top_in[y, rows, :]
             top = None
             for pieces in pairs(x, 6):
                 s = dot(q, gathered(pz, y, pieces), NT)
@@ -201,7 +197,12 @@
                     value = s[:, place(k)] + bias[y, UNITS.index((x, half)), :, place(3 + n)]
                     s_scr[x, half, :, place(n)] = value
                     top = larger(top, value)
-            top = jnp.maximum(filled(jnp.max(top, axis=1, keepdims=True)), top1)
+            tops.append(top)
+        factors = []
+        for x in range(4):
+            rows = slice(ROW * x, ROW * x + ROW)
+            top1 = top_in[y, rows, :]
+            top = jnp.maximum(filled(jnp.max(tops[x], axis=1, keepdims=True)), top1)
             total = jnp.zeros((ROW, 128), F32)
             for half in HALVES[x]:
                 for n in range(6):
@@ -211,8 +212,13 @@
             keep = jnp.exp(top1 - top)
             total = filled(jnp.sum(total, axis=1, keepdims=True)) + sum_in[y, rows, :] * keep
             inverse = 1.0 / total
-            f_edge = lanes(inverse, D)
-            f_mid = lanes(keep * inverse, D)
+            factors.append((keep * inverse, inverse))
+        deltas = []
+        for x in range(4):
+            rows = slice(ROW * x, ROW * x + ROW)
+            here = slice(CUBE * x, CUBE * x + CUBE)
+            f_mid, f_edge = (lanes(f, D) for f in factors[x])
+            q32, g32 = spreads[x]
             wide = sum(
                 dot(ee[half, rows, 384 * z : 384 * z + 384], half_window(vz, y, half, (z,)))
                 for half in HALVES[x]
@@ -222,11 +228,15 @@
             attended = attended.astype(BF16)
             att[y, here, :] = attended
             product = own_rows(g0, y, x).astype(F32) * attended.astype(F32)
-            delta = filled(jnp.sum(spread(product, mask), axis=1, keepdims=True))
+            deltas.append(filled(jnp.sum(spread(product, mask), axis=1, keepdims=True)))
             pf_mid[rows, :] = (q32 * f_mid).astype(BF16)
             pf_edge[rows, :] = (q32 * f_edge).astype(BF16)
             gf_mid[rows, :] = (g32 * f_mid).astype(BF16)
             gf_edge[rows, :] = (g32 * f_edge).astype(BF16)
+        for x in range(4):
+            rows = slice(ROW * x, ROW * x + ROW)
+            delta = deltas[x]
+            g = spreads[x][1].astype(BF16)
             for half in HALVES[x]:
                 for n in range(3):
                     value = pushed_in[y, half, rows, place(n)] - delta
@@ -237,6 +247,9 @@
                 for k, (half, n) in enumerate(pieces):
                     value = ee[half, rows, place(n)].astype(F32) * (pushed[:, place(k)] - delta)
                     slopes[half, rows, place(3 + n)] = value.astype(BF16)
+        for x in range(4):
+            rows = slice(ROW * x, ROW * x + ROW)
+            f_mid, f_edge = (lanes(f, D) for f in factors[x])
             near = sum(
                 dot(slopes[half, rows, 0:384], half_window(pm, y, half)) for half in HALVES[x]
             )
@@ -248,7 +261,8 @@
                 for half in HALVES[x]
                 for z in range(2)
             )
-            qg[y, here, :] = (collect(near * f_mid + far * f_edge, mask) * 0.125).astype(BF16)
+            near = collect(near * f_mid + far * f_edge, mask)
+            qg[y, CUBE * x : CUBE * x + CUBE, :] = (near * 0.125).astype(BF16)
         for half in range(2):
             sources = members(half)
             for grad, weights, near, p_mid, p_edge in (
@@ -258,12 +272,10 @@
                 mid = dot(near, p_mid[sources, :], TN)
                 far = dot(weights, p_edge[sources, :], TN)
                 for j in range(3):
-                    grad[0, y + j, place(half), :] += mid[place(j)]
-                    grad[1, y + j, place(half), :] += far[place(j)]
-                    grad[2, y + j, place(half), :] += far[place(3 + j)]
-        return carry
-
-    lax.fori_loop(0, 2, step, 0)
+                    for z, value in enumerate((mid[place(j)], far[place(j)], far[place(3 + j)])):
+                        if y == 1 and j < 2:
+                            value = value + grad[z, y + j, place(half), :]
+                        grad[z, y + j, place(half), :] = value
     gp = dot(xs[0], qg[0], TN) + dot(xs[1], qg[1], TN)
     gv = jnp.zeros((D, D), F32)
     for z, out in enumerate((back_mid, back_low, back_high)):

time: 122 us -> 118 us (0.967)
  Pallas kernels: 28.3 us -> 24.6 us
    pallas_call x1, Pallas kernels: 21.1 us -> 17.4 us  [on_device(): call(main_kernel, [((4,) + wide, BF16)] * 3 + [((2,) + wide, BF16)] * 2 +...]
where the time goes in v6:
time: 118 us
  starting transfers between devices  50.5 us (43%)
  waiting for transfers between devices  27.2 us (23%)
  Pallas kernels  24.6 us (21%)
  local copies, waits for them, and re-layouts  10.3 us (9%)
  other arithmetic  4.14 us (4%)
    ppermute x12, starting transfers between devices, shift(): return lax.ppermute(block, AXES, route)  28.6 us
    pallas_call x1, Pallas kernels, on_device(): call(main_kernel, [((4,) + wide, BF16)] * 3 + [((2,) + wide, BF16)] * 2 +...  17.4 us
    ppermute x12, waiting for transfers between devices, shift(): return lax.ppermute(block, AXES, route)  16.6 us
    all_to_all x1, starting transfers between devices, summed_share(): got = lax.all_to_all(mine.reshape(places, 2, -1), ('gz', 'gy'), 0, 0)  15 us
    all_to_all x1, waiting for transfers between devices, summed_share(): got = lax.all_to_all(mine.reshape(places, 2, -1), ('gz', 'gy'), 0, 0)  10.5 us
    all_to_all x1, starting transfers between devices, all_shares(): lax.all_to_all(jnp.broadcast_to(total[None], (places,) + total.shape), ('...  6.82 us
    pallas_call x1, Pallas kernels, on_device(): call(mid_kernel, [((4,) + wide, BF16)] * 3 + [((2, 2, 4 * ROW, 384), BF16...  5.35 us
    unnamed x13, local copies, waits for them, and re-layouts  4.69 us
  transfers between devices with their start and end apart: 14, of which 7 were waited for; matrix products, arithmetic and copies ran while one was open for 6% of the time, Pallas kernels for 6%

profile of v6, /device:TPU:1, one launch (start us, length us, event | category | flops | bytes accessed | tf_op | source)
XLA Modules:
  0.0 117.6 jit_solution(12119832832546233458)
XLA Ops:
  0.6 3.3 %collective-permute-start.1 = (bf16[4,8,16,256]{3,2,1,0:T(8,128)(2,1)}, bf16[4,8,16,256]{3,2,1,0:T(8,128)(2,1)S(1)}, u32[]{:S(2)}, u32[]{:S(2)}) collective-permute-start(bf16[4,8,16,256]{3,2,1,0:T(8,128)(2,1)} %bitcast.34), channel_id=1, source_target_pairs={{0,128},{1,129},{2,130},{3,131},{4,132},{5,133},{6,134},{7,135},{8... | collective-permute-start | bytes 786440 | tf_op jit(solution)/shard_map/ppermute | solution.py:330
  5.0 3.0 %collective-permute-start = (bf16[4,4,16,256]{3,2,1,0:T(8,128)(2,1)S(1)}, bf16[4,4,16,256]{3,2,1,0:T(8,128)(2,1)S(1)}, u32[]{:S(2)}, u32[]{:S(2)}) collective-permute-start(bf16[4,4,16,256]{3,2,1,0:T(8,128)(2,1)S(1)} %get-tuple-element.75), channel_id=1, source_target_pairs={{0,129},{1,130},{2,131},{3,132},{4,133},{5,134},{6,135},{8,137},{9... | collective-permute-start | bytes 393224 | tf_op jit(solution)/shard_map/ppermute | solution.py:330
  8.0 1.3 %collective-permute-start.2 = (bf16[4,4,16,256]{3,2,1,0:T(8,128)(2,1)S(1)}, bf16[4,4,16,256]{3,2,1,0:T(8,128)(2,1)S(1)}, u32[]{:S(2)}, u32[]{:S(2)}) collective-permute-start(bf16[4,4,16,256]{3,2,1,0:T(8,128)(2,1)S(1)} %get-tuple-element.74), channel_id=1, source_target_pairs={{1,128},{2,129},{3,130},{4,131},{5,132},{6,133},{7,134},{9,136},{1... | collective-permute-start | bytes 393224 | tf_op jit(solution)/shard_map/ppermute | solution.py:330
  12.6 4.5 %collective-permute-done.2 = bf16[4,4,16,256]{3,2,1,0:T(8,128)(2,1)S(1)} collective-permute-done((bf16[4,4,16,256]{3,2,1,0:T(8,128)(2,1)S(1)}, bf16[4,4,16,256]{3,2,1,0:T(8,128)(2,1)S(1)}, u32[]{:S(2)}, u32[]{:S(2)}) %collective-permute-start.2) | collective-permute-done | bytes 131104 | tf_op jit(solution)/shard_map/ppermute | solution.py:330
  17.1 3.6 %collective-permute-start.3 = (bf16[4,16,16,256]{3,2,1,0:T(8,128)(2,1)S(1)}, bf16[4,16,16,256]{3,2,1,0:T(8,128)(2,1)S(1)}, u32[]{:S(2)}, u32[]{:S(2)}) collective-permute-start(bf16[4,16,16,256]{3,2,1,0:T(8,128)(2,1)S(1)} %constant_dynamic-update-slice_fusion.slab), channel_id=1, source_target_pairs={{0,8},{1,9},{2,10},{3,11},{4,12},{5,13},{6,14},{7,15},{8,16},{9,17... | collective-permute-start | bytes 1572872 | tf_op jit(solution)/shard_map/ppermute | solution.py:330
  20.6 1.3 %collective-permute-start.4 = (bf16[4,16,16,256]{3,2,1,0:T(8,128)(2,1)S(1)}, bf16[4,16,16,256]{3,2,1,0:T(8,128)(2,1)S(1)}, u32[]{:S(2)}, u32[]{:S(2)}) collective-permute-start(bf16[4,16,16,256]{3,2,1,0:T(8,128)(2,1)S(1)} %constant_dynamic-update-slice_fusion.slab), channel_id=1, source_target_pairs={{8,0},{9,1},{10,2},{11,3},{12,4},{13,5},{14,6},{15,7},{16,8},{17,9... | collective-permute-start | bytes 1572872 | tf_op jit(solution)/shard_map/ppermute | solution.py:330
  27.1 5.3 %mid.1 = (bf16[4,256,256]{2,1,0:T(8,128)(2,1)S(1)}, bf16[4,256,256]{2,1,0:T(8,128)(2,1)S(1)}, bf16[4,256,256]{2,1,0:T(8,128)(2,1)S(1)}, bf16[2,2,1024,384]{3,2,1...) custom-call(bf16[4,16,16,256]{3,2,1,0:T(8,128)(2,1)S(1)} %constant_d, ...), custom_call_target="tpu_custom_call" | custom-call | flops 6710886400 | bytes 4194304 | tf_op jit(solution)/shard_map/mid/pallas_call | solution.py:406
  32.5 3.1 %collective-permute-done.4.high_z = bf16[4,16,16,256]{3,2,1,0:T(8,128)(2,1)S(1)} collective-permute-done((bf16[4,16,16,256]{3,2,1,0:T(8,128)(2,1)S(1)}, bf16[4,16,16,256]{3,2,1,0:T(8,128)(2,1)S(1)}, u32[]{:S(2)}, u32[]{:S(2)}) %collective-permute-start.4) | collective-permute-done | bytes 524320 | tf_op jit(solution)/shard_map/ppermute | solution.py:330
  35.7 17.4 %main.1 = (bf16[4,256,256]{2,1,0:T(8,128)(2,1)S(1)}, bf16[4,256,256]{2,1,0:T(8,128)(2,1)S(1)}, bf16[4,256,256]{2,1,0:T(8,128)(2,1)S(1)}, bf16[2,256,256]{2,1,0:T...) custom-call(bf16[4,16,16,256]{3,2,1,0:T(8,128)(2,1)S(1)} %collective-permute-done.3.low_z, ...), custom_call_target="tpu_custom_call" | custom-call | flops 30198988800 | bytes 4194304 | tf_op jit(solution)/shard_map/main/pallas_call | solution.py:415
  53.0 1.3 %collective-permute-start.5 = (bf16[4,256,256]{2,1,0:T(8,128)(2,1)S(1)}, bf16[4,256,256]{2,1,0:T(8,128)(2,1)S(1)}, u32[]{:S(2)}, u32[]{:S(2)}) collective-permute-start(bf16[4,256,256]{2,1,0:T(8,128)(2,1)S(1)} %get-tuple-element.57), channel_id=1, source_target_pairs={{8,128},{9,129},{10,130},{11,131},{12,132},{13,133},{14,134},{15,1... | collective-permute-start | bytes 1572872 | tf_op jit(solution)/shard_map/ppermute | solution.py:330
  54.3 1.5 %collective-permute-start.6 = (bf16[4,256,256]{2,1,0:T(8,128)(2,1)S(1)}, bf16[4,256,256]{2,1,0:T(8,128)(2,1)}, u32[]{:S(2)}, u32[]{:S(2)}) collective-permute-start(bf16[4,256,256]{2,1,0:T(8,128)(2,1)S(1)} %get-tuple-element.58), channel_id=1, source_target_pairs={{0,128},{1,129},{2,130},{3,131},{4,132},{5,133},{6,134},{7,135},{8... | collective-permute-start | bytes 1572872 | tf_op jit(solution)/shard_map/ppermute | solution.py:330
  55.8 5.1 %collective-permute-start.7 = (bf16[4,256,256]{2,1,0:T(8,128)(2,1)S(1)}, bf16[4,256,256]{2,1,0:T(8,128)(2,1)}, u32[]{:S(2)}, u32[]{:S(2)}) collective-permute-start(bf16[4,256,256]{2,1,0:T(8,128)(2,1)S(1)} %get-tuple-element.59), channel_id=1, source_target_pairs={{0,136},{1,137},{2,138},{3,139},{4,140},{5,141},{6,142},{7,143},{8... | collective-permute-start | bytes 1572872 | tf_op jit(solution)/shard_map/ppermute | solution.py:330
  61.2 1.3 %collective-permute-done.10 = bf16[128,768]{1,0:T(8,128)(2,1)} collective-permute-done((bf16[128,768]{1,0:T(8,128)(2,1)S(1)}, bf16[128,768]{1,0:T(8,128)(2,1)}, u32[]{:S(2)}, u32[]{:S(2)}) %collective-permute-start.10) | collective-permute-done | bytes 196640 | tf_op jit(solution)/shard_map/ppermute | solution.py:330
  64.2 15.0 %all-to-all-start = ((bf16[128,2,384]{2,1,0:T(2,128)(2,1)}), bf16[128,2,384]{2,1,0:T(2,128)(2,1)S(1)}, u32[]{:S(2)}, u32[]{:S(2)}) async-start(bf16[128,2,384]{2,1,0:T(2,128)(2,1)} %reshape.47), calls=%async_computation | async-start | bytes 393216 | tf_op jit(solution)/shard_map/all_to_all | solution.py:367
  79.3 1.4 %fusion = (bf16[4,256,256]{2,1,0:T(8,128)(2,1)S(1)}, f32[4,256,256]{2,1,0:T(8,128)S(1)}) fusion(bf16[4,256,256]{2,1,0:T(8,128)(2,1)} %collective-permute-done.7, bf16[4,256,256]{2,1,0:T(8,128)(2,1)} %collective-permute-done.6, bf16[4,256,256]{2,1,0:T(8,128)(2,1)S(1)} %collective-permute-done.5), kind=kLoop, calls=%fused_computation.23 | loop fusion | flops 1572864 | bytes 3145728 | tf_op jit(solution)/shard_map/convert.3
  80.7 10.5 %all-to-all-done = bf16[128,2,384]{2,1,0:T(2,128)(2,1)S(1)} async-done(((bf16[128,2,384]{2,1,0:T(2,128)(2,1)}), bf16[128,2,384]{2,1,0:T(2,128)(2,1)S(1)}, u32[]{:S(2)}, u32[]{:S(2)}) %all-to-all-start) | async-done | bytes 196640 | tf_op jit(solution)/shard_map/all_to_all | solution.py:367
  92.3 6.8 %all-to-all-start.1 = ((bf16[128,2,384]{2,1,0:T(2,128)(2,1)}), bf16[128,2,384]{2,1,0:T(2,128)(2,1)S(1)}, u32[]{:S(2)}, u32[]{:S(2)}) async-start(bf16[128,2,384]{2,1,0:T(2,128)(2,1)} %broadcast_in_dim.32), calls=%async_computation.1 | async-start | bytes 393216 | tf_op jit(solution)/shard_map/all_to_all | solution.py:373
  99.1 4.0 %collective-permute-start.8 = (bf16[256,256]{1,0:T(8,128)(2,1)S(1)}, bf16[256,256]{1,0:T(8,128)(2,1)S(1)}, u32[]{:S(2)}, u32[]{:S(2)}) collective-permute-start(bf16[256,256]{1,0:T(8,128)(2,1)S(1)} %get-tuple-element.71), channel_id=1, source_target_pairs={{0,1},{1,2},{2,3},{3,4},{4,5},{5,6},{6,7},{8,9},{9,10},{10,11},{11... | collective-permute-start | bytes 393224 | tf_op jit(solution)/shard_map/ppermute | solution.py:330
  103.1 1.3 %collective-permute-start.9 = (bf16[256,256]{1,0:T(8,128)(2,1)S(1)}, bf16[256,256]{1,0:T(8,128)(2,1)S(1)}, u32[]{:S(2)}, u32[]{:S(2)}) collective-permute-start(bf16[256,256]{1,0:T(8,128)(2,1)S(1)} %get-tuple-element.70), channel_id=1, source_target_pairs={{1,0},{2,1},{3,2},{4,3},{5,4},{6,5},{7,6},{9,8},{10,9},{11,10},{12... | collective-permute-start | bytes 393224 | tf_op jit(solution)/shard_map/ppermute | solution.py:330
  104.5 1.1 collective-permute-done.8.from_low
  105.5 5.5 %collective-permute-done.9.from_high = bf16[256,256]{1,0:T(8,128)(2,1)S(1)} collective-permute-done((bf16[256,256]{1,0:T(8,128)(2,1)S(1)}, bf16[256,256]{1,0:T(8,128)(2,1)S(1)}, u32[]{:S(2)}, u32[]{:S(2)}) %collective-permute-start.9) | collective-permute-done | bytes 131104 | tf_op jit(solution)/shard_map/ppermute | solution.py:330
  111.1 1.3 %finish.1 = (bf16[4,8,16,256]{3,2,1,0:T(8,128)(2,1)}, bf16[4,8,16,256]{3,2,1,0:T(8,128)(2,1)}) custom-call(bf16[2,256,256]{2,1,0:T(8,128)(2,1)S(1)} %get-tuple-element.54.att, bf16[2,256,256]{2,1,0:T(8,128)(2,1)S(1)} %get-tuple-element.55.qg, bf16[256,256]{1,0:T(8,128)(2,1)S(1)} %get-tuple-element.40.wp, bf16[256,256]{1,0:T(8,128)(2,1)S(1)} %get-tuple-element.56.wo, ...), custom_call_target="tpu_custom_call" | custom-call | flops 335544320 | bytes 4194304 | tf_op jit(solution)/shard_map/finish/pallas_call | solution.py:443
  112.4 2.7 %collective-permute-start.11 = (bf16[128,2,384]{2,1,0:T(2,128)(2,1)S(1)}, bf16[128,2,384]{2,1,0:T(2,128)(2,1)S(1)}, u32[]{:S(2)}, u32[]{:S(2)}) collective-permute-start(bf16[128,2,384]{2,1,0:T(2,128)(2,1)S(1)} %all-to-all-done.1), channel_id=1, source_target_pairs={{0,128},{1,129},{2,130},{3,131},{4,132},{5,133},{6,134},{7,135},{8... | collective-permute-start | bytes 589832 | tf_op jit(solution)/shard_map/ppermute | solution.py:330
  115.1 1.1 collective-permute-done.11
  (54 shorter events, 14.0 us)
Async XLA Ops:
  0.6 11.9 %collective-permute-start.1 = (bf16[4,8,16,256]{3,2,1,0:T(8,128)(2,1)}, bf16[4,8,16,256]{3,2,1,0:T(8,128)(2,1)S(1)}, u32[]{:S(2)}, u32[]{:S(2)}) collective-permute-start(bf16[4,8,16,256]{3,2,1,0:T(8,128)(2,1)} %bitcast.34), channel_id=1, source_target_pairs={{0,128},{1,129},{2,130},{3,131},{4,132},{5,133},{6,134},{7,135},{8... | collective-permute-start | bytes 786440 | tf_op jit(solution)/shard_map/ppermute | solution.py:330
  5.0 7.5 %collective-permute-start = (bf16[4,4,16,256]{3,2,1,0:T(8,128)(2,1)S(1)}, bf16[4,4,16,256]{3,2,1,0:T(8,128)(2,1)S(1)}, u32[]{:S(2)}, u32[]{:S(2)}) collective-permute-start(bf16[4,4,16,256]{3,2,1,0:T(8,128)(2,1)S(1)} %get-tuple-element.75), channel_id=1, source_target_pairs={{0,129},{1,130},{2,131},{3,132},{4,133},{5,134},{6,135},{8,137},{9... | collective-permute-start | bytes 393224 | tf_op jit(solution)/shard_map/ppermute | solution.py:330
  8.0 9.1 %collective-permute-start.2 = (bf16[4,4,16,256]{3,2,1,0:T(8,128)(2,1)S(1)}, bf16[4,4,16,256]{3,2,1,0:T(8,128)(2,1)S(1)}, u32[]{:S(2)}, u32[]{:S(2)}) collective-permute-start(bf16[4,4,16,256]{3,2,1,0:T(8,128)(2,1)S(1)} %get-tuple-element.74), channel_id=1, source_target_pairs={{1,128},{2,129},{3,130},{4,131},{5,132},{6,133},{7,134},{9,136},{1... | collective-permute-start | bytes 393224 | tf_op jit(solution)/shard_map/ppermute | solution.py:330
  17.1 15.4 %collective-permute-start.3 = (bf16[4,16,16,256]{3,2,1,0:T(8,128)(2,1)S(1)}, bf16[4,16,16,256]{3,2,1,0:T(8,128)(2,1)S(1)}, u32[]{:S(2)}, u32[]{:S(2)}) collective-permute-start(bf16[4,16,16,256]{3,2,1,0:T(8,128)(2,1)S(1)} %constant_dynamic-update-slice_fusion.slab), channel_id=1, source_target_pairs={{0,8},{1,9},{2,10},{3,11},{4,12},{5,13},{6,14},{7,15},{8,16},{9,17... | collective-permute-start | bytes 1572872 | tf_op jit(solution)/shard_map/ppermute | solution.py:330
  20.6 15.0 %collective-permute-start.4 = (bf16[4,16,16,256]{3,2,1,0:T(8,128)(2,1)S(1)}, bf16[4,16,16,256]{3,2,1,0:T(8,128)(2,1)S(1)}, u32[]{:S(2)}, u32[]{:S(2)}) collective-permute-start(bf16[4,16,16,256]{3,2,1,0:T(8,128)(2,1)S(1)} %constant_dynamic-update-slice_fusion.slab), channel_id=1, source_target_pairs={{8,0},{9,1},{10,2},{11,3},{12,4},{13,5},{14,6},{15,7},{16,8},{17,9... | collective-permute-start | bytes 1572872 | tf_op jit(solution)/shard_map/ppermute | solution.py:330
  21.9 1.0 copy-start
  22.9 0.9 copy-start.1
  23.8 0.9 copy-start.2
  24.7 0.9 copy-start.3
  25.6 0.9 copy-start.4
  53.0 26.2 %collective-permute-start.5 = (bf16[4,256,256]{2,1,0:T(8,128)(2,1)S(1)}, bf16[4,256,256]{2,1,0:T(8,128)(2,1)S(1)}, u32[]{:S(2)}, u32[]{:S(2)}) collective-permute-start(bf16[4,256,256]{2,1,0:T(8,128)(2,1)S(1)} %get-tuple-element.57), channel_id=1, source_target_pairs={{8,128},{9,129},{10,130},{11,131},{12,132},{13,133},{14,134},{15,1... | collective-permute-start | bytes 1572872 | tf_op jit(solution)/shard_map/ppermute | solution.py:330
  54.3 24.9 %collective-permute-start.6 = (bf16[4,256,256]{2,1,0:T(8,128)(2,1)S(1)}, bf16[4,256,256]{2,1,0:T(8,128)(2,1)}, u32[]{:S(2)}, u32[]{:S(2)}) collective-permute-start(bf16[4,256,256]{2,1,0:T(8,128)(2,1)S(1)} %get-tuple-element.58), channel_id=1, source_target_pairs={{0,128},{1,129},{2,130},{3,131},{4,132},{5,133},{6,134},{7,135},{8... | collective-permute-start | bytes 1572872 | tf_op jit(solution)/shard_map/ppermute | solution.py:330
  55.8 23.5 %collective-permute-start.7 = (bf16[4,256,256]{2,1,0:T(8,128)(2,1)S(1)}, bf16[4,256,256]{2,1,0:T(8,128)(2,1)}, u32[]{:S(2)}, u32[]{:S(2)}) collective-permute-start(bf16[4,256,256]{2,1,0:T(8,128)(2,1)S(1)} %get-tuple-element.59), channel_id=1, source_target_pairs={{0,136},{1,137},{2,138},{3,139},{4,140},{5,141},{6,142},{7,143},{8... | collective-permute-start | bytes 1572872 | tf_op jit(solution)/shard_map/ppermute | solution.py:330
  60.9 1.7 %collective-permute-start.10 = (bf16[128,768]{1,0:T(8,128)(2,1)S(1)}, bf16[128,768]{1,0:T(8,128)(2,1)}, u32[]{:S(2)}, u32[]{:S(2)}) collective-permute-start(bf16[128,768]{1,0:T(8,128)(2,1)S(1)} %constant_dynamic-slice_fusion), channel_id=1, source_target_pairs={{0,128},{1,129},{2,130},{3,131},{4,132},{5,133},{6,134},{7,135},{8... | collective-permute-start | bytes 589832 | tf_op jit(solution)/shard_map/ppermute | solution.py:330
  64.2 27.0 %all-to-all-start = ((bf16[128,2,384]{2,1,0:T(2,128)(2,1)}), bf16[128,2,384]{2,1,0:T(2,128)(2,1)S(1)}, u32[]{:S(2)}, u32[]{:S(2)}) async-start(bf16[128,2,384]{2,1,0:T(2,128)(2,1)} %reshape.47), calls=%async_computation | async-start | bytes 393216 | tf_op jit(solution)/shard_map/all_to_all | solution.py:367
  92.3 20.1 %all-to-all-start.1 = ((bf16[128,2,384]{2,1,0:T(2,128)(2,1)}), bf16[128,2,384]{2,1,0:T(2,128)(2,1)S(1)}, u32[]{:S(2)}, u32[]{:S(2)}) async-start(bf16[128,2,384]{2,1,0:T(2,128)(2,1)} %broadcast_in_dim.32), calls=%async_computation.1 | async-start | bytes 393216 | tf_op jit(solution)/shard_map/all_to_all | solution.py:373
  99.1 6.4 %collective-permute-start.8 = (bf16[256,256]{1,0:T(8,128)(2,1)S(1)}, bf16[256,256]{1,0:T(8,128)(2,1)S(1)}, u32[]{:S(2)}, u32[]{:S(2)}) collective-permute-start(bf16[256,256]{1,0:T(8,128)(2,1)S(1)} %get-tuple-element.71), channel_id=1, source_target_pairs={{0,1},{1,2},{2,3},{3,4},{4,5},{5,6},{6,7},{8,9},{9,10},{10,11},{11... | collective-permute-start | bytes 393224 | tf_op jit(solution)/shard_map/ppermute | solution.py:330
  103.1 8.0 %collective-permute-start.9 = (bf16[256,256]{1,0:T(8,128)(2,1)S(1)}, bf16[256,256]{1,0:T(8,128)(2,1)S(1)}, u32[]{:S(2)}, u32[]{:S(2)}) collective-permute-start(bf16[256,256]{1,0:T(8,128)(2,1)S(1)} %get-tuple-element.70), channel_id=1, source_target_pairs={{1,0},{2,1},{3,2},{4,3},{5,4},{6,5},{7,6},{9,8},{10,9},{11,10},{12... | collective-permute-start | bytes 393224 | tf_op jit(solution)/shard_map/ppermute | solution.py:330
  112.4 3.7 %collective-permute-start.11 = (bf16[128,2,384]{2,1,0:T(2,128)(2,1)S(1)}, bf16[128,2,384]{2,1,0:T(2,128)(2,1)S(1)}, u32[]{:S(2)}, u32[]{:S(2)}) collective-permute-start(bf16[128,2,384]{2,1,0:T(2,128)(2,1)S(1)} %all-to-all-done.1), channel_id=1, source_target_pairs={{0,128},{1,129},{2,130},{3,131},{4,132},{5,133},{6,134},{7,135},{8... | collective-permute-start | bytes 589832 | tf_op jit(solution)/shard_map/ppermute | solution.py:330

commit v7 on v6

--- a/solution.py
+++ b/solution.py
@@ -443,7 +443,7 @@
     mixed, grad = call(finish_kernel, [(own.shape, BF16)] * 2, flops=10 * unit, name="finish")(
         att, qg, wp, wo, got[1:3], from_low, from_high
     )
-    sums = both_halves(after(shares, grad), part.shape[0] // 2)
+    sums = both_halves(after(shares, (from_low, from_high)), part.shape[0] // 2)
     return (
         mixed[None],
         grad[None],

time: 118 us -> 117 us (level)
  transfers between devices with their start and end apart: 14 -> 14, of which waited for: 7 -> 6; matrix products, arithmetic and copies ran while one was open for 6% -> 6% of each run, Pallas kernels for 6% -> 6%
where the time goes in v7:
time: 117 us
  starting transfers between devices  50.5 us (43%)
  waiting for transfers between devices  26.1 us (22%)
  Pallas kernels  24.6 us (21%)
  local copies, waits for them, and re-layouts  10.3 us (9%)
  other arithmetic  4.14 us (4%)
    ppermute x12, starting transfers between devices, shift(): return lax.ppermute(block, AXES, route)  28.6 us
    pallas_call x1, Pallas kernels, on_device(): call(main_kernel, [((4,) + wide, BF16)] * 3 + [((2,) + wide, BF16)] * 2 +...  17.4 us
    ppermute x12, waiting for transfers between devices, shift(): return lax.ppermute(block, AXES, route)  15.6 us
    all_to_all x1, starting transfers between devices, summed_share(): got = lax.all_to_all(mine.reshape(places, 2, -1), ('gz', 'gy'), 0, 0)  15 us
    all_to_all x1, waiting for transfers between devices, summed_share(): got = lax.all_to_all(mine.reshape(places, 2, -1), ('gz', 'gy'), 0, 0)  10.5 us
    all_to_all x1, starting transfers between devices, all_shares(): lax.all_to_all(jnp.broadcast_to(total[None], (places,) + total.shape), ('...  6.82 us
    pallas_call x1, Pallas kernels, on_device(): call(mid_kernel, [((4,) + wide, BF16)] * 3 + [((2, 2, 4 * ROW, 384), BF16...  5.35 us
    unnamed x13, local copies, waits for them, and re-layouts  4.69 us
  transfers between devices with their start and end apart: 14, of which 6 were waited for; matrix products, arithmetic and copies ran while one was open for 6% of the time, Pallas kernels for 6%

profile of v7, /device:TPU:1, one launch (start us, length us, event | category | flops | bytes accessed | tf_op | source)
XLA Modules:
  0.0 116.5 jit_solution(15170552695488096330)
XLA Ops:
  0.6 3.3 %collective-permute-start.1 = (bf16[4,8,16,256]{3,2,1,0:T(8,128)(2,1)}, bf16[4,8,16,256]{3,2,1,0:T(8,128)(2,1)S(1)}, u32[]{:S(2)}, u32[]{:S(2)}) collective-permute-start(bf16[4,8,16,256]{3,2,1,0:T(8,128)(2,1)} %bitcast.34), channel_id=1, source_target_pairs={{0,128},{1,129},{2,130},{3,131},{4,132},{5,133},{6,134},{7,135},{8... | collective-permute-start | bytes 786440 | tf_op jit(solution)/shard_map/ppermute | solution.py:330
  4.0 1.0 fusion.2
  5.0 3.0 %collective-permute-start = (bf16[4,4,16,256]{3,2,1,0:T(8,128)(2,1)S(1)}, bf16[4,4,16,256]{3,2,1,0:T(8,128)(2,1)S(1)}, u32[]{:S(2)}, u32[]{:S(2)}) collective-permute-start(bf16[4,4,16,256]{3,2,1,0:T(8,128)(2,1)S(1)} %get-tuple-element.75), channel_id=1, source_target_pairs={{0,129},{1,130},{2,131},{3,132},{4,133},{5,134},{6,135},{8,137},{9... | collective-permute-start | bytes 393224 | tf_op jit(solution)/shard_map/ppermute | solution.py:330
  8.0 1.3 %collective-permute-start.2 = (bf16[4,4,16,256]{3,2,1,0:T(8,128)(2,1)S(1)}, bf16[4,4,16,256]{3,2,1,0:T(8,128)(2,1)S(1)}, u32[]{:S(2)}, u32[]{:S(2)}) collective-permute-start(bf16[4,4,16,256]{3,2,1,0:T(8,128)(2,1)S(1)} %get-tuple-element.74), channel_id=1, source_target_pairs={{1,128},{2,129},{3,130},{4,131},{5,132},{6,133},{7,134},{9,136},{1... | collective-permute-start | bytes 393224 | tf_op jit(solution)/shard_map/ppermute | solution.py:330
  12.6 4.5 %collective-permute-done.2 = bf16[4,4,16,256]{3,2,1,0:T(8,128)(2,1)S(1)} collective-permute-done((bf16[4,4,16,256]{3,2,1,0:T(8,128)(2,1)S(1)}, bf16[4,4,16,256]{3,2,1,0:T(8,128)(2,1)S(1)}, u32[]{:S(2)}, u32[]{:S(2)}) %collective-permute-start.2) | collective-permute-done | bytes 131104 | tf_op jit(solution)/shard_map/ppermute | solution.py:330
  17.1 3.6 %collective-permute-start.3 = (bf16[4,16,16,256]{3,2,1,0:T(8,128)(2,1)S(1)}, bf16[4,16,16,256]{3,2,1,0:T(8,128)(2,1)S(1)}, u32[]{:S(2)}, u32[]{:S(2)}) collective-permute-start(bf16[4,16,16,256]{3,2,1,0:T(8,128)(2,1)S(1)} %constant_dynamic-update-slice_fusion.slab), channel_id=1, source_target_pairs={{0,8},{1,9},{2,10},{3,11},{4,12},{5,13},{6,14},{7,15},{8,16},{9,17... | collective-permute-start | bytes 1572872 | tf_op jit(solution)/shard_map/ppermute | solution.py:330
  20.6 1.3 %collective-permute-start.4 = (bf16[4,16,16,256]{3,2,1,0:T(8,128)(2,1)S(1)}, bf16[4,16,16,256]{3,2,1,0:T(8,128)(2,1)S(1)}, u32[]{:S(2)}, u32[]{:S(2)}) collective-permute-start(bf16[4,16,16,256]{3,2,1,0:T(8,128)(2,1)S(1)} %constant_dynamic-update-slice_fusion.slab), channel_id=1, source_target_pairs={{8,0},{9,1},{10,2},{11,3},{12,4},{13,5},{14,6},{15,7},{16,8},{17,9... | collective-permute-start | bytes 1572872 | tf_op jit(solution)/shard_map/ppermute | solution.py:330
  27.1 5.3 %mid.1 = (bf16[4,256,256]{2,1,0:T(8,128)(2,1)S(1)}, bf16[4,256,256]{2,1,0:T(8,128)(2,1)S(1)}, bf16[4,256,256]{2,1,0:T(8,128)(2,1)S(1)}, bf16[2,2,1024,384]{3,2,1...) custom-call(bf16[4,16,16,256]{3,2,1,0:T(8,128)(2,1)S(1)} %constant_d, ...), custom_call_target="tpu_custom_call" | custom-call | flops 6710886400 | bytes 4194304 | tf_op jit(solution)/shard_map/mid/pallas_call | solution.py:406
  32.5 3.1 %collective-permute-done.4.high_z = bf16[4,16,16,256]{3,2,1,0:T(8,128)(2,1)S(1)} collective-permute-done((bf16[4,16,16,256]{3,2,1,0:T(8,128)(2,1)S(1)}, bf16[4,16,16,256]{3,2,1,0:T(8,128)(2,1)S(1)}, u32[]{:S(2)}, u32[]{:S(2)}) %collective-permute-start.4) | collective-permute-done | bytes 524320 | tf_op jit(solution)/shard_map/ppermute | solution.py:330
  35.7 17.4 %main.1 = (bf16[4,256,256]{2,1,0:T(8,128)(2,1)S(1)}, bf16[4,256,256]{2,1,0:T(8,128)(2,1)S(1)}, bf16[4,256,256]{2,1,0:T(8,128)(2,1)S(1)}, bf16[2,256,256]{2,1,0:T...) custom-call(bf16[4,16,16,256]{3,2,1,0:T(8,128)(2,1)S(1)} %collective-permute-done.3.low_z, ...), custom_call_target="tpu_custom_call" | custom-call | flops 30198988800 | bytes 4194304 | tf_op jit(solution)/shard_map/main/pallas_call | solution.py:415
  53.0 1.3 %collective-permute-start.5 = (bf16[4,256,256]{2,1,0:T(8,128)(2,1)S(1)}, bf16[4,256,256]{2,1,0:T(8,128)(2,1)S(1)}, u32[]{:S(2)}, u32[]{:S(2)}) collective-permute-start(bf16[4,256,256]{2,1,0:T(8,128)(2,1)S(1)} %get-tuple-element.57), channel_id=1, source_target_pairs={{8,128},{9,129},{10,130},{11,131},{12,132},{13,133},{14,134},{15,1... | collective-permute-start | bytes 1572872 | tf_op jit(solution)/shard_map/ppermute | solution.py:330
  54.3 1.5 %collective-permute-start.6 = (bf16[4,256,256]{2,1,0:T(8,128)(2,1)S(1)}, bf16[4,256,256]{2,1,0:T(8,128)(2,1)}, u32[]{:S(2)}, u32[]{:S(2)}) collective-permute-start(bf16[4,256,256]{2,1,0:T(8,128)(2,1)S(1)} %get-tuple-element.58), channel_id=1, source_target_pairs={{0,128},{1,129},{2,130},{3,131},{4,132},{5,133},{6,134},{7,135},{8... | collective-permute-start | bytes 1572872 | tf_op jit(solution)/shard_map/ppermute | solution.py:330
  55.8 5.1 %collective-permute-start.7 = (bf16[4,256,256]{2,1,0:T(8,128)(2,1)S(1)}, bf16[4,256,256]{2,1,0:T(8,128)(2,1)}, u32[]{:S(2)}, u32[]{:S(2)}) collective-permute-start(bf16[4,256,256]{2,1,0:T(8,128)(2,1)S(1)} %get-tuple-element.59), channel_id=1, source_target_pairs={{0,136},{1,137},{2,138},{3,139},{4,140},{5,141},{6,142},{7,143},{8... | collective-permute-start | bytes 1572872 | tf_op jit(solution)/shard_map/ppermute | solution.py:330
  61.2 1.3 %collective-permute-done.10 = bf16[128,768]{1,0:T(8,128)(2,1)} collective-permute-done((bf16[128,768]{1,0:T(8,128)(2,1)S(1)}, bf16[128,768]{1,0:T(8,128)(2,1)}, u32[]{:S(2)}, u32[]{:S(2)}) %collective-permute-start.10) | collective-permute-done | bytes 196640 | tf_op jit(solution)/shard_map/ppermute | solution.py:330
  64.2 15.0 %all-to-all-start = ((bf16[128,2,384]{2,1,0:T(2,128)(2,1)}), bf16[128,2,384]{2,1,0:T(2,128)(2,1)S(1)}, u32[]{:S(2)}, u32[]{:S(2)}) async-start(bf16[128,2,384]{2,1,0:T(2,128)(2,1)} %reshape.47), calls=%async_computation | async-start | bytes 393216 | tf_op jit(solution)/shard_map/all_to_all | solution.py:367
  79.3 1.4 %fusion = (bf16[4,256,256]{2,1,0:T(8,128)(2,1)S(1)}, f32[4,256,256]{2,1,0:T(8,128)S(1)}) fusion(bf16[4,256,256]{2,1,0:T(8,128)(2,1)} %collective-permute-done.7, bf16[4,256,256]{2,1,0:T(8,128)(2,1)} %collective-permute-done.6, bf16[4,256,256]{2,1,0:T(8,128)(2,1)S(1)} %collective-permute-done.5), kind=kLoop, calls=%fused_computation.23 | loop fusion | flops 1572864 | bytes 3145728 | tf_op jit(solution)/shard_map/convert.3
  80.7 10.5 %all-to-all-done = bf16[128,2,384]{2,1,0:T(2,128)(2,1)S(1)} async-done(((bf16[128,2,384]{2,1,0:T(2,128)(2,1)}), bf16[128,2,384]{2,1,0:T(2,128)(2,1)S(1)}, u32[]{:S(2)}, u32[]{:S(2)}) %all-to-all-start) | async-done | bytes 196640 | tf_op jit(solution)/shard_map/all_to_all | solution.py:367
  92.3 6.8 %all-to-all-start.1 = ((bf16[128,2,384]{2,1,0:T(2,128)(2,1)}), bf16[128,2,384]{2,1,0:T(2,128)(2,1)S(1)}, u32[]{:S(2)}, u32[]{:S(2)}) async-start(bf16[128,2,384]{2,1,0:T(2,128)(2,1)} %broadcast_in_dim.32), calls=%async_computation.1 | async-start | bytes 393216 | tf_op jit(solution)/shard_map/all_to_all | solution.py:373
  99.1 4.0 %collective-permute-start.8 = (bf16[256,256]{1,0:T(8,128)(2,1)S(1)}, bf16[256,256]{1,0:T(8,128)(2,1)S(1)}, u32[]{:S(2)}, u32[]{:S(2)}) collective-permute-start(bf16[256,256]{1,0:T(8,128)(2,1)S(1)} %get-tuple-element.71), channel_id=1, source_target_pairs={{0,1},{1,2},{2,3},{3,4},{4,5},{5,6},{6,7},{8,9},{9,10},{10,11},{11... | collective-permute-start | bytes 393224 | tf_op jit(solution)/shard_map/ppermute | solution.py:330
  103.1 1.3 %collective-permute-start.9 = (bf16[256,256]{1,0:T(8,128)(2,1)S(1)}, bf16[256,256]{1,0:T(8,128)(2,1)S(1)}, u32[]{:S(2)}, u32[]{:S(2)}) collective-permute-start(bf16[256,256]{1,0:T(8,128)(2,1)S(1)} %get-tuple-element.70), channel_id=1, source_target_pairs={{1,0},{2,1},{3,2},{4,3},{5,4},{6,5},{7,6},{9,8},{10,9},{11,10},{12... | collective-permute-start | bytes 393224 | tf_op jit(solution)/shard_map/ppermute | solution.py:330
  104.4 1.1 collective-permute-done.8.from_low
  105.5 5.5 %collective-permute-done.9.from_high = bf16[256,256]{1,0:T(8,128)(2,1)S(1)} collective-permute-done((bf16[256,256]{1,0:T(8,128)(2,1)S(1)}, bf16[256,256]{1,0:T(8,128)(2,1)S(1)}, u32[]{:S(2)}, u32[]{:S(2)}) %collective-permute-start.9) | collective-permute-done | bytes 131104 | tf_op jit(solution)/shard_map/ppermute | solution.py:330
  111.1 2.7 %collective-permute-start.11 = (bf16[128,2,384]{2,1,0:T(2,128)(2,1)S(1)}, bf16[128,2,384]{2,1,0:T(2,128)(2,1)S(1)}, u32[]{:S(2)}, u32[]{:S(2)}) collective-permute-start(bf16[128,2,384]{2,1,0:T(2,128)(2,1)S(1)} %all-to-all-done.1), channel_id=1, source_target_pairs={{0,128},{1,129},{2,130},{3,131},{4,132},{5,133},{6,134},{7,135},{8... | collective-permute-start | bytes 589832 | tf_op jit(solution)/shard_map/ppermute | solution.py:330
  113.8 1.3 %finish.1 = (bf16[4,8,16,256]{3,2,1,0:T(8,128)(2,1)}, bf16[4,8,16,256]{3,2,1,0:T(8,128)(2,1)}) custom-call(bf16[2,256,256]{2,1,0:T(8,128)(2,1)S(1)} %get-tuple-element.54.att, bf16[2,256,256]{2,1,0:T(8,128)(2,1)S(1)} %get-tuple-element.55.qg, bf16[256,256]{1,0:T(8,128)(2,1)S(1)} %get-tuple-element.40.wp, bf16[256,256]{1,0:T(8,128)(2,1)S(1)} %get-tuple-element.56.wo, ...), custom_call_target="tpu_custom_call" | custom-call | flops 335544320 | bytes 4194304 | tf_op jit(solution)/shard_map/finish/pallas_call | solution.py:443
  (54 shorter events, 13.0 us)
Async XLA Ops:
  0.6 11.9 %collective-permute-start.1 = (bf16[4,8,16,256]{3,2,1,0:T(8,128)(2,1)}, bf16[4,8,16,256]{3,2,1,0:T(8,128)(2,1)S(1)}, u32[]{:S(2)}, u32[]{:S(2)}) collective-permute-start(bf16[4,8,16,256]{3,2,1,0:T(8,128)(2,1)} %bitcast.34), channel_id=1, source_target_pairs={{0,128},{1,129},{2,130},{3,131},{4,132},{5,133},{6,134},{7,135},{8... | collective-permute-start | bytes 786440 | tf_op jit(solution)/shard_map/ppermute | solution.py:330
  5.0 7.5 %collective-permute-start = (bf16[4,4,16,256]{3,2,1,0:T(8,128)(2,1)S(1)}, bf16[4,4,16,256]{3,2,1,0:T(8,128)(2,1)S(1)}, u32[]{:S(2)}, u32[]{:S(2)}) collective-permute-start(bf16[4,4,16,256]{3,2,1,0:T(8,128)(2,1)S(1)} %get-tuple-element.75), channel_id=1, source_target_pairs={{0,129},{1,130},{2,131},{3,132},{4,133},{5,134},{6,135},{8,137},{9... | collective-permute-start | bytes 393224 | tf_op jit(solution)/shard_map/ppermute | solution.py:330
  8.0 9.1 %collective-permute-start.2 = (bf16[4,4,16,256]{3,2,1,0:T(8,128)(2,1)S(1)}, bf16[4,4,16,256]{3,2,1,0:T(8,128)(2,1)S(1)}, u32[]{:S(2)}, u32[]{:S(2)}) collective-permute-start(bf16[4,4,16,256]{3,2,1,0:T(8,128)(2,1)S(1)} %get-tuple-element.74), channel_id=1, source_target_pairs={{1,128},{2,129},{3,130},{4,131},{5,132},{6,133},{7,134},{9,136},{1... | collective-permute-start | bytes 393224 | tf_op jit(solution)/shard_map/ppermute | solution.py:330
  17.1 15.4 %collective-permute-start.3 = (bf16[4,16,16,256]{3,2,1,0:T(8,128)(2,1)S(1)}, bf16[4,16,16,256]{3,2,1,0:T(8,128)(2,1)S(1)}, u32[]{:S(2)}, u32[]{:S(2)}) collective-permute-start(bf16[4,16,16,256]{3,2,1,0:T(8,128)(2,1)S(1)} %constant_dynamic-update-slice_fusion.slab), channel_id=1, source_target_pairs={{0,8},{1,9},{2,10},{3,11},{4,12},{5,13},{6,14},{7,15},{8,16},{9,17... | collective-permute-start | bytes 1572872 | tf_op jit(solution)/shard_map/ppermute | solution.py:330
  20.6 15.0 %collective-permute-start.4 = (bf16[4,16,16,256]{3,2,1,0:T(8,128)(2,1)S(1)}, bf16[4,16,16,256]{3,2,1,0:T(8,128)(2,1)S(1)}, u32[]{:S(2)}, u32[]{:S(2)}) collective-permute-start(bf16[4,16,16,256]{3,2,1,0:T(8,128)(2,1)S(1)} %constant_dynamic-update-slice_fusion.slab), channel_id=1, source_target_pairs={{8,0},{9,1},{10,2},{11,3},{12,4},{13,5},{14,6},{15,7},{16,8},{17,9... | collective-permute-start | bytes 1572872 | tf_op jit(solution)/shard_map/ppermute | solution.py:330
  21.9 1.0 copy-start
  22.9 0.9 copy-start.1
  23.8 0.9 copy-start.2
  24.7 0.9 copy-start.3
  25.6 0.9 copy-start.4
  53.0 26.2 %collective-permute-start.5 = (bf16[4,256,256]{2,1,0:T(8,128)(2,1)S(1)}, bf16[4,256,256]{2,1,0:T(8,128)(2,1)S(1)}, u32[]{:S(2)}, u32[]{:S(2)}) collective-permute-start(bf16[4,256,256]{2,1,0:T(8,128)(2,1)S(1)} %get-tuple-element.57), channel_id=1, source_target_pairs={{8,128},{9,129},{10,130},{11,131},{12,132},{13,133},{14,134},{15,1... | collective-permute-start | bytes 1572872 | tf_op jit(solution)/shard_map/ppermute | solution.py:330
  54.3 24.9 %collective-permute-start.6 = (bf16[4,256,256]{2,1,0:T(8,128)(2,1)S(1)}, bf16[4,256,256]{2,1,0:T(8,128)(2,1)}, u32[]{:S(2)}, u32[]{:S(2)}) collective-permute-start(bf16[4,256,256]{2,1,0:T(8,128)(2,1)S(1)} %get-tuple-element.58), channel_id=1, source_target_pairs={{0,128},{1,129},{2,130},{3,131},{4,132},{5,133},{6,134},{7,135},{8... | collective-permute-start | bytes 1572872 | tf_op jit(solution)/shard_map/ppermute | solution.py:330
  55.8 23.5 %collective-permute-start.7 = (bf16[4,256,256]{2,1,0:T(8,128)(2,1)S(1)}, bf16[4,256,256]{2,1,0:T(8,128)(2,1)}, u32[]{:S(2)}, u32[]{:S(2)}) collective-permute-start(bf16[4,256,256]{2,1,0:T(8,128)(2,1)S(1)} %get-tuple-element.59), channel_id=1, source_target_pairs={{0,136},{1,137},{2,138},{3,139},{4,140},{5,141},{6,142},{7,143},{8... | collective-permute-start | bytes 1572872 | tf_op jit(solution)/shard_map/ppermute | solution.py:330
  60.9 1.7 %collective-permute-start.10 = (bf16[128,768]{1,0:T(8,128)(2,1)S(1)}, bf16[128,768]{1,0:T(8,128)(2,1)}, u32[]{:S(2)}, u32[]{:S(2)}) collective-permute-start(bf16[128,768]{1,0:T(8,128)(2,1)S(1)} %constant_dynamic-slice_fusion), channel_id=1, source_target_pairs={{0,128},{1,129},{2,130},{3,131},{4,132},{5,133},{6,134},{7,135},{8... | collective-permute-start | bytes 589832 | tf_op jit(solution)/shard_map/ppermute | solution.py:330
  64.2 27.0 %all-to-all-start = ((bf16[128,2,384]{2,1,0:T(2,128)(2,1)}), bf16[128,2,384]{2,1,0:T(2,128)(2,1)S(1)}, u32[]{:S(2)}, u32[]{:S(2)}) async-start(bf16[128,2,384]{2,1,0:T(2,128)(2,1)} %reshape.47), calls=%async_computation | async-start | bytes 393216 | tf_op jit(solution)/shard_map/all_to_all | solution.py:367
  92.3 18.8 %all-to-all-start.1 = ((bf16[128,2,384]{2,1,0:T(2,128)(2,1)}), bf16[128,2,384]{2,1,0:T(2,128)(2,1)S(1)}, u32[]{:S(2)}, u32[]{:S(2)}) async-start(bf16[128,2,384]{2,1,0:T(2,128)(2,1)} %broadcast_in_dim.32), calls=%async_computation.1 | async-start | bytes 393216 | tf_op jit(solution)/shard_map/all_to_all | solution.py:373
  99.1 6.4 %collective-permute-start.8 = (bf16[256,256]{1,0:T(8,128)(2,1)S(1)}, bf16[256,256]{1,0:T(8,128)(2,1)S(1)}, u32[]{:S(2)}, u32[]{:S(2)}) collective-permute-start(bf16[256,256]{1,0:T(8,128)(2,1)S(1)} %get-tuple-element.71), channel_id=1, source_target_pairs={{0,1},{1,2},{2,3},{3,4},{4,5},{5,6},{6,7},{8,9},{9,10},{10,11},{11... | collective-permute-start | bytes 393224 | tf_op jit(solution)/shard_map/ppermute | solution.py:330
  103.1 8.0 %collective-permute-start.9 = (bf16[256,256]{1,0:T(8,128)(2,1)S(1)}, bf16[256,256]{1,0:T(8,128)(2,1)S(1)}, u32[]{:S(2)}, u32[]{:S(2)}) collective-permute-start(bf16[256,256]{1,0:T(8,128)(2,1)S(1)} %get-tuple-element.70), channel_id=1, source_target_pairs={{1,0},{2,1},{3,2},{4,3},{5,4},{6,5},{7,6},{9,8},{10,9},{11,10},{12... | collective-permute-start | bytes 393224 | tf_op jit(solution)/shard_map/ppermute | solution.py:330
  111.1 4.0 %collective-permute-start.11 = (bf16[128,2,384]{2,1,0:T(2,128)(2,1)S(1)}, bf16[128,2,384]{2,1,0:T(2,128)(2,1)S(1)}, u32[]{:S(2)}, u32[]{:S(2)}) collective-permute-start(bf16[128,2,384]{2,1,0:T(2,128)(2,1)S(1)} %all-to-all-done.1), channel_id=1, source_target_pairs={{0,128},{1,129},{2,130},{3,131},{4,132},{5,133},{6,134},{7,135},{8... | collective-permute-start | bytes 589832 | tf_op jit(solution)/shard_map/ppermute | solution.py:330
